TPU v7x, 256 devices: a whole 4x4x8 slice. The times are simulated.
256 devices in a mesh: grp: 8 (over x, z_lo), dev: 32 (over y, z_hi, core).
Axes of the slice: x: 4, y: 4, z: 8 (z_hi: 4, z_lo: 2; z = z_hi * 2 + z_lo), core: 2. Of those that a mesh axis runs over, the one named last changes fastest.
Arguments:
- hidden_first: bfloat16 [65536, 8192], P(('grp', 'dev')), may hold values from -24 to 24
- logit_grads: bfloat16 [65536, 512], P(('grp', 'dev')), may hold values from -0.00018310547 to 0.00018310547
- hidden_second: bfloat16 [65536, 8192], P(('grp', 'dev')), may hold values from -400 to 400
- labels_second: int32 [65536], P(('grp', 'dev')), may hold values from 0 to 511
- master: float32 [8192, 512], P(('grp', 'dev')), may hold values from -0.0625 to 0.0625
- moment_one: float32 [8192, 512], P(('grp', 'dev')), may hold values from -0.00390625 to 0.00390625
- moment_two: float32 [8192, 512], P(('grp', 'dev')), may hold values from 1e-08 to 1e-06
Outputs:
- new_master: float32 [8192, 512], P(('grp', 'dev'))
- new_moment_one: float32 [8192, 512], P(('grp', 'dev'))
- new_moment_two: float32 [8192, 512], P(('grp', 'dev'))
- loss_second: float32 [65536], P(('grp', 'dev'))
All inputs are finite; a program needn't handle non-finite values.
Results may differ from a plain program's by a relative error of at most 0.0014.
Values may be sent and summed in bfloat16 or wider, within the bound.
No kernel may reach another device: no remote copies, remote signals or barrier semaphores. Data moves between devices by JAX's collectives and lax.ppermute only.
A program may use at most 128 MiB of HBM per device.

v0:
```python
import jax
import jax.numpy as jnp
from jax import lax
from jax.sharding import PartitionSpec as P

STEP = 10


def on_device(
    hidden_first, logit_grads, hidden_second, labels_second, master, moment_one, moment_two
):
    groups = lax.axis_size("grp")
    members = lax.axis_size("dev")
    owned = master.shape[0]
    vocab = master.shape[1]

    def regroup(hidden):
        rows = hidden.shape[0]
        return (
            hidden.reshape(rows, groups, members, owned)
            .transpose(0, 2, 1, 3)
            .reshape(rows, groups * members * owned)
        )

    columns = regroup(hidden_first)
    group_sum = lax.psum_scatter(
        jnp.einsum("tc,tv->cv", columns, logit_grads, preferred_element_type=jnp.float32),
        "dev",
        scatter_dimension=0,
        tiled=True,
    )
    weight_grad = lax.psum_scatter(group_sum, "grp", scatter_dimension=0, tiled=True)
    new_moment_one = 0.9 * moment_one + 0.1 * weight_grad
    new_moment_two = 0.95 * moment_two + 0.05 * weight_grad * weight_grad
    first_fix = 1.0 - 0.9**STEP
    second_fix = 1.0 - 0.95**STEP
    update = (
        new_moment_one / first_fix / (jnp.sqrt(new_moment_two / second_fix) + 1e-08) + 0.1 * master
    )
    new_master = master - 0.002 * update
    copy_rows = new_master.astype(jnp.bfloat16)
    reordered = regroup(hidden_second)
    group_rows = lax.all_gather(copy_rows, "grp", axis=0, tiled=True)
    columns = reordered
    logits = jnp.dot(
        columns,
        lax.all_gather(group_rows, "dev", axis=0, tiled=True),
        preferred_element_type=jnp.float32,
    )
    top = jnp.max(logits, axis=1, keepdims=True)
    lse = top + jnp.log(jnp.sum(jnp.exp(logits - top), axis=1, keepdims=True))
    onehot = (labels_second[:, None] == jnp.arange(vocab, dtype=jnp.int32)[None, :]).astype(
        jnp.float32
    )
    loss_second = lse[:, 0] - jnp.sum(onehot * logits, axis=1)
    return (new_master, new_moment_one, new_moment_two, loss_second)


def solution(mesh):
    return jax.shard_map(
        on_device,
        mesh=mesh,
        in_specs=(
            P(("grp", "dev"), None),
            P(("grp", "dev"), None),
            P(("grp", "dev"), None),
            P(("grp", "dev")),
            P(("grp", "dev"), None),
            P(("grp", "dev"), None),
            P(("grp", "dev"), None),
        ),
        out_specs=(
            P(("grp", "dev"), None),
            P(("grp", "dev"), None),
            P(("grp", "dev"), None),
            P(("grp", "dev")),
        ),
        check_vma=False,
    )
```

profile of v0, /device:TPU:33, one launch (start us, length us, event | category | flops | bytes accessed | tf_op | source)
XLA Modules:
  0.0 359.6 jit_solution(9039419300726291449)
XLA Ops:
  7.2 0.0 copy-start
  7.2 0.0 reduce-scatter.3.cloned.1.call-start
  7.2 6.4 %copy.11 = bf16[256,8192]{0,1:T(8,128)(2,1)} copy(bf16[256,8192]{1,0:T(8,128)(2,1)} %param.7) | data formatting | bytes 8388608 | tf_op args[0]
  13.7 2.6 copy.12
  16.3 0.0 copy-done
  16.3 8.1 %fusion.7 = f32[8192,512]{1,0:T(8,128)} fusion(bf16[256,8192]{0,1:T(8,128)(2,1)S(1)} %bitcast.24, bf16[256,512]{1,0:T(8,128)(2,1)S(1)} %copy-done), kind=kOutput, calls=%fused_computation.13 | convolution fusion | flops 2147483648 | bytes 21233664 | tf_op jit(solution)/shard_map/tc,tv->cv/dot_general | solution.py:27
  24.4 0.0 copy-start.1
  24.4 0.0 copy-start.2
  24.4 0.0 copy-start.3
  24.4 0.0 reduce-scatter.3.cloned.1.call-update
  24.4 0.0 reduce-scatter.5.cloned.1.call-start
  24.5 168.7 %reduce-scatter.3.cloned.1.call-done = f32[256,512]{1,0:T(8,128)} async-done(((f32[8192,512]{1,0:T(8,128)}), f32[256,512]{1,0:T(8,128)}) %reduce-scatter.3.cloned.1.call-update) | async-done | bytes 524304 | tf_op jit(solution)/shard_map/reduce_scatter | solution.py:26
  193.1 0.0 reduce-scatter.5.cloned.1.call-update
  193.2 0.0 all-gather.2.cloned.1.call-start
  193.2 35.5 %reduce-scatter.5.cloned.1.call-done = f32[32,512]{1,0:T(8,128)} async-done(((f32[256,512]{1,0:T(8,128)}), f32[32,512]{1,0:T(8,128)}) %reduce-scatter.5.cloned.1.call-update) | async-done | bytes 65552 | tf_op jit(solution)/shard_map/reduce_scatter | solution.py:32
  228.7 0.0 copy-done.1
  228.7 0.0 copy-done.2
  228.7 0.0 copy-done.3
  228.7 1.5 fusion.4
  230.3 24.5 %all_gather.6 = bf16[256,512]{1,0:T(8,128)(2,1)} all-gather(bf16[32,512]{1,0:T(8,128)(2,1)S(1)} %get-tuple-element.6), channel_id=1, replica_groups=mesh['grp'=8,'dev'=32] {'grp'}, dimensions={0}, use_global_device_ids=true | all-gather | bytes 294912 | tf_op jit(solution)/shard_map/all_gather | solution.py:43
  254.8 0.0 all-gather.2.cloned.1.call-update
  254.8 6.4 %copy.13 = bf16[256,8192]{0,1:T(8,128)(2,1)} copy(bf16[256,8192]{1,0:T(8,128)(2,1)} %param.9) | data formatting | bytes 8388608 | tf_op args[2]
  261.2 4.8 %copy.14 = bf16[256,32,8,32]{0,3,2,1:T(8,128)(2,1)} copy(bf16[256,32,8,32]{0,3,1,2:T(8,128)(2,1)} %bitcast.23) | data formatting | bytes 8388608 | tf_op jit(solution)/shard_map/transpose | solution.py:21
  266.0 79.4 %all-gather.2.cloned.1.call-done = bf16[8192,512]{1,0:T(8,128)(2,1)} async-done(((bf16[256,512]{1,0:T(8,128)(2,1)}), bf16[8192,512]{1,0:T(8,128)(2,1)}) %all-gather.2.cloned.1.call-update) | async-done | bytes 8388624 | tf_op jit(solution)/shard_map/all_gather | solution.py:47
  345.4 0.0 copy-start.4
  345.4 7.0 %fusion.6 = (f32[256]{0:T(256)S(1)}, f32[512,256]{1,0:T(8,128)S(1)}) fusion(bf16[8192,512]{1,0:T(8,128)(2,1)} %all-gather.2.cloned.1.call-done, bf16[256,8192]{0,1:T(8,128)(2,1)} %bitcast.21), kind=kOutput, calls=%fused_computation.12 | convolution fusion | flops 2147614464 | bytes 13108224 | tf_op jit(solution)/shard_map/dot_general | solution.py:45
  352.3 0.0 copy-done.4
  352.3 0.2 fusion.1
  352.5 0.6 add_subtract_fusion
Async XLA Ops:
  7.2 9.1 %copy-start = (bf16[256,512]{1,0:T(8,128)(2,1)S(1)}, bf16[256,512]{1,0:T(8,128)(2,1)}, u32[]{:S(2)}) copy-start(bf16[256,512]{1,0:T(8,128)(2,1)} %param.8) | copy-start | bytes 786436
  7.2 186.0 %reduce-scatter.3.cloned.1.call-start = ((), (), s32[]{:S(2)}) async-start(), calls=%async_computation.2 | async-start | bytes 17301504 | tf_op jit(solution)/shard_map/reduce_scatter | solution.py:26
  24.4 204.4 %copy-start.1 = (f32[32,512]{1,0:T(8,128)S(1)}, f32[32,512]{1,0:T(8,128)}, u32[]{:S(2)}) copy-start(f32[32,512]{1,0:T(8,128)} %param.11) | copy-start | bytes 196612
  24.4 204.4 %copy-start.2 = (f32[32,512]{1,0:T(8,128)S(1)}, f32[32,512]{1,0:T(8,128)}, u32[]{:S(2)}) copy-start(f32[32,512]{1,0:T(8,128)} %param.12) | copy-start | bytes 196612
  24.4 204.4 %copy-start.3 = (f32[32,512]{1,0:T(8,128)S(1)}, f32[32,512]{1,0:T(8,128)}, u32[]{:S(2)}) copy-start(f32[32,512]{1,0:T(8,128)} %param.13) | copy-start | bytes 196612
  24.4 204.3 %reduce-scatter.5.cloned.1.call-start = ((), (), s32[]{:S(2)}) async-start(), calls=%async_computation.3 | async-start | bytes 589824 | tf_op jit(solution)/shard_map/reduce_scatter | solution.py:32
  193.2 152.2 %all-gather.2.cloned.1.call-start = ((), (), s32[]{:S(2)}) async-start(), calls=%async_computation.4 | async-start | bytes 8650752 | tf_op jit(solution)/shard_map/all_gather | solution.py:47
  345.4 7.0 %copy-start.4 = (s32[256]{0:T(256)S(1)}, s32[256]{0:T(256)}, u32[]{:S(2)}) copy-start(s32[256]{0:T(256)} %param.10) | copy-start | bytes 3076
Sparse Core Ops, SparseCore 0:
  24.5 168.5 reduce-scatter.2
  195.6 33.0 reduce-scatter.4
  254.9 90.4 all-gather.1
where the time goes:
time: 360 us
  waiting for transfers between devices  284 us (79%)
  blocking collectives  24.5 us (7%)
  local copies, waits for them, and re-layouts  20.3 us (6%)
  matrix products  15 us (4%)
  between operations  13.8 us (4%)
    reduce_scatter x1, waiting for transfers between devices, on_device(): lax.psum_scatter(jnp.einsum('tc,tv->cv', columns, logit_grads, preferred_...  169 us
    all_gather x1, waiting for transfers between devices, on_device(): lax.all_gather(group_rows, 'dev', axis=0, tiled=True)  79.4 us
    reduce_scatter x1, waiting for transfers between devices, on_device(): lax.psum_scatter(group_sum, 'grp', scatter_dimension=0, tiled=True)  35.5 us
    all_gather x1, blocking collectives, on_device(): group_rows = lax.all_gather(copy_rows, 'grp', axis=0, tiled=True)  24.5 us
    unnamed x12, local copies, waits for them, and re-layouts  12.9 us
    dot_general x1, matrix products, on_device(): jnp.einsum('tc,tv->cv', columns, logit_grads, preferred_element_type=jnp....  8.08 us
    transpose x2, local copies, waits for them, and re-layouts, regroup(): return hidden.reshape(rows, groups, members, owned).transpose(0, 2, 1, 3)...  7.41 us
  transfers between devices with their start and end apart: 3, of which 3 were waited for; matrix products, arithmetic and copies ran while one was open for 3% of the time, Pallas kernels for 0%

commit v1 on v0

v1 whole, which is shorter than its diff:
```python
import jax
import jax.numpy as jnp
from jax import lax
from jax.experimental import pallas as pl
from jax.experimental.pallas import tpu as pltpu
from jax.sharding import Mesh
from jax.sharding import PartitionSpec as P

STEP = 10
AXES = ("x", "zl", "y", "zh", "c")
SIZES = (4, 2, 4, 4, 2)
F32, BF16, I16, I32 = jnp.float32, jnp.bfloat16, jnp.int16, jnp.int32
T = 128
PARAMS = pltpu.CompilerParams(vmem_limit_bytes=52 * 1024 * 1024)


def encode(tile):
    most = jnp.max(jnp.abs(tile), axis=0, keepdims=True)
    level = jnp.floor(8.0 * (14.98 - jnp.log2(jnp.maximum(most, 1e-30))))
    scale = jnp.exp2(level * 0.125)
    return jnp.round(tile * scale).astype(I32).astype(I16), level


def rows(i, n=T):
    return slice(i * n, (i + 1) * n)


def levels_tile(levels):
    short = 16 - len(levels)
    if short:
        levels = levels + [jnp.zeros((short, T), F32)]
    return jnp.concatenate(levels, axis=0).astype(I32).astype(I16)


def scales_of(ref, first):
    level = ref[first : first + 16, :].astype(I32).astype(F32)
    return jnp.exp2(level * -0.125)


def decode(ref, i, inverse):
    return ref[rows(i), :].astype(I32).astype(F32) * inverse[i : i + 1, :]


def grad_kernel(place, h, hr, l, lr, x0, x1, x2, x3, y0, y1, y2, y3, lt, prod, ylevels):
    k = pl.program_id(0)
    y = place[1]

    @pl.when(k == 0)
    def _():
        lt[:, 0:256] = l[...].T
        lt[:, 256:512] = lr[...].T

    prod[...] = jnp.dot(lt[:, 0:256], h[...], preferred_element_type=F32) + jnp.dot(
        lt[:, 256:512], hr[...], preferred_element_type=F32
    )

    def lanes(zl, j, half):
        at = zl * 1024 + lax.rem(y + j, 4) * 256 + half * T
        return pl.ds(pl.multiple_of(at, T), T)

    for step, out in enumerate((x0, x1, x2, x3)):

        @pl.when(k == step)
        def _(step=step, out=out):
            levels = []
            for zl in range(2):
                for j in range(4):
                    for half in range(2):
                        tile = prod[0:T, lanes(zl, j, half)]
                        i = zl * 8 + j * 2 + half
                        if step == 0:
                            out[rows(i), :] = tile
                        else:
                            out[rows(i), :], level = encode(tile)
                            levels.append(level)
            if step:
                out[2048:2064, :] = levels_tile(levels)

    for j, out in enumerate((y0, y1, y2, y3)):
        for zl in range(2):
            for half in range(2):
                tile = prod[T : 2 * T, lanes(zl, j, half)]
                i = k * 4 + zl * 2 + half
                at = pl.ds(pl.multiple_of(i * T, T), T)
                if j == 0:
                    out[at, :] = tile
                else:
                    out[at, :], level = encode(tile)
                    ylevels[j - 1, pl.ds(i, 1), :] = level

    @pl.when(k == 3)
    def _():
        for j, out in enumerate((y1, y2, y3)):
            out[2048:2064, :] = ylevels[j].astype(I32).astype(I16)


def first_sum_kernel(x0, x1, x2, x3, y0, y1, y2, y3, xs0, xs1, xs2, xs3, ys0, ys1, ys2, ys3):
    for own, taken, outs, index in (
        (x0, (x1, x2, x3), (xs0, xs1, xs2, xs3), lambda d, zl, half: zl * 8 + d * 2 + half),
        (y0, (y1, y2, y3), (ys0, ys1, ys2, ys3), lambda d, zl, half: d * 4 + zl * 2 + half),
    ):
        inverse = [scales_of(r, 2048) for r in taken]
        for d, out in enumerate(outs):
            levels = []
            for zl in range(2):
                for half in range(2):
                    i = index(d, zl, half)
                    total = own[rows(i), :]
                    for r, s in zip(taken, inverse):
                        total += decode(r, i, s)
                    o = zl * 2 + half
                    if d == 0:
                        out[rows(o), :] = total
                    else:
                        out[rows(o), :], level = encode(total)
                        levels.append(level)
            if d:
                out[512:528, :] = levels_tile(levels)


def second_sum_kernel(x0, x1, x2, x3, y0, y1, y2, y3, out):
    sx = [scales_of(r, 512) for r in (x1, x2, x3)]
    sy = [scales_of(r, 512) for r in (y1, y2, y3)]
    low = lax.broadcasted_iota(I32, (T, T), 1) < 64
    for zl in range(2):
        for half in range(2):
            i = zl * 2 + half
            a, b = x0[rows(i), :], y0[rows(i), :]
            for r, s in zip((x1, x2, x3), sx):
                a += decode(r, i, s)
            for r, s in zip((y1, y2, y3), sy):
                b += decode(r, i, s)
            first = jnp.where(low, a, pltpu.roll(b, 64, 1))
            second = jnp.where(low, pltpu.roll(a, 64, 1), b)
            for n, tile in ((0, first), (1, second)):
                at = (zl * 4 + half * 2 + n) * 144
                out[at : at + T, :], level = encode(tile)
                out[at + T : at + 144, :] = levels_tile([level])


def third_sum_kernel(taken, out):
    total = None
    for n in range(8):
        at = n * 144
        inverse = scales_of(taken, at + T)[0:1, :]
        part = taken[at : at + T, :].astype(I32).astype(F32) * inverse
        total = part if total is None else total + part
    out[...] = total.T


def adam_kernel(place, own, other, master, one, two, new_master, new_one, new_two, copy):
    c = place[2]
    first = pl.ds(pl.multiple_of(c * 32, 32), 32)
    second = pl.ds(pl.multiple_of(64 + c * 32, 32), 32)
    mine = jnp.concatenate([own[first, :], own[second, :]], axis=1)
    theirs = jnp.concatenate([other[first, :], other[second, :]], axis=1)
    grad = jnp.where(
        c == 0,
        jnp.concatenate([mine, theirs], axis=1),
        jnp.concatenate([theirs, mine], axis=1),
    )
    moment_one = 0.9 * one[...] + 0.1 * grad
    moment_two = 0.95 * two[...] + 0.05 * grad * grad
    first_fix = 1.0 - 0.9**STEP
    second_fix = 1.0 - 0.95**STEP
    update = (
        moment_one / first_fix / (jnp.sqrt(moment_two / second_fix) + 1e-08) + 0.1 * master[...]
    )
    weights = master[...] - 0.002 * update
    new_master[...] = weights
    new_one[...] = moment_one
    new_two[...] = moment_two
    copy[...] = weights.astype(BF16)


def spread_kernel(place, own, other, out):
    c = place[2]
    low = pl.ds(pl.multiple_of(c * 256, 256), T)
    high = pl.ds(pl.multiple_of(c * 256 + T, T), T)
    parts = []
    for lanes in (low, high):
        mine, theirs = own[:, lanes], other[:, lanes]
        parts.append(jnp.where(c == 0, mine, theirs))
        parts.append(jnp.where(c == 0, theirs, mine))
    block = jnp.concatenate(parts, axis=0)
    for n in range(8):
        out[rows(n), :] = block


def head_kernel(
    place, h, hr, labels, labels_r, x0, x1, x2, x3, y0, y1, y2, y3, stats, stats_r, logits
):
    k = pl.program_id(0)
    y, c = place[1], place[2]

    for step, wx in enumerate((x0, x1, x2, x3)):

        @pl.when(k == step)
        def _(step=step, wx=wx):
            for n, tokens in enumerate((h, hr)):
                total = None
                for s, wy in enumerate((y0, y1, y2, y3)):
                    for zl in range(2):
                        at = zl * 1024 + lax.rem(y - s + 4, 4) * 256
                        left = tokens[:, pl.ds(pl.multiple_of(at, 256), 256)]
                        a = s * 512 + zl * 256
                        b = step * 512 + zl * 256
                        right = jnp.concatenate([wx[a : a + 256, :], wy[b : b + 256, :]], axis=1)
                        term = jnp.dot(left, right, preferred_element_type=F32)
                        total = term if total is None else total + term
                if step == 0:
                    logits[n] = total
                else:
                    logits[n] += total

    @pl.when(k == 3)
    def _():
        lane = lax.broadcasted_iota(I32, (256, T), 1)
        column = lax.broadcasted_iota(I32, (256, 256), 1) + c * 256
        for n, (label, out) in enumerate(((labels, stats), (labels_r, stats_r))):
            rows_ = logits[n]
            top = jnp.max(rows_, axis=1, keepdims=True)
            total = jnp.sum(jnp.exp(rows_ - top), axis=1, keepdims=True)
            hit = jnp.sum(jnp.where(column == label[...], rows_, 0.0), axis=1, keepdims=True)
            out[...] = jnp.where(lane == 0, top, jnp.where(lane == 1, total, hit))


def loss_kernel(a, b, out):
    top = jnp.maximum(a[:, 0:1], b[:, 0:1])
    total = a[:, 1:2] * jnp.exp(a[:, 0:1] - top) + b[:, 1:2] * jnp.exp(b[:, 0:1] - top)
    loss = top + jnp.log(total) - (a[:, 2:3] + b[:, 2:3])
    out[...] = jnp.broadcast_to(loss, (256, T)).T[0:1, :]


def shape(*dims, dtype=F32):
    return jax.ShapeDtypeStruct(dims, dtype)


def whole(*dims):
    return pl.BlockSpec(dims, lambda *_: (0,) * len(dims))


def simple(kernel, outs, *args, place=None):
    specs = [whole(*a.shape) for a in args]
    many = isinstance(outs, (list, tuple))
    out_specs = [whole(*o.shape) for o in outs] if many else whole(*outs.shape)
    return pl.pallas_call(
        kernel,
        out_shape=outs,
        grid_spec=pltpu.PrefetchScalarGridSpec(
            num_scalar_prefetch=0 if place is None else 1,
            grid=(1,),
            in_specs=specs,
            out_specs=out_specs,
        ),
        compiler_params=PARAMS,
    )(*(() if place is None else (place,)), *args)


def swap(a):
    return lax.ppermute(a, "c", [(0, 1), (1, 0)])


def shift(a, axis, by):
    return lax.ppermute(a, axis, [(i, (i + by) % 4) for i in range(4)])


def on_device(
    hidden_first, logit_grads, hidden_second, labels_second, master, moment_one, moment_two
):
    place = jnp.stack([lax.axis_index("x"), lax.axis_index("y"), lax.axis_index("c")])
    labels = labels_second[:, None]

    other_grads = swap(logit_grads)
    other_first = swap(hidden_first)
    hold = lax.optimization_barrier((other_first, hidden_second, labels))
    other_first = hold[0]
    other_second = swap(hold[1])
    other_labels = swap(hold[2])

    near = pl.BlockSpec((256, 2048), lambda k, p: (0, lax.rem(p[0] + k, 4)))
    half = pl.BlockSpec((256, 256), lambda k, p: (0, p[2]))
    message = shape(2064, T, dtype=I16)
    sums = pl.pallas_call(
        grad_kernel,
        out_shape=[shape(2048, T), message, message, message] * 2,
        grid_spec=pltpu.PrefetchScalarGridSpec(
            num_scalar_prefetch=1,
            grid=(4,),
            in_specs=[near, near, half, half],
            out_specs=[whole(2048, T), whole(2064, T), whole(2064, T), whole(2064, T)] * 2,
            scratch_shapes=[
                pltpu.VMEM((256, 512), BF16),
                pltpu.VMEM((256, 2048), F32),
                pltpu.VMEM((3, 16, T), F32),
            ],
        ),
        compiler_params=PARAMS,
    )(place, hidden_first, other_first, logit_grads, other_grads)

    def cross(blocks, first, second):
        sent = [None] * 8
        for by in (2, 1, 3):
            sent[by] = shift(blocks[by], first, by)
            sent[4 + by] = shift(blocks[4 + by], second, by)
        sent[0], sent[4] = blocks[0], blocks[4]
        return sent

    message = shape(528, T, dtype=I16)
    sums = simple(
        first_sum_kernel,
        [shape(512, T), message, message, message] * 2,
        *cross(sums, "x", "y"),
    )
    chunks = simple(second_sum_kernel, shape(1152, T, dtype=I16), *cross(sums, "y", "x"))
    chunks = lax.all_to_all(chunks, ("zl", "zh"), 0, 0, tiled=True)
    total = simple(third_sum_kernel, shape(T, T), chunks)
    new_master, new_one, new_two, copy = simple(
        adam_kernel,
        [shape(32, 512)] * 3 + [shape(32, 512, dtype=BF16)],
        total,
        swap(total),
        master,
        moment_one,
        moment_two,
        place=place,
    )

    blocks = simple(spread_kernel, shape(1024, T, dtype=BF16), copy, swap(copy), place=place)
    blocks = lax.all_to_all(blocks, ("zl", "zh"), 0, 0, tiled=True).reshape(8, 2, 64, T)
    low, high = (blocks[:, n].reshape(512, T) for n in range(2))
    pieces = cross([low] * 4 + [high] * 4, "y", "x")
    low, high = jnp.concatenate(pieces[:4]), jnp.concatenate(pieces[4:])
    pieces = cross([low] * 4 + [high] * 4, "x", "y")

    back = pl.BlockSpec((256, 2048), lambda k, p: (0, lax.rem(p[0] - k + 4, 4)))
    stats, other_stats = pl.pallas_call(
        head_kernel,
        out_shape=[shape(256, T)] * 2,
        grid_spec=pltpu.PrefetchScalarGridSpec(
            num_scalar_prefetch=1,
            grid=(4,),
            in_specs=[back, back, whole(256, 1), whole(256, 1)] + [whole(2048, T)] * 8,
            out_specs=[whole(256, T)] * 2,
            scratch_shapes=[pltpu.VMEM((2, 256, 256), F32)],
        ),
        compiler_params=PARAMS,
    )(place, hidden_second, other_second, labels, other_labels, *pieces)
    loss = simple(loss_kernel, shape(1, 256), stats, swap(other_stats))
    return new_master, new_one, new_two, loss.reshape(256)


def solution(mesh):
    fine = Mesh(mesh.devices.reshape(SIZES), AXES)
    two, one = P(AXES, None), P(AXES)
    return jax.shard_map(
        on_device,
        mesh=fine,
        in_specs=(two, two, two, one, two, two, two),
        out_specs=(two, two, two, one),
        check_vma=False,
    )
```

time: 360 us -> 201 us (0.56)
  waiting for transfers between devices: 284 us -> 96.8 us
  starting transfers between devices: 0.12 us -> 47.3 us
  Pallas kernels: 0 us -> 23.4 us
  local copies, waits for them, and re-layouts: 20.3 us -> 2.06 us
  matrix products: 15 us -> 0 us
  between operations: 13.8 us -> 0.81 us
  blocking collectives: 24.5 us -> 30 us
    reduce_scatter x2 -> x0, waiting for transfers between devices: 204 us -> none  [the longest x1 169 us: on_device(): lax.psum_scatter(jnp.einsum('tc,tv->cv', columns, logit_grads, preferred_...]
    ppermute x0 -> x31, waiting for transfers between devices: none -> 96.8 us  [the longest x24 85.9 us: shift(): return lax.ppermute(a, axis, [(i, (i + by) % 4) for i in range(4)])]
    all_gather x1 -> x0, waiting for transfers between devices: 79.4 us -> none  [on_device(): lax.all_gather(group_rows, 'dev', axis=0, tiled=True)]
    ppermute x0 -> x31, starting transfers between devices: none -> 47.3 us  [the longest x24 30 us: shift(): return lax.ppermute(a, axis, [(i, (i + by) % 4) for i in range(4)])]
    all_to_all x0 -> x2, blocking collectives: none -> 30 us  [the longest x1 16.3 us: on_device(): chunks = lax.all_to_all(chunks, ('zl', 'zh'), 0, 0, tiled=True)]
    all_gather x1 -> x0, blocking collectives: 24.5 us -> none  [on_device(): group_rows = lax.all_gather(copy_rows, 'grp', axis=0, tiled=True)]
    pallas_call x0 -> x8, Pallas kernels: none -> 23.4 us  [the longest x1 9.47 us: on_device(): pl.pallas_call(grad_kernel, out_shape=[shape(2048, T), message, message,...]
    dot_general x2 -> x0, matrix products: 15 us -> none  [the longest x1 8.08 us: on_device(): jnp.einsum('tc,tv->cv', columns, logit_grads, preferred_element_type=jnp....]
  transfers between devices with their start and end apart: 3 -> 31, of which waited for: 3 -> 17; matrix products, arithmetic and copies ran while one was open for 3% -> 0% of each run, Pallas kernels for 0% -> 8%
where the time goes in v1:
time: 201 us
  waiting for transfers between devices  96.8 us (48%)
  starting transfers between devices  47.3 us (24%)
  blocking collectives  30 us (15%)
  Pallas kernels  23.4 us (12%)
  local copies, waits for them, and re-layouts  2.06 us (1%)
    ppermute x24, waiting for transfers between devices, shift(): return lax.ppermute(a, axis, [(i, (i + by) % 4) for i in range(4)])  85.9 us
    ppermute x24, starting transfers between devices, shift(): return lax.ppermute(a, axis, [(i, (i + by) % 4) for i in range(4)])  30 us
    ppermute x7, starting transfers between devices, swap(): return lax.ppermute(a, 'c', [(0, 1), (1, 0)])  17.3 us
    all_to_all x1, blocking collectives, on_device(): chunks = lax.all_to_all(chunks, ('zl', 'zh'), 0, 0, tiled=True)  16.3 us
    all_to_all x1, blocking collectives, on_device(): lax.all_to_all(blocks, ('zl', 'zh'), 0, 0, tiled=True).reshape(8, 2, 64, T)  13.7 us
    ppermute x7, waiting for transfers between devices, swap(): return lax.ppermute(a, 'c', [(0, 1), (1, 0)])  10.9 us
    pallas_call x1, Pallas kernels, on_device(): pl.pallas_call(grad_kernel, out_shape=[shape(2048, T), message, message,...  9.47 us
    pallas_call x1, Pallas kernels, on_device(): pl.pallas_call(head_kernel, out_shape=[shape(256, T)] * 2, grid_spec=pltp...  7.23 us
  transfers between devices with their start and end apart: 31, of which 17 were waited for; matrix products, arithmetic and copies ran while one was open for 0% of the time, Pallas kernels for 8%

profile of v1, /device:TPU:33, one launch (start us, length us, event | category | flops | bytes accessed | tf_op | source)
XLA Modules:
  0.0 200.5 jit_solution(6206363373910904632)
XLA Ops:
  0.6 0.8 collective-permute-start
  1.5 7.4 %collective-permute-done.hr = bf16[256,8192]{1,0:T(8,128)(2,1)} collective-permute-done((bf16[256,8192]{1,0:T(8,128)(2,1)}, bf16[256,8192]{1,0:T(8,128)(2,1)}, u32[]{:S(2)}, u32[]{:S(2)}) %collective-permute-start) | collective-permute-done | bytes 4194336 | tf_op jit(solution)/shard_map/ppermute | solution.py:261
  9.3 1.0 copy-done
  10.3 9.5 %shard_map.102 = (f32[2048,128]{1,0:T(8,128)}, s16[2064,128]{1,0:T(8,128)(2,1)S(1)}, s16[2064,128]{1,0:T(8,128)(2,1)S(1)}, s16[2064,128]{1,0:T(8,128)(2,1)}, f32...) custom-call(s32[3]{0:T(128)S(1)} %pad_add_fusion.place, ...), custom_call_target="tpu_custom_call" | custom-call | tf_op jit(solution)/shard_map/pallas_call | solution.py:284
  19.8 1.3 collective-permute-start.2
  21.1 2.5 %collective-permute-start.3 = (s16[2064,128]{1,0:T(8,128)(2,1)S(1)}, s16[2064,128]{1,0:T(8,128)(2,1)S(1)}, u32[]{:S(2)}, u32[]{:S(2)}) collective-permute-start(s16[2064,128]{1,0:T(8,128)(2,1)S(1)} %get-tuple-element.32), channel_id=1, source_target_pairs={{0,128},{64,192},{128,0},{192,64},{1,129},{65,193},{129,1},{193,65... | collective-permute-start | bytes 1585160 | tf_op jit(solution)/shard_map/ppermute | solution.py:265
  23.5 1.2 collective-permute-start.4
  24.7 1.3 collective-permute-start.5
  26.0 8.6 %collective-permute-done.2.x1 = s16[2064,128]{1,0:T(8,128)(2,1)S(1)} collective-permute-done((s16[2064,128]{1,0:T(8,128)(2,1)S(1)}, s16[2064,128]{1,0:T(8,128)(2,1)S(1)}, u32[]{:S(2)}, u32[]{:S(2)}) %collective-permute-start.2) | collective-permute-done | bytes 528416 | tf_op jit(solution)/shard_map/ppermute | solution.py:265
  34.5 2.9 %collective-permute-start.6 = (s16[2064,128]{1,0:T(8,128)(2,1)}, s16[2064,128]{1,0:T(8,128)(2,1)S(1)}, u32[]{:S(2)}, u32[]{:S(2)}) collective-permute-start(s16[2064,128]{1,0:T(8,128)(2,1)} %get-tuple-element.36), channel_id=1, source_target_pairs={{0,16},{8,24},{16,0},{24,8},{1,17},{9,25},{17,1},{25,9},{2,18},{10... | collective-permute-start | bytes 1585160 | tf_op jit(solution)/shard_map/ppermute | solution.py:265
  37.5 9.4 %collective-permute-done.3.x2 = s16[2064,128]{1,0:T(8,128)(2,1)S(1)} collective-permute-done((s16[2064,128]{1,0:T(8,128)(2,1)S(1)}, s16[2064,128]{1,0:T(8,128)(2,1)S(1)}, u32[]{:S(2)}, u32[]{:S(2)}) %collective-permute-start.3) | collective-permute-done | bytes 528416 | tf_op jit(solution)/shard_map/ppermute | solution.py:265
  46.9 2.7 %collective-permute-start.7 = (s16[2064,128]{1,0:T(8,128)(2,1)}, s16[2064,128]{1,0:T(8,128)(2,1)S(1)}, u32[]{:S(2)}, u32[]{:S(2)}) collective-permute-start(s16[2064,128]{1,0:T(8,128)(2,1)} %get-tuple-element.37), channel_id=1, source_target_pairs={{0,24},{8,0},{16,8},{24,16},{1,25},{9,1},{17,9},{25,17},{2,26},{10... | collective-permute-start | bytes 1585160 | tf_op jit(solution)/shard_map/ppermute | solution.py:265
  49.6 1.6 collective-permute-done.6.y2
  51.2 10.0 %collective-permute-done.7.y3 = s16[2064,128]{1,0:T(8,128)(2,1)S(1)} collective-permute-done((s16[2064,128]{1,0:T(8,128)(2,1)}, s16[2064,128]{1,0:T(8,128)(2,1)S(1)}, u32[]{:S(2)}, u32[]{:S(2)}) %collective-permute-start.7) | collective-permute-done | bytes 528416 | tf_op jit(solution)/shard_map/ppermute | solution.py:265
  61.2 0.8 copy-done.9
  62.0 3.4 %shard_map.103 = (f32[512,128]{1,0:T(8,128)S(1)}, s16[528,128]{1,0:T(8,128)(2,1)S(1)}, s16[528,128]{1,0:T(8,128)(2,1)S(1)}, s16[528,128]{1,0:T(8,128)(2,1)S(1)},...) custom-call(f32[2048,128]{1,0:T(8,128)} %get-tuple-element.30.x0, ...), custom_call_target="tpu_custom_call" | custom-call | tf_op jit(solution)/shard_map/pallas_call | solution.py:247
  65.4 2.6 %collective-permute-start.10 = (s16[528,128]{1,0:T(8,128)(2,1)S(1)}, s16[528,128]{1,0:T(8,128)(2,1)S(1)}, u32[]{:S(2)}, u32[]{:S(2)}) collective-permute-start(s16[528,128]{1,0:T(8,128)(2,1)S(1)} %get-tuple-element.41), channel_id=1, source_target_pairs={{0,24},{8,0},{16,8},{24,16},{1,25},{9,1},{17,9},{25,17},{2,26},{10... | collective-permute-start | bytes 405512 | tf_op jit(solution)/shard_map/ppermute | solution.py:265
  68.0 0.6 collective-permute-start.11
  68.6 2.5 %collective-permute-start.12 = (s16[528,128]{1,0:T(8,128)(2,1)S(1)}, s16[528,128]{1,0:T(8,128)(2,1)S(1)}, u32[]{:S(2)}, u32[]{:S(2)}) collective-permute-start(s16[528,128]{1,0:T(8,128)(2,1)S(1)} %get-tuple-element.44), channel_id=1, source_target_pairs={{0,128},{64,192},{128,0},{192,64},{1,129},{65,193},{129,1},{193,65... | collective-permute-start | bytes 405512 | tf_op jit(solution)/shard_map/ppermute | solution.py:265
  71.0 1.2 collective-permute-start.13
  72.2 0.8 collective-permute-done.11.y1
  73.0 1.2 collective-permute-start.9
  74.2 2.5 %collective-permute-done.12.y2 = s16[528,128]{1,0:T(8,128)(2,1)S(1)} collective-permute-done((s16[528,128]{1,0:T(8,128)(2,1)S(1)}, s16[528,128]{1,0:T(8,128)(2,1)S(1)}, u32[]{:S(2)}, u32[]{:S(2)}) %collective-permute-start.12) | collective-permute-done | bytes 135200 | tf_op jit(solution)/shard_map/ppermute | solution.py:265
  76.8 2.4 %collective-permute-done.8.x1 = s16[528,128]{1,0:T(8,128)(2,1)S(1)} collective-permute-done((s16[528,128]{1,0:T(8,128)(2,1)S(1)}, s16[528,128]{1,0:T(8,128)(2,1)S(1)}, u32[]{:S(2)}, u32[]{:S(2)}) %collective-permute-start.8) | collective-permute-done | bytes 135200 | tf_op jit(solution)/shard_map/ppermute | solution.py:265
  79.5 16.3 %all_to_all.20 = s16[8,144,128]{2,1,0:T(8,128)(2,1)S(1)} all-to-all(s16[8,144,128]{2,1,0:T(8,128)(2,1)S(1)} %bitcast.11), channel_id=1, replica_groups=mesh['x'=4,'zl'=2,'y'=4,'zh'=4,'c'=2] {'zl','zh'}, dimensions={0} | all-to-all | bytes 589824 | tf_op jit(solution)/shard_map/all_to_all | solution.py:316
  96.0 7.8 %collective-permute-start.14 = (f32[128,128]{1,0:T(8,128)S(1)}, f32[128,128]{1,0:T(8,128)S(1)}, u32[]{:S(2)}, u32[]{:S(2)}) collective-permute-start(f32[128,128]{1,0:T(8,128)S(1)} %shard_map.105.own), channel_id=1, source_target_pairs={{0,1},{1,0},{2,3},{3,2},{4,5},{5,4},{6,7},{7,6},{8,9},{9,8},{10,11... | collective-permute-start | bytes 196616 | tf_op jit(solution)/shard_map/ppermute | solution.py:261
  103.7 0.9 collective-permute-done.14.other
  104.6 1.3 shard_map.106
  106.3 0.9 collective-permute-done.17.other
  107.1 0.6 shard_map.107
  107.7 13.7 %all_to_all.21 = bf16[8,128,128]{2,1,0:T(8,128)(2,1)S(1)} all-to-all(bf16[8,128,128]{2,1,0:T(8,128)(2,1)S(1)} %bitcast.13), channel_id=1, replica_groups=mesh['x'=4,'zl'=2,'y'=4,'zh'=4,'c'=2] {'zl','zh'}, dimensions={0} | all-to-all | bytes 524288 | tf_op jit(solution)/shard_map/all_to_all | solution.py:330
  121.5 0.7 collective-permute-start.25
  122.3 2.0 collective-permute-start.26
  124.2 5.7 %collective-permute-done.24 = bf16[512,128]{1,0:T(8,128)(2,1)S(1)} collective-permute-done((bf16[512,128]{1,0:T(8,128)(2,1)S(1)}, bf16[512,128]{1,0:T(8,128)(2,1)S(1)}, u32[]{:S(2)}, u32[]{:S(2)}) %collective-permute-start.24) | collective-permute-done | bytes 131104 | tf_op jit(solution)/shard_map/ppermute | solution.py:265
  130.1 1.3 collective-permute-start.28
  131.3 2.0 collective-permute-start.18
  133.3 0.6 collective-permute-start.19
  133.9 24.0 %collective-permute-done.18 = bf16[512,128]{1,0:T(8,128)(2,1)S(1)} collective-permute-done((bf16[512,128]{1,0:T(8,128)(2,1)S(1)}, bf16[512,128]{1,0:T(8,128)(2,1)S(1)}, u32[]{:S(2)}, u32[]{:S(2)}) %collective-permute-start.18) | collective-permute-done | bytes 131104 | tf_op jit(solution)/shard_map/ppermute | solution.py:265
  158.1 4.6 %collective-permute-start.16 = (s32[256,1]{1,0:T(8,128)S(1)}, s32[256,1]{1,0:T(8,128)S(1)}, u32[]{:S(2)}, u32[]{:S(2)}) collective-permute-start(s32[256,1]{1,0:T(8,128)S(1)} %copy.11), channel_id=1, source_target_pairs={{0,1},{1,0},{2,3},{3,2},{4,5},{5,4},{6,7},{7,6},{8,9},{9,8},{10,11... | collective-permute-start | bytes 3080 | tf_op jit(solution)/shard_map/ppermute | solution.py:261
  163.0 0.7 collective-permute-done.16.labels_r
  163.7 3.2 %collective-permute-start.22 = (bf16[2048,128]{1,0:T(8,128)(2,1)S(1)}, bf16[2048,128]{1,0:T(8,128)(2,1)}, u32[]{:S(2)}, u32[]{:S(2)}) collective-permute-start(bf16[2048,128]{1,0:T(8,128)(2,1)S(1)} %pad_maximum_fusion.x0), channel_id=1, source_target_pairs={{0,128},{64,192},{128,0},{192,64},{1,129},{65,193},{129,1},{193,65... | collective-permute-start | bytes 1572872 | tf_op jit(solution)/shard_map/ppermute | solution.py:265
  167.0 6.3 %collective-permute-done.29.y3 = bf16[2048,128]{1,0:T(8,128)(2,1)S(1)} collective-permute-done((bf16[2048,128]{1,0:T(8,128)(2,1)S(1)}, bf16[2048,128]{1,0:T(8,128)(2,1)S(1)}, u32[]{:S(2)}, u32[]{:S(2)}) %collective-permute-start.29) | collective-permute-done | bytes 524320 | tf_op jit(solution)/shard_map/ppermute | solution.py:265
  173.3 10.1 %collective-permute-done.22.x2 = bf16[2048,128]{1,0:T(8,128)(2,1)} collective-permute-done((bf16[2048,128]{1,0:T(8,128)(2,1)S(1)}, bf16[2048,128]{1,0:T(8,128)(2,1)}, u32[]{:S(2)}, u32[]{:S(2)}) %collective-permute-start.22) | collective-permute-done | bytes 524320 | tf_op jit(solution)/shard_map/ppermute | solution.py:265
  183.4 4.6 %collective-permute-done.23.x3 = bf16[2048,128]{1,0:T(8,128)(2,1)} collective-permute-done((bf16[2048,128]{1,0:T(8,128)(2,1)S(1)}, bf16[2048,128]{1,0:T(8,128)(2,1)}, u32[]{:S(2)}, u32[]{:S(2)}) %collective-permute-start.23) | collective-permute-done | bytes 524320 | tf_op jit(solution)/shard_map/ppermute | solution.py:265
  188.0 7.2 %shard_map.108 = (f32[256,128]{1,0:T(8,128)S(1)}, f32[256,128]{1,0:T(8,128)S(1)}) custom-call(s32[3]{0:T(128)S(1)} %pad_add_fusion.place, bf16[256,8192]{1,0:T(8,128)(2,1)} %h.3, bf16[256,8192]{1,0:T(8,128)(2,1)} %collective-permute-done.15.hr, s32[256,1]{1,0:T(8,128)S(1)} %copy.12.labels, s32[256,1]{1,0:T(8,128)S(1)} %collective-permute-done.16.labels_r, ...), custom_call_target="tpu_custom_call" | custom-call | tf_op jit(solution)/shard_map/pallas_call | solution.py:337
  195.3 3.3 %collective-permute-start.30 = (f32[256,128]{1,0:T(8,128)S(1)}, f32[256,128]{1,0:T(8,128)S(1)}, u32[]{:S(2)}, u32[]{:S(2)}) collective-permute-start(f32[256,128]{1,0:T(8,128)S(1)} %get-tuple-element.53), channel_id=1, source_target_pairs={{0,1},{1,0},{2,3},{3,2},{4,5},{5,4},{6,7},{7,6},{8,9},{9,8},{10,11... | collective-permute-start | bytes 393224 | tf_op jit(solution)/shard_map/ppermute | solution.py:261
  198.6 1.0 collective-permute-done.30.b
  199.6 0.9 shard_map.109
  (58 shorter events, 2.3 us)
Async XLA Ops:
  0.6 8.3 %collective-permute-start = (bf16[256,8192]{1,0:T(8,128)(2,1)}, bf16[256,8192]{1,0:T(8,128)(2,1)}, u32[]{:S(2)}, u32[]{:S(2)}) collective-permute-start(bf16[256,8192]{1,0:T(8,128)(2,1)} %h.2), channel_id=1, source_target_pairs={{0,1},{1,0},{2,3},{3,2},{4,5},{5,4},{6,7},{7,6},{8,9},{9,8},{10,11... | collective-permute-start | bytes 12582920 | tf_op jit(solution)/shard_map/ppermute | solution.py:261
  1.4 8.0 %collective-permute-start.1 = (bf16[256,512]{1,0:T(8,128)(2,1)}, bf16[256,512]{1,0:T(8,128)(2,1)S(1)}, u32[]{:S(2)}, u32[]{:S(2)}) collective-permute-start(bf16[256,512]{1,0:T(8,128)(2,1)} %l.1), channel_id=1, source_target_pairs={{0,1},{1,0},{2,3},{3,2},{4,5},{5,4},{6,7},{7,6},{8,9},{9,8},{10,11... | collective-permute-start | bytes 786440 | tf_op jit(solution)/shard_map/ppermute | solution.py:261
  8.9 179.1 %collective-permute-start.15 = (bf16[256,8192]{1,0:T(8,128)(2,1)}, bf16[256,8192]{1,0:T(8,128)(2,1)}, u32[]{:S(2)}, u32[]{:S(2)}) collective-permute-start(bf16[256,8192]{1,0:T(8,128)(2,1)} %h.3), channel_id=1, source_target_pairs={{0,1},{1,0},{2,3},{3,2},{4,5},{5,4},{6,7},{7,6},{8,9},{9,8},{10,11... | collective-permute-start | bytes 12582920 | tf_op jit(solution)/shard_map/ppermute | solution.py:261
  9.3 1.0 copy-start
  19.8 84.9 %copy-start.1 = (f32[32,512]{1,0:T(8,128)S(1)}, f32[32,512]{1,0:T(8,128)}, u32[]{:S(2)}) copy-start(f32[32,512]{1,0:T(8,128)} %master.1) | copy-start | bytes 196612
  19.8 84.9 %copy-start.2 = (f32[32,512]{1,0:T(8,128)S(1)}, f32[32,512]{1,0:T(8,128)}, u32[]{:S(2)}) copy-start(f32[32,512]{1,0:T(8,128)} %one.1) | copy-start | bytes 196612
  19.8 84.9 %copy-start.3 = (f32[32,512]{1,0:T(8,128)S(1)}, f32[32,512]{1,0:T(8,128)}, u32[]{:S(2)}) copy-start(f32[32,512]{1,0:T(8,128)} %two.1) | copy-start | bytes 196612
  19.8 14.8 %collective-permute-start.2 = (s16[2064,128]{1,0:T(8,128)(2,1)S(1)}, s16[2064,128]{1,0:T(8,128)(2,1)S(1)}, u32[]{:S(2)}, u32[]{:S(2)}) collective-permute-start(s16[2064,128]{1,0:T(8,128)(2,1)S(1)} %get-tuple-element.31), channel_id=1, source_target_pairs={{0,64},{64,128},{128,192},{192,0},{1,65},{65,129},{129,193},{193,1... | collective-permute-start | bytes 1585160 | tf_op jit(solution)/shard_map/ppermute | solution.py:265
  21.1 25.8 %collective-permute-start.3 = (s16[2064,128]{1,0:T(8,128)(2,1)S(1)}, s16[2064,128]{1,0:T(8,128)(2,1)S(1)}, u32[]{:S(2)}, u32[]{:S(2)}) collective-permute-start(s16[2064,128]{1,0:T(8,128)(2,1)S(1)} %get-tuple-element.32), channel_id=1, source_target_pairs={{0,128},{64,192},{128,0},{192,64},{1,129},{65,193},{129,1},{193,65... | collective-permute-start | bytes 1585160 | tf_op jit(solution)/shard_map/ppermute | solution.py:265
  23.5 26.1 %collective-permute-start.4 = (s16[2064,128]{1,0:T(8,128)(2,1)}, s16[2064,128]{1,0:T(8,128)(2,1)S(1)}, u32[]{:S(2)}, u32[]{:S(2)}) collective-permute-start(s16[2064,128]{1,0:T(8,128)(2,1)} %get-tuple-element.33), channel_id=1, source_target_pairs={{0,192},{64,0},{128,64},{192,128},{1,193},{65,1},{129,65},{193,129... | collective-permute-start | bytes 1585160 | tf_op jit(solution)/shard_map/ppermute | solution.py:265
  24.7 24.9 %collective-permute-start.5 = (s16[2064,128]{1,0:T(8,128)(2,1)}, s16[2064,128]{1,0:T(8,128)(2,1)S(1)}, u32[]{:S(2)}, u32[]{:S(2)}) collective-permute-start(s16[2064,128]{1,0:T(8,128)(2,1)} %get-tuple-element.35), channel_id=1, source_target_pairs={{0,8},{8,16},{16,24},{24,0},{1,9},{9,17},{17,25},{25,1},{2,10},{10... | collective-permute-start | bytes 1585160 | tf_op jit(solution)/shard_map/ppermute | solution.py:265
  34.5 16.6 %collective-permute-start.6 = (s16[2064,128]{1,0:T(8,128)(2,1)}, s16[2064,128]{1,0:T(8,128)(2,1)S(1)}, u32[]{:S(2)}, u32[]{:S(2)}) collective-permute-start(s16[2064,128]{1,0:T(8,128)(2,1)} %get-tuple-element.36), channel_id=1, source_target_pairs={{0,16},{8,24},{16,0},{24,8},{1,17},{9,25},{17,1},{25,9},{2,18},{10... | collective-permute-start | bytes 1585160 | tf_op jit(solution)/shard_map/ppermute | solution.py:265
  46.9 14.3 %copy-start.5 = (s16[2064,128]{1,0:T(8,128)(2,1)}, s16[2064,128]{1,0:T(8,128)(2,1)S(1)}, u32[]{:S(2)}) copy-start(s16[2064,128]{1,0:T(8,128)(2,1)S(1)} %collective-permute-done.3.x2) | copy-start | bytes 1585156
  46.9 14.3 %collective-permute-start.7 = (s16[2064,128]{1,0:T(8,128)(2,1)}, s16[2064,128]{1,0:T(8,128)(2,1)S(1)}, u32[]{:S(2)}, u32[]{:S(2)}) collective-permute-start(s16[2064,128]{1,0:T(8,128)(2,1)} %get-tuple-element.37), channel_id=1, source_target_pairs={{0,24},{8,0},{16,8},{24,16},{1,25},{9,1},{17,9},{25,17},{2,26},{10... | collective-permute-start | bytes 1585160 | tf_op jit(solution)/shard_map/ppermute | solution.py:265
  49.6 11.6 %copy-start.6 = (s16[2064,128]{1,0:T(8,128)(2,1)}, s16[2064,128]{1,0:T(8,128)(2,1)S(1)}, u32[]{:S(2)}) copy-start(s16[2064,128]{1,0:T(8,128)(2,1)S(1)} %collective-permute-done.4.x3) | copy-start | bytes 1585156
  49.6 11.6 %copy-start.7 = (s16[2064,128]{1,0:T(8,128)(2,1)}, s16[2064,128]{1,0:T(8,128)(2,1)S(1)}, u32[]{:S(2)}) copy-start(s16[2064,128]{1,0:T(8,128)(2,1)S(1)} %collective-permute-done.5.y1) | copy-start | bytes 1585156
  51.2 10.0 %copy-start.8 = (s16[2064,128]{1,0:T(8,128)(2,1)}, s16[2064,128]{1,0:T(8,128)(2,1)S(1)}, u32[]{:S(2)}) copy-start(s16[2064,128]{1,0:T(8,128)(2,1)S(1)} %collective-permute-done.6.y2) | copy-start | bytes 1585156
  61.2 0.8 copy-start.9
  62.0 95.9 %copy-start.13 = (s32[256]{0:T(256)S(1)}, s32[256]{0:T(256)}, u32[]{:S(2)}) copy-start(s32[256]{0:T(256)} %param.10) | copy-start | bytes 3076
  65.4 6.9 %collective-permute-start.10 = (s16[528,128]{1,0:T(8,128)(2,1)S(1)}, s16[528,128]{1,0:T(8,128)(2,1)S(1)}, u32[]{:S(2)}, u32[]{:S(2)}) collective-permute-start(s16[528,128]{1,0:T(8,128)(2,1)S(1)} %get-tuple-element.41), channel_id=1, source_target_pairs={{0,24},{8,0},{16,8},{24,16},{1,25},{9,1},{17,9},{25,17},{2,26},{10... | collective-permute-start | bytes 405512 | tf_op jit(solution)/shard_map/ppermute | solution.py:265
  68.0 5.1 %collective-permute-start.11 = (s16[528,128]{1,0:T(8,128)(2,1)S(1)}, s16[528,128]{1,0:T(8,128)(2,1)S(1)}, u32[]{:S(2)}, u32[]{:S(2)}) collective-permute-start(s16[528,128]{1,0:T(8,128)(2,1)S(1)} %get-tuple-element.43), channel_id=1, source_target_pairs={{0,64},{64,128},{128,192},{192,0},{1,65},{65,129},{129,193},{193,1... | collective-permute-start | bytes 405512 | tf_op jit(solution)/shard_map/ppermute | solution.py:265
  68.6 8.2 %collective-permute-start.12 = (s16[528,128]{1,0:T(8,128)(2,1)S(1)}, s16[528,128]{1,0:T(8,128)(2,1)S(1)}, u32[]{:S(2)}, u32[]{:S(2)}) collective-permute-start(s16[528,128]{1,0:T(8,128)(2,1)S(1)} %get-tuple-element.44), channel_id=1, source_target_pairs={{0,128},{64,192},{128,0},{192,64},{1,129},{65,193},{129,1},{193,65... | collective-permute-start | bytes 405512 | tf_op jit(solution)/shard_map/ppermute | solution.py:265
  71.0 5.8 %collective-permute-start.13 = (s16[528,128]{1,0:T(8,128)(2,1)S(1)}, s16[528,128]{1,0:T(8,128)(2,1)S(1)}, u32[]{:S(2)}, u32[]{:S(2)}) collective-permute-start(s16[528,128]{1,0:T(8,128)(2,1)S(1)} %get-tuple-element.45), channel_id=1, source_target_pairs={{0,192},{64,0},{128,64},{192,128},{1,193},{65,1},{129,65},{193,129... | collective-permute-start | bytes 405512 | tf_op jit(solution)/shard_map/ppermute | solution.py:265
  72.2 6.9 %collective-permute-start.8 = (s16[528,128]{1,0:T(8,128)(2,1)S(1)}, s16[528,128]{1,0:T(8,128)(2,1)S(1)}, u32[]{:S(2)}, u32[]{:S(2)}) collective-permute-start(s16[528,128]{1,0:T(8,128)(2,1)S(1)} %get-tuple-element.39), channel_id=1, source_target_pairs={{0,8},{8,16},{16,24},{24,0},{1,9},{9,17},{17,25},{25,1},{2,10},{10... | collective-permute-start | bytes 405512 | tf_op jit(solution)/shard_map/ppermute | solution.py:265
  73.0 6.1 %collective-permute-start.9 = (s16[528,128]{1,0:T(8,128)(2,1)S(1)}, s16[528,128]{1,0:T(8,128)(2,1)S(1)}, u32[]{:S(2)}, u32[]{:S(2)}) collective-permute-start(s16[528,128]{1,0:T(8,128)(2,1)S(1)} %get-tuple-element.40), channel_id=1, source_target_pairs={{0,16},{8,24},{16,0},{24,8},{1,17},{9,25},{17,1},{25,9},{2,18},{10... | collective-permute-start | bytes 405512 | tf_op jit(solution)/shard_map/ppermute | solution.py:265
  96.0 8.7 %collective-permute-start.14 = (f32[128,128]{1,0:T(8,128)S(1)}, f32[128,128]{1,0:T(8,128)S(1)}, u32[]{:S(2)}, u32[]{:S(2)}) collective-permute-start(f32[128,128]{1,0:T(8,128)S(1)} %shard_map.105.own), channel_id=1, source_target_pairs={{0,1},{1,0},{2,3},{3,2},{4,5},{5,4},{6,7},{7,6},{8,9},{9,8},{10,11... | collective-permute-start | bytes 196616 | tf_op jit(solution)/shard_map/ppermute | solution.py:261
  105.9 1.2 collective-permute-start.17
  121.5 8.5 %collective-permute-start.24 = (bf16[512,128]{1,0:T(8,128)(2,1)S(1)}, bf16[512,128]{1,0:T(8,128)(2,1)S(1)}, u32[]{:S(2)}, u32[]{:S(2)}) collective-permute-start(bf16[512,128]{1,0:T(8,128)(2,1)S(1)} %bitcast.19), channel_id=1, source_target_pairs={{0,64},{64,128},{128,192},{192,0},{1,65},{65,129},{129,193},{193,1... | collective-permute-start | bytes 393224 | tf_op jit(solution)/shard_map/ppermute | solution.py:265
  121.5 8.4 %collective-permute-start.25 = (bf16[512,128]{1,0:T(8,128)(2,1)S(1)}, bf16[512,128]{1,0:T(8,128)(2,1)S(1)}, u32[]{:S(2)}, u32[]{:S(2)}) collective-permute-start(bf16[512,128]{1,0:T(8,128)(2,1)S(1)} %bitcast.20), channel_id=1, source_target_pairs={{0,128},{64,192},{128,0},{192,64},{1,129},{65,193},{129,1},{193,65... | collective-permute-start | bytes 393224 | tf_op jit(solution)/shard_map/ppermute | solution.py:265
  122.3 7.7 %collective-permute-start.26 = (bf16[512,128]{1,0:T(8,128)(2,1)S(1)}, bf16[512,128]{1,0:T(8,128)(2,1)S(1)}, u32[]{:S(2)}, u32[]{:S(2)}) collective-permute-start(bf16[512,128]{1,0:T(8,128)(2,1)S(1)} %bitcast.21), channel_id=1, source_target_pairs={{0,192},{64,0},{128,64},{192,128},{1,193},{65,1},{129,65},{193,129... | collective-permute-start | bytes 393224 | tf_op jit(solution)/shard_map/ppermute | solution.py:265
  130.0 58.1 %copy-start.4 = (bf16[2048,128]{1,0:T(8,128)(2,1)}, bf16[2048,128]{1,0:T(8,128)(2,1)S(1)}, u32[]{:S(2)}) copy-start(bf16[2048,128]{1,0:T(8,128)(2,1)S(1)} %pad_maximum_fusion.1.y0) | copy-start | bytes 1572868
  130.0 33.7 %collective-permute-start.27 = (bf16[2048,128]{1,0:T(8,128)(2,1)S(1)}, bf16[2048,128]{1,0:T(8,128)(2,1)S(1)}, u32[]{:S(2)}, u32[]{:S(2)}) collective-permute-start(bf16[2048,128]{1,0:T(8,128)(2,1)S(1)} %pad_maximum_fusion.1.y0), channel_id=1, source_target_pairs={{0,8},{8,16},{16,24},{24,0},{1,9},{9,17},{17,25},{25,1},{2,10},{10... | collective-permute-start | bytes 1572872 | tf_op jit(solution)/shard_map/ppermute | solution.py:265
  130.1 36.8 %collective-permute-start.28 = (bf16[2048,128]{1,0:T(8,128)(2,1)S(1)}, bf16[2048,128]{1,0:T(8,128)(2,1)S(1)}, u32[]{:S(2)}, u32[]{:S(2)}) collective-permute-start(bf16[2048,128]{1,0:T(8,128)(2,1)S(1)} %pad_maximum_fusion.1.y0), channel_id=1, source_target_pairs={{0,16},{8,24},{16,0},{24,8},{1,17},{9,25},{17,1},{25,9},{2,18},{10... | collective-permute-start | bytes 1572872 | tf_op jit(solution)/shard_map/ppermute | solution.py:265
  131.3 26.6 %collective-permute-start.18 = (bf16[512,128]{1,0:T(8,128)(2,1)S(1)}, bf16[512,128]{1,0:T(8,128)(2,1)S(1)}, u32[]{:S(2)}, u32[]{:S(2)}) collective-permute-start(bf16[512,128]{1,0:T(8,128)(2,1)S(1)} %bitcast.15), channel_id=1, source_target_pairs={{0,8},{8,16},{16,24},{24,0},{1,9},{9,17},{17,25},{25,1},{2,10},{10... | collective-permute-start | bytes 393224 | tf_op jit(solution)/shard_map/ppermute | solution.py:265
  133.3 24.7 %collective-permute-start.19 = (bf16[512,128]{1,0:T(8,128)(2,1)S(1)}, bf16[512,128]{1,0:T(8,128)(2,1)S(1)}, u32[]{:S(2)}, u32[]{:S(2)}) collective-permute-start(bf16[512,128]{1,0:T(8,128)(2,1)S(1)} %bitcast.16), channel_id=1, source_target_pairs={{0,16},{8,24},{16,0},{24,8},{1,17},{9,25},{17,1},{25,9},{2,18},{10... | collective-permute-start | bytes 393224 | tf_op jit(solution)/shard_map/ppermute | solution.py:265
  157.9 4.8 %collective-permute-start.20 = (bf16[512,128]{1,0:T(8,128)(2,1)S(1)}, bf16[512,128]{1,0:T(8,128)(2,1)S(1)}, u32[]{:S(2)}, u32[]{:S(2)}) collective-permute-start(bf16[512,128]{1,0:T(8,128)(2,1)S(1)} %bitcast.17), channel_id=1, source_target_pairs={{0,24},{8,0},{16,8},{24,16},{1,25},{9,1},{17,9},{25,17},{2,26},{10... | collective-permute-start | bytes 393224 | tf_op jit(solution)/shard_map/ppermute | solution.py:265
  158.1 5.6 %collective-permute-start.16 = (s32[256,1]{1,0:T(8,128)S(1)}, s32[256,1]{1,0:T(8,128)S(1)}, u32[]{:S(2)}, u32[]{:S(2)}) collective-permute-start(s32[256,1]{1,0:T(8,128)S(1)} %copy.11), channel_id=1, source_target_pairs={{0,1},{1,0},{2,3},{3,2},{4,5},{5,4},{6,7},{7,6},{8,9},{9,8},{10,11... | collective-permute-start | bytes 3080 | tf_op jit(solution)/shard_map/ppermute | solution.py:261
  162.7 10.6 %collective-permute-start.29 = (bf16[2048,128]{1,0:T(8,128)(2,1)S(1)}, bf16[2048,128]{1,0:T(8,128)(2,1)S(1)}, u32[]{:S(2)}, u32[]{:S(2)}) collective-permute-start(bf16[2048,128]{1,0:T(8,128)(2,1)S(1)} %pad_maximum_fusion.1.y0), channel_id=1, source_target_pairs={{0,24},{8,0},{16,8},{24,16},{1,25},{9,1},{17,9},{25,17},{2,26},{10... | collective-permute-start | bytes 1572872 | tf_op jit(solution)/shard_map/ppermute | solution.py:265
  163.7 9.6 %collective-permute-start.21 = (bf16[2048,128]{1,0:T(8,128)(2,1)S(1)}, bf16[2048,128]{1,0:T(8,128)(2,1)S(1)}, u32[]{:S(2)}, u32[]{:S(2)}) collective-permute-start(bf16[2048,128]{1,0:T(8,128)(2,1)S(1)} %pad_maximum_fusion.x0), channel_id=1, source_target_pairs={{0,64},{64,128},{128,192},{192,0},{1,65},{65,129},{129,193},{193,1... | collective-permute-start | bytes 1572872 | tf_op jit(solution)/shard_map/ppermute | solution.py:265
  163.7 24.3 %copy-start.10 = (bf16[2048,128]{1,0:T(8,128)(2,1)}, bf16[2048,128]{1,0:T(8,128)(2,1)S(1)}, u32[]{:S(2)}) copy-start(bf16[2048,128]{1,0:T(8,128)(2,1)S(1)} %collective-permute-done.27.y1) | copy-start | bytes 1572868
  163.7 19.7 %collective-permute-start.22 = (bf16[2048,128]{1,0:T(8,128)(2,1)S(1)}, bf16[2048,128]{1,0:T(8,128)(2,1)}, u32[]{:S(2)}, u32[]{:S(2)}) collective-permute-start(bf16[2048,128]{1,0:T(8,128)(2,1)S(1)} %pad_maximum_fusion.x0), channel_id=1, source_target_pairs={{0,128},{64,192},{128,0},{192,64},{1,129},{65,193},{129,1},{193,65... | collective-permute-start | bytes 1572872 | tf_op jit(solution)/shard_map/ppermute | solution.py:265
  166.8 21.2 %copy-start.11 = (bf16[2048,128]{1,0:T(8,128)(2,1)}, bf16[2048,128]{1,0:T(8,128)(2,1)S(1)}, u32[]{:S(2)}) copy-start(bf16[2048,128]{1,0:T(8,128)(2,1)S(1)} %collective-permute-done.28.y2) | copy-start | bytes 1572868
  166.9 21.2 %collective-permute-start.23 = (bf16[2048,128]{1,0:T(8,128)(2,1)S(1)}, bf16[2048,128]{1,0:T(8,128)(2,1)}, u32[]{:S(2)}, u32[]{:S(2)}) collective-permute-start(bf16[2048,128]{1,0:T(8,128)(2,1)S(1)} %pad_maximum_fusion.x0), channel_id=1, source_target_pairs={{0,192},{64,0},{128,64},{192,128},{1,193},{65,1},{129,65},{193,129... | collective-permute-start | bytes 1572872 | tf_op jit(solution)/shard_map/ppermute | solution.py:265
  173.3 14.7 %copy-start.12 = (bf16[2048,128]{1,0:T(8,128)(2,1)}, bf16[2048,128]{1,0:T(8,128)(2,1)S(1)}, u32[]{:S(2)}) copy-start(bf16[2048,128]{1,0:T(8,128)(2,1)S(1)} %collective-permute-done.29.y3) | copy-start | bytes 1572868
  195.3 4.3 %collective-permute-start.30 = (f32[256,128]{1,0:T(8,128)S(1)}, f32[256,128]{1,0:T(8,128)S(1)}, u32[]{:S(2)}, u32[]{:S(2)}) collective-permute-start(f32[256,128]{1,0:T(8,128)S(1)} %get-tuple-element.53), channel_id=1, source_target_pairs={{0,1},{1,0},{2,3},{3,2},{4,5},{5,4},{6,7},{7,6},{8,9},{9,8},{10,11... | collective-permute-start | bytes 393224 | tf_op jit(solution)/shard_map/ppermute | solution.py:261

commit v2 on v0

v2 whole, which is shorter than its diff:
```python
import jax
import jax.numpy as jnp
from jax import lax
from jax.experimental import pallas as pl
from jax.experimental.pallas import tpu as pltpu
from jax.sharding import Mesh
from jax.sharding import PartitionSpec as P

STEP = 10
AXES = ("x", "zl", "y", "zh", "c")
SIZES = (4, 2, 4, 4, 2)
F32, BF16, I16, I32 = jnp.float32, jnp.bfloat16, jnp.int16, jnp.int32
T = 128
ROUND = 12582912.0
ORDER = (2, 1, 3)


def encode(tiles):
    most = [jnp.max(jnp.abs(tile), axis=0, keepdims=True) for tile in tiles]
    most = jnp.concatenate(most, axis=0)
    level = jnp.floor(8.0 * (14.98 - jnp.log2(jnp.maximum(most, 1e-30))))
    scale = jnp.exp2(level * 0.125)
    whole_numbers = [
        ((tile * scale[i : i + 1, :] + ROUND) - ROUND).astype(I32).astype(I16)
        for i, tile in enumerate(tiles)
    ]
    return whole_numbers, level


def rows(i, n=T):
    return slice(i * n, (i + 1) * n)


def levels_tile(level):
    level = jnp.concatenate([level, jnp.zeros((16 - level.shape[0], T), F32)], axis=0)
    return level.astype(I32).astype(I16)


def scales_of(ref, first):
    level = ref[first : first + 16, :].astype(I32).astype(F32)
    return jnp.exp2(level * -0.125)


def added(refs, i, block=0):
    total = None
    for ref in refs:
        part = ref[block + i * 256 : block + i * 256 + 256, :].astype(I32).astype(F32)
        part *= scales_of(ref, block + 1024)[i : i + 1, :]
        total = part if total is None else total + part
    return total


def turn_kernel(place, l, lr, out):
    out[:, 0:256] = l[...].T
    out[:, 256:512] = lr[...].T


def pick_kernel(place, *refs):
    for i, h in enumerate(refs[:8]):
        refs[8][:, rows(i, 256)] = h[...]


def store(outs, tiles):
    tiles, level = encode(tiles)
    blocks = len(tiles) // 4
    for a in range(blocks):
        out, at = outs[a * len(outs) // blocks], a % (blocks // len(outs)) * 1040
        for i in range(4):
            out[at + i * 256 : at + i * 256 + 256, :] = tiles[a * 4 + i]
        out[at + 1024 : at + 1040, :] = levels_tile(level[rows(a, 4), :])


def grad_kernel(place, lt, *refs):
    hr, outs, tiles = refs[8], refs[9:], []
    for i, h in enumerate(refs[:8]):
        prod = jnp.dot(lt[:, 0:256], h[...], preferred_element_type=F32)
        prod += jnp.dot(lt[:, 256:512], hr[:, rows(i, 256)], preferred_element_type=F32)
        tiles += [prod[:, 0:T], prod[:, T:256]]
    store(outs, tiles)


def sum_kernel(place, *refs):
    taken, out = refs[:-1], refs[-1]
    tiles = []
    for a in range(out.shape[0] // 1040):
        tiles += [added(taken, i, a * 1040) for i in range(4)]
    store([out], tiles)


def second_sum_kernel(m0, m1, m2, m3, out):
    low = lax.broadcasted_iota(I32, (T, T), 1) < 64
    tiles = []
    for i in range(4):
        total = added((m0, m1, m2, m3), i)
        a, b = total[0:T, :], total[T:256, :]
        tiles.append(jnp.where(low, a, pltpu.roll(b, 64, 1)))
        tiles.append(jnp.where(low, pltpu.roll(a, 64, 1), b))
    tiles, level = encode(tiles)
    for i in range(8):
        out[i * 144 : i * 144 + T, :] = tiles[i]
        out[i * 144 + T : i * 144 + 144, :] = levels_tile(level[i : i + 1, :])


def owner_kernel(place, taken, master, one, two, given, kept, sent, out):
    c = place[2]
    total = None
    for n in range(8):
        at = n * 144
        inverse = scales_of(taken, at + T)[0:1, :]
        part = taken[at : at + T, :].astype(I32).astype(F32) * inverse
        total = part if total is None else total + part
    total = total.T
    lanes = pl.ds(pl.multiple_of(c * 256, 256), 256)
    mine = [r[:, lanes] for r in (master, one, two)]
    theirs = [given[rows(n, 32), :] for n in range(3)]
    results, copies = [], []
    for block in range(2):
        grad = jnp.concatenate(
            [total[block * 32 : block * 32 + 32], total[64 + block * 32 : 96 + block * 32]], axis=1
        )
        old, moment_one, moment_two = (
            jnp.where(c == block, a, b) for a, b in zip(mine, theirs)
        )
        moment_one = 0.9 * moment_one + 0.1 * grad
        moment_two = 0.95 * moment_two + 0.05 * grad * grad
        first_fix = 1.0 - 0.9**STEP
        second_fix = 1.0 - 0.95**STEP
        update = (
            moment_one / first_fix / (jnp.sqrt(moment_two / second_fix) + 1e-08) + 0.1 * old
        )
        weights = old - 0.002 * update
        results.append((weights, moment_one, moment_two))
        copies.append(weights.astype(BF16))
    for n in range(3):
        kept[rows(n, 32), :] = jnp.where(c == 0, results[0][n], results[1][n])
        sent[rows(n, 32), :] = jnp.where(c == 0, results[1][n], results[0][n])
    block = jnp.concatenate(
        [copies[0][:, 0:T], copies[1][:, 0:T], copies[0][:, T:], copies[1][:, T:]], axis=0
    )
    for n in range(8):
        out[rows(n), :] = block


def join_kernel(place, kept, given, *outs):
    first = place[2] == 0
    for n, out in enumerate(outs):
        a, b = kept[rows(n, 32), :], given[rows(n, 32), :]
        out[:, 0:256] = jnp.where(first, a, b)
        out[:, 256:512] = jnp.where(first, b, a)


def products(halves, tokens):
    totals = [None, None]
    for i in range(8):
        parts = [
            jnp.concatenate(
                [halves[i // 4][rows((i % 4 * 4 + zh) * 2 + p, 64), :] for zh in range(4)], axis=0
            )
            for p in range(2)
        ]
        weight = jnp.concatenate(parts, axis=1)
        for n in range(2):
            part = jnp.dot(tokens(n, i), weight, preferred_element_type=F32)
            totals[n] = part if i == 0 else totals[n] + part
    return totals


def first_head_kernel(place, w0, w1, *refs):
    total = refs[16]
    for n, term in enumerate(products((w0, w1), lambda n, i: refs[n * 8 + i][...])):
        total[rows(n, 256), :] = term


def next_head_kernel(place, w0, w1, *refs):
    before, total = refs[16:]
    for n, term in enumerate(products((w0, w1), lambda n, i: refs[n * 8 + i][...])):
        total[rows(n, 256), :] = before[rows(n, 256), :] + term


def last_head_kernel(place, w0, w1, *refs):
    before, labels, labels_r, stats, stats_r = refs[2:]
    totals = products((w0, w1), lambda n, i: refs[n][:, rows(i, 256)])
    lane = lax.broadcasted_iota(I32, (256, T), 1)
    column = lax.broadcasted_iota(I32, (256, 256), 1) + place[2] * 256
    for n, (label, out) in enumerate(((labels, stats), (labels_r, stats_r))):
        logits = before[rows(n, 256), :] + totals[n]
        top = jnp.max(logits, axis=1, keepdims=True)
        expsum = jnp.sum(jnp.exp(logits - top), axis=1, keepdims=True)
        hit = jnp.sum(jnp.where(column == label[...], logits, 0.0), axis=1, keepdims=True)
        out[...] = jnp.where(lane == 0, top, jnp.where(lane == 1, expsum, hit))


def loss_kernel(place, a, b, out):
    a, b = a[...].T, b[...].T
    top = jnp.maximum(a[0:1, :], b[0:1, :])
    total = a[1:2, :] * jnp.exp(a[0:1, :] - top) + b[1:2, :] * jnp.exp(b[0:1, :] - top)
    out[...] = top + jnp.log(total) - (a[2:3, :] + b[2:3, :])


def shape(*dims, dtype=F32):
    return jax.ShapeDtypeStruct(dims, dtype)


def whole(*dims):
    return pl.BlockSpec(dims, lambda *_: (0,) * len(dims))


def call(kernel, outs, place, args, specs=None):
    many = isinstance(outs, (list, tuple))
    specs = specs or [None] * len(args)
    specs = [s or whole(*a.shape) for s, a in zip(specs, args)]
    return pl.pallas_call(
        kernel,
        out_shape=outs,
        grid_spec=pltpu.PrefetchScalarGridSpec(
            num_scalar_prefetch=1,
            grid=(1,),
            in_specs=specs,
            out_specs=[whole(*o.shape) for o in outs] if many else whole(*outs.shape),
        ),
        compiler_params=pltpu.CompilerParams(vmem_limit_bytes=16 * 1024 * 1024),
        cost_estimate=pl.CostEstimate(flops=1, bytes_accessed=1, transcendentals=0),
    )(place, *args)


def columns(far, sign, other=False):
    def index(near, zl, place):
        x, y, c = place[0], place[1], place[2]
        c = 1 - c if other else c
        x = x + 8 + sign * (far * (1 - c) + near * c)
        y = y + 8 + sign * (far * c + near * (1 - c))
        return 0, lax.rem(x, 4) * 8 + zl * 4 + lax.rem(y, 4)

    return [
        pl.BlockSpec((256, 256), lambda _, p, near=near, zl=zl: index(near, zl, p))
        for near in range(4)
        for zl in range(2)
    ]


def swap(a):
    return lax.ppermute(a, "c", [(0, 1), (1, 0)])


def send(a, by, first):
    pairs = []
    for i in range(256):
        x, y, c = i // 64, i // 8 % 4, i % 2
        to = (x + by) % 4, (y + by) % 4
        pairs.append((i, i + ((to[0] - x) * 64 if (c == 0) == first else (to[1] - y) * 8)))
    return lax.ppermute(a, AXES, pairs)


def on_device(
    hidden_first, logit_grads, hidden_second, labels_second, master, moment_one, moment_two
):
    hold = lax.optimization_barrier
    place = jnp.stack([lax.axis_index("x"), lax.axis_index("y"), lax.axis_index("c")])
    labels = labels_second[:, None]
    states = (master, moment_one, moment_two)
    far_half = (1 - place[2]) * 256
    state = jnp.concatenate([lax.dynamic_slice(a, (0, far_half), (32, 256)) for a in states])

    other_grads = swap(logit_grads)
    def pick(far, after):
        h, after = hold((hidden_first, after))
        args = [h] * 8
        block = shape(256, 2048, dtype=BF16)
        return call(pick_kernel, block, place, args, columns(far, 1, True)), after

    def grad(far, taken):
        return call(
            grad_kernel,
            [shape(2080, T, dtype=I16)] * 2,
            place,
            (turned, *[hidden_first] * 8, taken),
            [None] + columns(far, 1) + [None],
        )

    block, _ = pick(ORDER[0], place)
    block, other_grads = hold((block, other_grads))
    taken = swap(block)
    half = pl.BlockSpec((256, 256), lambda step, p: (0, p[2]))
    turned = call(
        turn_kernel,
        shape(256, 512, dtype=BF16),
        place,
        (logit_grads, other_grads),
        [half, half],
    )
    block, turned = pick(ORDER[1], turned)
    following = swap(block)
    two = grad(2, taken)
    block, two = pick(3, two)
    taken, following = following, swap(block)
    turned, block = hold((turned, block))
    relayed = send(two[0], 1, True), send(two[1], 3, True)
    ahead = grad(1, taken)
    block, ahead = pick(0, ahead)
    taken, following = following, swap(block)
    turned, block = hold((turned, block))
    from_behind = [None, send(ahead[1], 1, True)]
    back = grad(3, taken)
    from_ahead = [send(back[0], 3, True), None]
    half_message = shape(2080, T, dtype=I16)
    from_behind[0] = send(call(sum_kernel, half_message, place, (ahead[0], relayed[0])), 1, True)
    from_ahead[1] = send(call(sum_kernel, half_message, place, (back[1], relayed[1])), 3, True)
    own = grad(0, following)
    sums = [own, from_behind, from_ahead]
    sums, state = hold((sums, state))
    state = swap(state)

    blocks = [None] * 4
    for far in ORDER + (0,):
        spec = pl.BlockSpec((1040, T), lambda s, p, far=far: (far % 2, 0))
        blocks[far] = call(
            sum_kernel,
            shape(1040, T, dtype=I16),
            place,
            [taken[far // 2] for taken in sums],
            [spec] * 3,
        )
        if far:
            blocks[far] = send(blocks[far], far, False)
    blocks, second, labels = hold((blocks, hidden_second, labels))
    other_second, other_labels = swap(second), swap(labels)
    chunks = call(
        lambda _, *refs: second_sum_kernel(*refs), shape(1152, T, dtype=I16), place, blocks
    )
    chunks = lax.all_to_all(chunks, ("zl", "zh"), 0, 0, tiled=True)
    kept, sent, copies = call(
        owner_kernel,
        [shape(96, 256)] * 2 + [shape(1024, T, dtype=BF16)],
        place,
        (chunks, *states, state),
    )

    copies = lax.all_to_all(copies, ("zl", "zh"), 0, 0, tiled=True)
    pieces = [copies] + [None] * 3
    for far in ORDER:
        pieces[far] = send(copies, far, False)
    picked = [
        call(pick_kernel, shape(256, 2048, dtype=BF16), place, [h] * 8, columns(2, -1))
        for h in (hidden_second, other_second)
    ]
    pieces, picked, other_labels = hold((pieces, picked, other_labels))
    own = jnp.concatenate(pieces[:2]), jnp.concatenate(pieces[2:])
    behind, ahead = [None, None], [None, None]
    behind[0], ahead[1] = send(own[0], 1, True), send(own[1], 3, True)
    behind[1], ahead[0] = send(own[1], 1, True), send(own[0], 3, True)
    tokens = [hidden_second] * 8 + [other_second] * 8
    specs = [[None] * 2 + columns(far, -1) * 2 for far in range(4)]
    total = call(first_head_kernel, shape(512, 256), place, (*own, *tokens), specs[0])
    behind[0], ahead[1], total = hold((behind[0], ahead[1], total))
    two = send(behind[0], 1, True), send(ahead[1], 3, True)
    behind, sent = hold((behind, sent))
    sent = swap(sent)
    for far, piece in ((1, behind), (3, ahead)):
        total = call(
            next_head_kernel,
            shape(512, 256),
            place,
            (*piece, *tokens, total),
            specs[far] + [None],
        )
    two, total = hold((two, total))
    stats, other_stats = call(
        last_head_kernel,
        [shape(256, T)] * 2,
        place,
        (*two, *picked, total, labels, other_labels),
    )
    updated = call(join_kernel, [shape(32, 512)] * 3, place, (kept, sent))
    other_stats, updated = hold((swap(other_stats), updated))
    loss = call(loss_kernel, shape(1, 256), place, (stats, other_stats))
    return *updated, loss.reshape(256)


def solution(mesh):
    fine = Mesh(mesh.devices.reshape(SIZES), AXES)
    two, one = P(AXES, None), P(AXES)
    return jax.shard_map(
        on_device,
        mesh=fine,
        in_specs=(two, two, two, one, two, two, two),
        out_specs=(two, two, two, one),
        check_vma=False,
    )
```

time: 360 us -> 137 us (0.38)
  waiting for transfers between devices: 284 us -> 34.8 us
  starting transfers between devices: 0.12 us -> 42.9 us
  Pallas kernels: 0 us -> 39.3 us
  matrix products: 15 us -> 0 us
  local copies, waits for them, and re-layouts: 20.3 us -> 6.21 us
  between operations: 13.8 us -> 0.92 us
  blocking collectives: 24.5 us -> 11.9 us
    reduce_scatter x2 -> x0, waiting for transfers between devices: 204 us -> none  [the longest x1 169 us: on_device(): lax.psum_scatter(jnp.einsum('tc,tv->cv', columns, logit_grads, preferred_...]
    all_gather x1 -> x0, waiting for transfers between devices: 79.4 us -> none  [on_device(): lax.all_gather(group_rows, 'dev', axis=0, tiled=True)]
    pallas_call x0 -> x25, Pallas kernels: none -> 39.3 us  [call(): pl.pallas_call(kernel, out_shape=outs, grid_spec=pltpu.PrefetchScalarGrid...]
    ppermute x0 -> x28, starting transfers between devices: none -> 34.8 us  [the longest x18 21.9 us: send(): return lax.ppermute(a, AXES, pairs)]
    ppermute x0 -> x28, waiting for transfers between devices: none -> 24.8 us  [the longest x18 22.2 us: send(): return lax.ppermute(a, AXES, pairs)]
    all_gather x1 -> x0, blocking collectives: 24.5 us -> none  [on_device(): group_rows = lax.all_gather(copy_rows, 'grp', axis=0, tiled=True)]
    dot_general x2 -> x0, matrix products: 15 us -> none  [the longest x1 8.08 us: on_device(): jnp.einsum('tc,tv->cv', columns, logit_grads, preferred_element_type=jnp....]
    all_to_all x0 -> x1, blocking collectives: none -> 11.9 us  [on_device(): copies = lax.all_to_all(copies, ('zl', 'zh'), 0, 0, tiled=True)]
  transfers between devices with their start and end apart: 3 -> 29, of which waited for: 3 -> 16; matrix products, arithmetic and copies ran while one was open for 3% -> 1% of each run, Pallas kernels for 0% -> 25%
where the time goes in v2:
time: 137 us
  starting transfers between devices  42.9 us (31%)
  Pallas kernels  39.3 us (29%)
  waiting for transfers between devices  34.8 us (25%)
  blocking collectives  11.9 us (9%)
  local copies, waits for them, and re-layouts  6.21 us (5%)
    pallas_call x25, Pallas kernels, call(): pl.pallas_call(kernel, out_shape=outs, grid_spec=pltpu.PrefetchScalarGrid...  39.3 us
    ppermute x18, waiting for transfers between devices, send(): return lax.ppermute(a, AXES, pairs)  22.2 us
    ppermute x18, starting transfers between devices, send(): return lax.ppermute(a, AXES, pairs)  21.9 us
    ppermute x10, starting transfers between devices, swap(): return lax.ppermute(a, 'c', [(0, 1), (1, 0)])  13 us
    all_to_all x1, blocking collectives, on_device(): copies = lax.all_to_all(copies, ('zl', 'zh'), 0, 0, tiled=True)  11.9 us
    all_to_all x1, waiting for transfers between devices, on_device(): chunks = lax.all_to_all(chunks, ('zl', 'zh'), 0, 0, tiled=True)  10.1 us
    all_to_all x1, starting transfers between devices, on_device(): chunks = lax.all_to_all(chunks, ('zl', 'zh'), 0, 0, tiled=True)  8.02 us
    unnamed x20, local copies, waits for them, and re-layouts  5.23 us
  transfers between devices with their start and end apart: 29, of which 16 were waited for; matrix products, arithmetic and copies ran while one was open for 1% of the time, Pallas kernels for 25%

profile of v2, /device:TPU:33, one launch (start us, length us, event | category | flops | bytes accessed | tf_op | source)
XLA Modules:
  0.0 136.8 jit_solution(10105268933899833528)
XLA Ops:
  1.5 2.2 %copy-done = bf16[256,8192]{1,0:T(8,128)(2,1)S(1)} copy-done((bf16[256,8192]{1,0:T(8,128)(2,1)S(1)}, bf16[256,8192]{1,0:T(8,128)(2,1)}, u32[]{:S(2)}) %copy-start) | copy-done | bytes 4194328
  7.1 1.7 %shard_map.104 = (s16[2080,128]{1,0:T(8,128)(2,1)S(1)}, s16[2080,128]{1,0:T(8,128)(2,1)S(1)}) custom-call(s32[3]{0:T(128)S(1)} %pad_add_fusion.place._, bf16[256,512]{1,0:T(8,128)(2,1)S(1)} %shard_map.103.lt, bf16[256,8192]{1,0:T(8,128)(2,1)S(1)} %copy-done.1, bf16[256,8192]{1,0:T(8,128)(2,1)S(1)} %copy-done.1, bf16[256,8192]{1,0:T(8,128)(2,1)S(1)} %copy-done.1, ...), custom_call_target="tpu_custom_call" | custom-call | flops 1 | bytes 1 | tf_op jit(solution)/shard_map/pallas_call | solution.py:212
  9.7 1.3 collective-permute-start.4
  11.0 1.5 %collective-permute-start.9 = (s16[2080,128]{1,0:T(8,128)(2,1)S(1)}, s16[2080,128]{1,0:T(8,128)(2,1)S(1)}, u32[]{:S(2)}, u32[]{:S(2)}) collective-permute-start(s16[2080,128]{1,0:T(8,128)(2,1)S(1)} %get-tuple-element.86), channel_id=1, source_target_pairs={{0,192},{1,25},{2,194},{3,27},{4,196},{5,29},{6,198},{7,31},{8,200... | collective-permute-start | bytes 1597448 | tf_op jit(solution)/shard_map/ppermute | solution.py:251
  12.5 2.5 %shard_map.107 = (s16[2080,128]{1,0:T(8,128)(2,1)S(1)}, s16[2080,128]{1,0:T(8,128)(2,1)}) custom-call(s32[3]{0:T(128)S(1)} %pad_add_fusion.place._, bf16[256,512]{1,0:T(8,128)(2,1)S(1)} %shard_map.103.lt, bf16[256,8192]{1,0:T(8,128)(2,1)S(1)} %copy-done.1, bf16[256,8192]{1,0:T(8,128)(2,1)S(1)} %copy-done.1, bf16[256,8192]{1,0:T(8,128)(2,1)S(1)} %copy-done.1, ...), custom_call_target="tpu_custom_call" | custom-call | flops 1 | bytes 1 | tf_op jit(solution)/shard_map/pallas_call | solution.py:212
  15.0 1.7 %shard_map.108 = bf16[256,2048]{1,0:T(8,128)(2,1)} custom-call(s32[3]{0:T(128)S(1)} %pad_add_fusion.place._, bf16[256,8192]{1,0:T(8,128)(2,1)S(1)} %copy-done.1, bf16[256,8192]{1,0:T(8,128)(2,1)S(1)} %copy-done.1, bf16[256,8192]{1,0:T(8,128)(2,1)S(1)} %copy-done.1, bf16[256,8192]{1,0:T(8,128)(2,1)S(1)} %copy-done.1, bf16[256,8192]{1,0:T(8,128)(2,1)S(1)} %copy-done.1, ...), custom_call_target="tpu_custom_call" | custom-call | flops 1 | bytes 1 | tf_op jit(solution)/shard_map/pallas_call | solution.py:212
  17.6 1.3 collective-permute-start.6
  19.4 1.9 %shard_map.110 = s16[2080,128]{1,0:T(8,128)(2,1)} custom-call(s32[3]{0:T(128)S(1)} %pad_add_fusion.place._, s16[2080,128]{1,0:T(8,128)(2,1)S(1)} %get-tuple-element.81.refs_0_, s16[2080,128]{1,0:T(8,128)(2,1)S(1)} %collective-permute-done.4.refs_1_), custom_call_target="tpu_custom_call" | custom-call | flops 1 | bytes 1 | tf_op jit(solution)/shard_map/pallas_call | solution.py:212
  22.0 2.6 %shard_map.111 = (s16[2080,128]{1,0:T(8,128)(2,1)}, s16[2080,128]{1,0:T(8,128)(2,1)S(1)}) custom-call(s32[3]{0:T(128)S(1)} %pad_add_fusion.place._, bf16[256,512]{1,0:T(8,128)(2,1)S(1)} %shard_map.103.lt, bf16[256,8192]{1,0:T(8,128)(2,1)S(1)} %copy-done.1, bf16[256,8192]{1,0:T(8,128)(2,1)S(1)} %copy-done.1, bf16[256,8192]{1,0:T(8,128)(2,1)S(1)} %copy-done.1, ...), custom_call_target="tpu_custom_call" | custom-call | flops 1 | bytes 1 | tf_op jit(solution)/shard_map/pallas_call | solution.py:212
  24.7 1.9 %shard_map.112 = s16[2080,128]{1,0:T(8,128)(2,1)} custom-call(s32[3]{0:T(128)S(1)} %pad_add_fusion.place._, s16[2080,128]{1,0:T(8,128)(2,1)S(1)} %get-tuple-element.85.refs_0_, s16[2080,128]{1,0:T(8,128)(2,1)S(1)} %collective-permute-done.9.refs_1_), custom_call_target="tpu_custom_call" | custom-call | flops 1 | bytes 1 | tf_op jit(solution)/shard_map/pallas_call | solution.py:212
  26.6 2.0 %collective-permute-start.10 = (s16[2080,128]{1,0:T(8,128)(2,1)}, s16[2080,128]{1,0:T(8,128)(2,1)S(1)}, u32[]{:S(2)}, u32[]{:S(2)}) collective-permute-start(s16[2080,128]{1,0:T(8,128)(2,1)} %shard_map.112), channel_id=1, source_target_pairs={{0,192},{1,25},{2,194},{3,27},{4,196},{5,29},{6,198},{7,31},{8,200... | collective-permute-start | bytes 1597448 | tf_op jit(solution)/shard_map/ppermute | solution.py:251
  30.2 2.2 %copy-done.2 = bf16[256,8192]{1,0:T(8,128)(2,1)S(1)} copy-done((bf16[256,8192]{1,0:T(8,128)(2,1)S(1)}, bf16[256,8192]{1,0:T(8,128)(2,1)}, u32[]{:S(2)}) %copy-start.2) | copy-done | bytes 4194328
  32.4 1.7 %shard_map.109 = (s16[2080,128]{1,0:T(8,128)(2,1)S(1)}, s16[2080,128]{1,0:T(8,128)(2,1)S(1)}) custom-call(s32[3]{0:T(128)S(1)} %pad_add_fusion.place._, bf16[256,512]{1,0:T(8,128)(2,1)S(1)} %shard_map.103.lt, bf16[256,8192]{1,0:T(8,128)(2,1)S(1)} %copy-done.2, bf16[256,8192]{1,0:T(8,128)(2,1)S(1)} %copy-done.2, bf16[256,8192]{1,0:T(8,128)(2,1)S(1)} %copy-done.2, ...), custom_call_target="tpu_custom_call" | custom-call | flops 1 | bytes 1 | tf_op jit(solution)/shard_map/pallas_call | solution.py:212
  34.1 1.1 collective-permute-done.10.refs_2_
  35.2 5.7 %collective-permute-done.8.refs_2_ = s16[2080,128]{1,0:T(8,128)(2,1)S(1)} collective-permute-done((s16[2080,128]{1,0:T(8,128)(2,1)}, s16[2080,128]{1,0:T(8,128)(2,1)S(1)}, u32[]{:S(2)}, u32[]{:S(2)}) %collective-permute-start.8) | collective-permute-done | bytes 532512 | tf_op jit(solution)/shard_map/ppermute | solution.py:251
  40.9 0.9 shard_map.116
  41.8 0.9 shard_map.115
  42.7 2.4 %collective-permute-start.12 = (s16[1040,128]{1,0:T(8,128)(2,1)S(1)}, s16[1040,128]{1,0:T(8,128)(2,1)S(1)}, u32[]{:S(2)}, u32[]{:S(2)}) collective-permute-start(s16[1040,128]{1,0:T(8,128)(2,1)S(1)} %shard_map.115), channel_id=1, source_target_pairs={{0,16},{1,129},{2,18},{3,131},{4,20},{5,133},{6,22},{7,135},{8,24}... | collective-permute-start | bytes 798728 | tf_op jit(solution)/shard_map/ppermute | solution.py:251
  47.5 0.9 shard_map.113.refs_0_
  48.4 1.4 %collective-permute-done.12.refs_2_ = s16[1040,128]{1,0:T(8,128)(2,1)S(1)} collective-permute-done((s16[1040,128]{1,0:T(8,128)(2,1)S(1)}, s16[1040,128]{1,0:T(8,128)(2,1)S(1)}, u32[]{:S(2)}, u32[]{:S(2)}) %collective-permute-start.12) | collective-permute-done | bytes 266272 | tf_op jit(solution)/shard_map/ppermute | solution.py:251
  49.9 2.6 %collective-permute-done.13.refs_3_ = s16[1040,128]{1,0:T(8,128)(2,1)S(1)} collective-permute-done((s16[1040,128]{1,0:T(8,128)(2,1)S(1)}, s16[1040,128]{1,0:T(8,128)(2,1)S(1)}, u32[]{:S(2)}, u32[]{:S(2)}) %collective-permute-start.13) | collective-permute-done | bytes 266272 | tf_op jit(solution)/shard_map/ppermute | solution.py:251
  52.5 0.9 collective-permute-done.11.refs_1_
  53.4 4.4 %collective-permute-start.18 = (bf16[256,8192]{1,0:T(8,128)(2,1)}, bf16[256,8192]{1,0:T(8,128)(2,1)}, u32[]{:S(2)}, u32[]{:S(2)}) collective-permute-start(bf16[256,8192]{1,0:T(8,128)(2,1)} %refs_7_.19), channel_id=1, source_target_pairs={{0,1},{1,0},{2,3},{3,2},{4,5},{5,4},{6,7},{7,6},{8,9},{9,8},{10,11... | collective-permute-start | bytes 12582920 | tf_op jit(solution)/shard_map/ppermute | solution.py:242
  57.8 1.8 %shard_map.117 = s16[1152,128]{1,0:T(8,128)(2,1)} custom-call(s32[3]{0:T(128)S(1)} %pad_add_fusion.place._, s16[1040,128]{1,0:T(8,128)(2,1)S(1)} %shard_map.113.refs_0_, s16[1040,128]{1,0:T(8,128)(2,1)S(1)} %collective-permute-done.11.refs_1_, s16[1040,128]{1,0:T(8,128)(2,1)S(1)} %collective-permute-done.12.refs_2_, ...), custom_call_target="tpu_custom_call" | custom-call | flops 1 | bytes 1 | tf_op jit(solution)/shard_map/pallas_call | solution.py:212
  59.6 8.0 %all-to-all-start = ((s16[8,144,128]{2,1,0:T(8,128)(2,1)}), s16[8,144,128]{2,1,0:T(8,128)(2,1)S(1)}, u32[]{:S(2)}, u32[]{:S(2)}) async-start(s16[8,144,128]{2,1,0:T(8,128)(2,1)} %bitcast.4), calls=%async_computation | async-start | bytes 589824 | tf_op jit(solution)/shard_map/all_to_all | solution.py:330
  68.2 0.9 collective-permute-done.14.given
  69.1 10.1 %all-to-all-done = s16[8,144,128]{2,1,0:T(8,128)(2,1)S(1)} async-done(((s16[8,144,128]{2,1,0:T(8,128)(2,1)}), s16[8,144,128]{2,1,0:T(8,128)(2,1)S(1)}, u32[]{:S(2)}, u32[]{:S(2)}) %all-to-all-start) | async-done | bytes 294944 | tf_op jit(solution)/shard_map/all_to_all | solution.py:330
  79.9 11.9 %all_to_all.23 = bf16[8,128,128]{2,1,0:T(8,128)(2,1)S(1)} all-to-all(bf16[8,128,128]{2,1,0:T(8,128)(2,1)S(1)} %bitcast.10), channel_id=1, replica_groups=mesh['x'=4,'zl'=2,'y'=4,'zh'=4,'c'=2] {'zl','zh'}, dimensions={0} | all-to-all | bytes 524288 | tf_op jit(solution)/shard_map/all_to_all | solution.py:338
  91.9 3.3 %collective-permute-start.17 = (bf16[1024,128]{1,0:T(8,128)(2,1)S(1)}, bf16[1024,128]{1,0:T(8,128)(2,1)S(1)}, u32[]{:S(2)}, u32[]{:S(2)}) collective-permute-start(bf16[1024,128]{1,0:T(8,128)(2,1)S(1)} %bitcast.11), channel_id=1, source_target_pairs={{0,24},{1,193},{2,26},{3,195},{4,28},{5,197},{6,30},{7,199},{8,0},... | collective-permute-start | bytes 786440 | tf_op jit(solution)/shard_map/ppermute | solution.py:251
  95.9 0.9 collective-permute-start.19
  96.9 2.0 %shard_map.119.refs_0_ = bf16[256,2048]{1,0:T(8,128)(2,1)S(1)} custom-call(s32[3]{0:T(128)S(1)} %pad_add_fusion.place._, bf16[256,8192]{1,0:T(8,128)(2,1)} %refs_7_.19, bf16[256,8192]{1,0:T(8,128)(2,1)} %refs_7_.19, bf16[256,8192]{1,0:T(8,128)(2,1)} %refs_7_.19, bf16[256,8192]{1,0:T(8,128)(2,1)} %refs_7_.19, bf16[256,8192]{1,0:T(8,128)(2,1)} %refs_7_.19, ...), custom_call_target="tpu_custom_call" | custom-call | flops 1 | bytes 1 | tf_op jit(solution)/shard_map/pallas_call | solution.py:212
  98.8 2.0 %shard_map.120.refs_1_ = bf16[256,2048]{1,0:T(8,128)(2,1)S(1)} custom-call(s32[3]{0:T(128)S(1)} %pad_add_fusion.place._, bf16[256,8192]{1,0:T(8,128)(2,1)} %collective-permute-done.18.refs_0_.refs_1_.refs_2_.refs_3_.refs_4_.refs_5_.refs_6_.refs_7_.refs_8_.refs_9_.refs_10_.refs_11_.refs_12_.refs_13_.refs_14_.refs_15_, ...), custom_call_target="tpu_custom_call" | custom-call | flops 1 | bytes 1 | tf_op jit(solution)/shard_map/pallas_call | solution.py:212
  101.3 0.9 collective-permute-done.16
  102.2 2.5 %collective-permute-done.15 = bf16[1024,128]{1,0:T(8,128)(2,1)S(1)} collective-permute-done((bf16[1024,128]{1,0:T(8,128)(2,1)S(1)}, bf16[1024,128]{1,0:T(8,128)(2,1)S(1)}, u32[]{:S(2)}, u32[]{:S(2)}) %collective-permute-start.15) | collective-permute-done | bytes 262176 | tf_op jit(solution)/shard_map/ppermute | solution.py:251
  105.5 1.0 collective-permute-start.20
  106.8 2.4 %collective-permute-start.24 = (bf16[2048,128]{1,0:T(8,128)(2,1)S(1)}, bf16[2048,128]{1,0:T(8,128)(2,1)S(1)}, u32[]{:S(2)}, u32[]{:S(2)}) collective-permute-start(bf16[2048,128]{1,0:T(8,128)(2,1)S(1)} %constant_dynamic-update-slice_fusion.w0), channel_id=1, source_target_pairs={{0,192},{1,25},{2,194},{3,27},{4,196},{5,29},{6,198},{7,31},{8,200... | collective-permute-start | bytes 1572872 | tf_op jit(solution)/shard_map/ppermute | solution.py:251
  109.1 2.9 %shard_map.121.refs_16_ = f32[512,256]{1,0:T(8,128)S(1)} custom-call(s32[3]{0:T(128)S(1)} %pad_add_fusion.place._, bf16[2048,128]{1,0:T(8,128)(2,1)S(1)} %constant_dynamic-update-slice_fusion.w0, bf16[2048,128]{1,0:T(8,128)(2,1)S(1)} %constant_dynamic-update-slice_fusion.2.w1, bf16[256,8192]{1,0:T(8,128)(2,1)} %refs_7_.19, bf16[256,8192]{1,0:T(8,128)(2,1)} %refs_7_.19, ...), custom_call_target="tpu_custom_call" | custom-call | flops 1 | bytes 1 | tf_op jit(solution)/shard_map/pallas_call | solution.py:212
  112.0 1.2 collective-permute-done.21.w1
  113.2 1.9 %collective-permute-done.20.w0 = bf16[2048,128]{1,0:T(8,128)(2,1)S(1)} collective-permute-done((bf16[2048,128]{1,0:T(8,128)(2,1)S(1)}, bf16[2048,128]{1,0:T(8,128)(2,1)S(1)}, u32[]{:S(2)}, u32[]{:S(2)}) %collective-permute-start.20) | collective-permute-done | bytes 524320 | tf_op jit(solution)/shard_map/ppermute | solution.py:251
  115.1 2.7 %collective-permute-start.23 = (bf16[2048,128]{1,0:T(8,128)(2,1)S(1)}, bf16[2048,128]{1,0:T(8,128)(2,1)S(1)}, u32[]{:S(2)}, u32[]{:S(2)}) collective-permute-start(bf16[2048,128]{1,0:T(8,128)(2,1)S(1)} %collective-permute-done.21.w1), channel_id=1, source_target_pairs={{0,192},{1,25},{2,194},{3,27},{4,196},{5,29},{6,198},{7,31},{8,200... | collective-permute-start | bytes 1572872 | tf_op jit(solution)/shard_map/ppermute | solution.py:251
  117.8 2.9 %collective-permute-done.25.w1 = bf16[2048,128]{1,0:T(8,128)(2,1)S(1)} collective-permute-done((bf16[2048,128]{1,0:T(8,128)(2,1)S(1)}, bf16[2048,128]{1,0:T(8,128)(2,1)S(1)}, u32[]{:S(2)}, u32[]{:S(2)}) %collective-permute-start.25) | collective-permute-done | bytes 524320 | tf_op jit(solution)/shard_map/ppermute | solution.py:251
  120.7 2.9 %shard_map.122.refs_16_ = f32[512,256]{1,0:T(8,128)S(1)} custom-call(s32[3]{0:T(128)S(1)} %pad_add_fusion.place._, bf16[2048,128]{1,0:T(8,128)(2,1)S(1)} %collective-permute-done.20.w0, bf16[2048,128]{1,0:T(8,128)(2,1)S(1)} %collective-permute-done.25.w1, bf16[256,8192]{1,0:T(8,128)(2,1)} %refs_7_.19, bf16[256,8192]{1,0:T(8,128)(2,1)} %refs_7_.19, ...), custom_call_target="tpu_custom_call" | custom-call | flops 1 | bytes 1 | tf_op jit(solution)/shard_map/pallas_call | solution.py:212
  123.7 2.9 %shard_map.123.refs_2_ = f32[512,256]{1,0:T(8,128)S(1)} custom-call(s32[3]{0:T(128)S(1)} %pad_add_fusion.place._, bf16[2048,128]{1,0:T(8,128)(2,1)S(1)} %collective-permute-done.24.w0, bf16[2048,128]{1,0:T(8,128)(2,1)S(1)} %collective-permute-done.21.w1, bf16[256,8192]{1,0:T(8,128)(2,1)} %refs_7_.19, bf16[256,8192]{1,0:T(8,128)(2,1)} %refs_7_.19, ...), custom_call_target="tpu_custom_call" | custom-call | flops 1 | bytes 1 | tf_op jit(solution)/shard_map/pallas_call | solution.py:212
  126.6 1.5 %shard_map.124 = (f32[256,128]{1,0:T(8,128)S(1)}, f32[256,128]{1,0:T(8,128)S(1)}) custom-call(s32[3]{0:T(128)S(1)} %pad_add_fusion.place._, bf16[2048,128]{1,0:T(8,128)(2,1)S(1)} %collective-permute-done.22.w0, bf16[2048,128]{1,0:T(8,128)(2,1)S(1)} %collective-permute-done.23.w1, bf16[256,2048]{1,0:T(8,128)(2,1)S(1)} %shard_map.119.refs_0_, ...), custom_call_target="tpu_custom_call" | custom-call | flops 1 | bytes 1 | tf_op jit(solution)/shard_map/pallas_call | solution.py:212
  128.1 5.0 %collective-permute-start.26 = (f32[256,128]{1,0:T(8,128)S(1)}, f32[256,128]{1,0:T(8,128)S(1)}, u32[]{:S(2)}, u32[]{:S(2)}) collective-permute-start(f32[256,128]{1,0:T(8,128)S(1)} %get-tuple-element.117), channel_id=1, source_target_pairs={{0,1},{1,0},{2,3},{3,2},{4,5},{5,4},{6,7},{7,6},{8,9},{9,8},{10,11... | collective-permute-start | bytes 393224 | tf_op jit(solution)/shard_map/ppermute | solution.py:242
  133.2 1.2 collective-permute-done.27.given
  134.4 1.2 shard_map.125
  135.6 1.2 shard_map.126
  (63 shorter events, 15.1 us)
Async XLA Ops:
  0.6 3.7 %collective-permute-start = (bf16[256,512]{1,0:T(8,128)(2,1)}, bf16[256,512]{1,0:T(8,128)(2,1)S(1)}, u32[]{:S(2)}, u32[]{:S(2)}) collective-permute-start(bf16[256,512]{1,0:T(8,128)(2,1)} %l.1), channel_id=1, source_target_pairs={{0,1},{1,0},{2,3},{3,2},{4,5},{5,4},{6,7},{7,6},{8,9},{9,8},{10,11... | collective-permute-start | bytes 786440 | tf_op jit(solution)/shard_map/ppermute | solution.py:242
  1.5 2.2 %copy-start = (bf16[256,8192]{1,0:T(8,128)(2,1)S(1)}, bf16[256,8192]{1,0:T(8,128)(2,1)}, u32[]{:S(2)}) copy-start(bf16[256,8192]{1,0:T(8,128)(2,1)} %refs_7_.15) | copy-start | bytes 12582916
  3.7 0.9 copy-start.3
  3.7 2.3 %copy-start.1 = (bf16[256,8192]{1,0:T(8,128)(2,1)S(1)}, bf16[256,8192]{1,0:T(8,128)(2,1)}, u32[]{:S(2)}) copy-start(bf16[256,8192]{1,0:T(8,128)(2,1)} %refs_7_.15) | copy-start | bytes 12582916
  4.4 2.7 %collective-permute-start.1 = (bf16[256,2048]{1,0:T(8,128)(2,1)S(1)}, bf16[256,2048]{1,0:T(8,128)(2,1)S(1)}, u32[]{:S(2)}, u32[]{:S(2)}) collective-permute-start(bf16[256,2048]{1,0:T(8,128)(2,1)S(1)} %shard_map.102), channel_id=1, source_target_pairs={{0,1},{1,0},{2,3},{3,2},{4,5},{5,4},{6,7},{7,6},{8,9},{9,8},{10,11... | collective-permute-start | bytes 3145736 | tf_op jit(solution)/shard_map/ppermute | solution.py:242
  6.6 5.9 %collective-permute-start.2 = (bf16[256,2048]{1,0:T(8,128)(2,1)S(1)}, bf16[256,2048]{1,0:T(8,128)(2,1)S(1)}, u32[]{:S(2)}, u32[]{:S(2)}) collective-permute-start(bf16[256,2048]{1,0:T(8,128)(2,1)S(1)} %shard_map.106), channel_id=1, source_target_pairs={{0,1},{1,0},{2,3},{3,2},{4,5},{5,4},{6,7},{7,6},{8,9},{9,8},{10,11... | collective-permute-start | bytes 3145736 | tf_op jit(solution)/shard_map/ppermute | solution.py:242
  9.5 12.5 %collective-permute-start.7 = (bf16[256,2048]{1,0:T(8,128)(2,1)S(1)}, bf16[256,2048]{1,0:T(8,128)(2,1)S(1)}, u32[]{:S(2)}, u32[]{:S(2)}) collective-permute-start(bf16[256,2048]{1,0:T(8,128)(2,1)S(1)} %shard_map.105), channel_id=1, source_target_pairs={{0,1},{1,0},{2,3},{3,2},{4,5},{5,4},{6,7},{7,6},{8,9},{9,8},{10,11... | collective-permute-start | bytes 3145736 | tf_op jit(solution)/shard_map/ppermute | solution.py:242
  9.7 9.7 %collective-permute-start.4 = (s16[2080,128]{1,0:T(8,128)(2,1)S(1)}, s16[2080,128]{1,0:T(8,128)(2,1)S(1)}, u32[]{:S(2)}, u32[]{:S(2)}) collective-permute-start(s16[2080,128]{1,0:T(8,128)(2,1)S(1)} %get-tuple-element.82), channel_id=1, source_target_pairs={{0,64},{1,9},{2,66},{3,11},{4,68},{5,13},{6,70},{7,15},{8,72},{9,1... | collective-permute-start | bytes 1597448 | tf_op jit(solution)/shard_map/ppermute | solution.py:251
  11.0 13.6 %collective-permute-start.9 = (s16[2080,128]{1,0:T(8,128)(2,1)S(1)}, s16[2080,128]{1,0:T(8,128)(2,1)S(1)}, u32[]{:S(2)}, u32[]{:S(2)}) collective-permute-start(s16[2080,128]{1,0:T(8,128)(2,1)S(1)} %get-tuple-element.86), channel_id=1, source_target_pairs={{0,192},{1,25},{2,194},{3,27},{4,196},{5,29},{6,198},{7,31},{8,200... | collective-permute-start | bytes 1597448 | tf_op jit(solution)/shard_map/ppermute | solution.py:251
  16.8 13.5 %collective-permute-start.3 = (bf16[256,2048]{1,0:T(8,128)(2,1)}, bf16[256,2048]{1,0:T(8,128)(2,1)S(1)}, u32[]{:S(2)}, u32[]{:S(2)}) collective-permute-start(bf16[256,2048]{1,0:T(8,128)(2,1)} %shard_map.108), channel_id=1, source_target_pairs={{0,1},{1,0},{2,3},{3,2},{4,5},{5,4},{6,7},{7,6},{8,9},{9,8},{10,11... | collective-permute-start | bytes 3145736 | tf_op jit(solution)/shard_map/ppermute | solution.py:242
  17.6 16.5 %collective-permute-start.6 = (s16[2080,128]{1,0:T(8,128)(2,1)}, s16[2080,128]{1,0:T(8,128)(2,1)S(1)}, u32[]{:S(2)}, u32[]{:S(2)}) collective-permute-start(s16[2080,128]{1,0:T(8,128)(2,1)} %get-tuple-element.83), channel_id=1, source_target_pairs={{0,64},{1,9},{2,66},{3,11},{4,68},{5,13},{6,70},{7,15},{8,72},{9,1... | collective-permute-start | bytes 1597448 | tf_op jit(solution)/shard_map/ppermute | solution.py:251
  21.3 7.5 %copy-start.4 = (f32[32,512]{1,0:T(8,128)S(1)}, f32[32,512]{1,0:T(8,128)}, u32[]{:S(2)}) copy-start(f32[32,512]{1,0:T(8,128)} %master.1) | copy-start | bytes 196612
  21.3 12.7 %collective-permute-start.5 = (s16[2080,128]{1,0:T(8,128)(2,1)}, s16[2080,128]{1,0:T(8,128)(2,1)S(1)}, u32[]{:S(2)}, u32[]{:S(2)}) collective-permute-start(s16[2080,128]{1,0:T(8,128)(2,1)} %shard_map.110), channel_id=1, source_target_pairs={{0,64},{1,9},{2,66},{3,11},{4,68},{5,13},{6,70},{7,15},{8,72},{9,1... | collective-permute-start | bytes 1597448 | tf_op jit(solution)/shard_map/ppermute | solution.py:251
  26.6 8.6 %collective-permute-start.10 = (s16[2080,128]{1,0:T(8,128)(2,1)}, s16[2080,128]{1,0:T(8,128)(2,1)S(1)}, u32[]{:S(2)}, u32[]{:S(2)}) collective-permute-start(s16[2080,128]{1,0:T(8,128)(2,1)} %shard_map.112), channel_id=1, source_target_pairs={{0,192},{1,25},{2,194},{3,27},{4,196},{5,29},{6,198},{7,31},{8,200... | collective-permute-start | bytes 1597448 | tf_op jit(solution)/shard_map/ppermute | solution.py:251
  28.5 12.4 %collective-permute-start.8 = (s16[2080,128]{1,0:T(8,128)(2,1)}, s16[2080,128]{1,0:T(8,128)(2,1)S(1)}, u32[]{:S(2)}, u32[]{:S(2)}) collective-permute-start(s16[2080,128]{1,0:T(8,128)(2,1)} %get-tuple-element.84), channel_id=1, source_target_pairs={{0,192},{1,25},{2,194},{3,27},{4,196},{5,29},{6,198},{7,31},{8,200... | collective-permute-start | bytes 1597448 | tf_op jit(solution)/shard_map/ppermute | solution.py:251
  30.2 2.2 %copy-start.2 = (bf16[256,8192]{1,0:T(8,128)(2,1)S(1)}, bf16[256,8192]{1,0:T(8,128)(2,1)}, u32[]{:S(2)}) copy-start(bf16[256,8192]{1,0:T(8,128)(2,1)} %refs_7_.15) | copy-start | bytes 12582916
  41.8 25.8 %copy-start.7 = (f32[96,256]{1,0:T(8,128)S(1)}, f32[96,256]{1,0:T(8,128)}, u32[]{:S(2)}) copy-start(f32[96,256]{1,0:T(8,128)} %pad_maximum_fusion) | copy-start | bytes 294916
  41.8 37.4 %copy-start.5 = (f32[32,512]{1,0:T(8,128)S(1)}, f32[32,512]{1,0:T(8,128)}, u32[]{:S(2)}) copy-start(f32[32,512]{1,0:T(8,128)} %one.1) | copy-start | bytes 196612
  41.8 37.4 %copy-start.6 = (f32[32,512]{1,0:T(8,128)S(1)}, f32[32,512]{1,0:T(8,128)}, u32[]{:S(2)}) copy-start(f32[32,512]{1,0:T(8,128)} %two.1) | copy-start | bytes 196612
  41.8 53.9 %copy-start.8 = (s32[256]{0:T(256)S(1)}, s32[256]{0:T(256)}, u32[]{:S(2)}) copy-start(s32[256]{0:T(256)} %param.10) | copy-start | bytes 3076
  42.7 7.2 %collective-permute-start.12 = (s16[1040,128]{1,0:T(8,128)(2,1)S(1)}, s16[1040,128]{1,0:T(8,128)(2,1)S(1)}, u32[]{:S(2)}, u32[]{:S(2)}) collective-permute-start(s16[1040,128]{1,0:T(8,128)(2,1)S(1)} %shard_map.115), channel_id=1, source_target_pairs={{0,16},{1,129},{2,18},{3,131},{4,20},{5,133},{6,22},{7,135},{8,24}... | collective-permute-start | bytes 798728 | tf_op jit(solution)/shard_map/ppermute | solution.py:251
  45.1 7.4 %collective-permute-start.13 = (s16[1040,128]{1,0:T(8,128)(2,1)S(1)}, s16[1040,128]{1,0:T(8,128)(2,1)S(1)}, u32[]{:S(2)}, u32[]{:S(2)}) collective-permute-start(s16[1040,128]{1,0:T(8,128)(2,1)S(1)} %shard_map.116), channel_id=1, source_target_pairs={{0,24},{1,193},{2,26},{3,195},{4,28},{5,197},{6,30},{7,199},{8,0},... | collective-permute-start | bytes 798728 | tf_op jit(solution)/shard_map/ppermute | solution.py:251
  46.9 6.6 %collective-permute-start.11 = (s16[1040,128]{1,0:T(8,128)(2,1)S(1)}, s16[1040,128]{1,0:T(8,128)(2,1)S(1)}, u32[]{:S(2)}, u32[]{:S(2)}) collective-permute-start(s16[1040,128]{1,0:T(8,128)(2,1)S(1)} %shard_map.114), channel_id=1, source_target_pairs={{0,8},{1,65},{2,10},{3,67},{4,12},{5,69},{6,14},{7,71},{8,16},{9,7... | collective-permute-start | bytes 798728 | tf_op jit(solution)/shard_map/ppermute | solution.py:251
  53.4 45.4 %collective-permute-start.18 = (bf16[256,8192]{1,0:T(8,128)(2,1)}, bf16[256,8192]{1,0:T(8,128)(2,1)}, u32[]{:S(2)}, u32[]{:S(2)}) collective-permute-start(bf16[256,8192]{1,0:T(8,128)(2,1)} %refs_7_.19), channel_id=1, source_target_pairs={{0,1},{1,0},{2,3},{3,2},{4,5},{5,4},{6,7},{7,6},{8,9},{9,8},{10,11... | collective-permute-start | bytes 12582920 | tf_op jit(solution)/shard_map/ppermute | solution.py:242
  59.6 19.6 %all-to-all-start = ((s16[8,144,128]{2,1,0:T(8,128)(2,1)}), s16[8,144,128]{2,1,0:T(8,128)(2,1)S(1)}, u32[]{:S(2)}, u32[]{:S(2)}) async-start(s16[8,144,128]{2,1,0:T(8,128)(2,1)} %bitcast.4), calls=%async_computation | async-start | bytes 589824 | tf_op jit(solution)/shard_map/all_to_all | solution.py:330
  67.6 1.5 %collective-permute-start.14 = (f32[96,256]{1,0:T(8,128)S(1)}, f32[96,256]{1,0:T(8,128)S(1)}, u32[]{:S(2)}, u32[]{:S(2)}) collective-permute-start(f32[96,256]{1,0:T(8,128)S(1)} %copy-done.7), channel_id=1, source_target_pairs={{0,1},{1,0},{2,3},{3,2},{4,5},{5,4},{6,7},{7,6},{8,9},{9,8},{10,11... | collective-permute-start | bytes 294920 | tf_op jit(solution)/shard_map/ppermute | solution.py:242
  91.9 9.4 %collective-permute-start.17 = (bf16[1024,128]{1,0:T(8,128)(2,1)S(1)}, bf16[1024,128]{1,0:T(8,128)(2,1)S(1)}, u32[]{:S(2)}, u32[]{:S(2)}) collective-permute-start(bf16[1024,128]{1,0:T(8,128)(2,1)S(1)} %bitcast.11), channel_id=1, source_target_pairs={{0,24},{1,193},{2,26},{3,195},{4,28},{5,197},{6,30},{7,199},{8,0},... | collective-permute-start | bytes 786440 | tf_op jit(solution)/shard_map/ppermute | solution.py:251
  95.2 7.1 %collective-permute-start.16 = (bf16[1024,128]{1,0:T(8,128)(2,1)S(1)}, bf16[1024,128]{1,0:T(8,128)(2,1)S(1)}, u32[]{:S(2)}, u32[]{:S(2)}) collective-permute-start(bf16[1024,128]{1,0:T(8,128)(2,1)S(1)} %bitcast.12), channel_id=1, source_target_pairs={{0,16},{1,129},{2,18},{3,131},{4,20},{5,133},{6,22},{7,135},{8,24}... | collective-permute-start | bytes 786440 | tf_op jit(solution)/shard_map/ppermute | solution.py:251
  95.2 9.5 %collective-permute-start.15 = (bf16[1024,128]{1,0:T(8,128)(2,1)S(1)}, bf16[1024,128]{1,0:T(8,128)(2,1)S(1)}, u32[]{:S(2)}, u32[]{:S(2)}) collective-permute-start(bf16[1024,128]{1,0:T(8,128)(2,1)S(1)} %bitcast.13), channel_id=1, source_target_pairs={{0,8},{1,65},{2,10},{3,67},{4,12},{5,69},{6,14},{7,71},{8,16},{9,7... | collective-permute-start | bytes 786440 | tf_op jit(solution)/shard_map/ppermute | solution.py:251
  95.9 4.9 %collective-permute-start.19 = (s32[256,1]{1,0:T(8,128)S(1)}, s32[256,1]{1,0:T(8,128)S(1)}, u32[]{:S(2)}, u32[]{:S(2)}) collective-permute-start(s32[256,1]{1,0:T(8,128)S(1)} %copy.11.refs_3_), channel_id=1, source_target_pairs={{0,1},{1,0},{2,3},{3,2},{4,5},{5,4},{6,7},{7,6},{8,9},{9,8},{10,11... | collective-permute-start | bytes 3080 | tf_op jit(solution)/shard_map/ppermute | solution.py:242
  104.8 8.4 %collective-permute-start.21 = (bf16[2048,128]{1,0:T(8,128)(2,1)S(1)}, bf16[2048,128]{1,0:T(8,128)(2,1)S(1)}, u32[]{:S(2)}, u32[]{:S(2)}) collective-permute-start(bf16[2048,128]{1,0:T(8,128)(2,1)S(1)} %constant_dynamic-update-slice_fusion.2.w1), channel_id=1, source_target_pairs={{0,192},{1,25},{2,194},{3,27},{4,196},{5,29},{6,198},{7,31},{8,200... | collective-permute-start | bytes 1572872 | tf_op jit(solution)/shard_map/ppermute | solution.py:251
  105.5 9.6 %collective-permute-start.20 = (bf16[2048,128]{1,0:T(8,128)(2,1)S(1)}, bf16[2048,128]{1,0:T(8,128)(2,1)S(1)}, u32[]{:S(2)}, u32[]{:S(2)}) collective-permute-start(bf16[2048,128]{1,0:T(8,128)(2,1)S(1)} %constant_dynamic-update-slice_fusion.w0), channel_id=1, source_target_pairs={{0,64},{1,9},{2,66},{3,11},{4,68},{5,13},{6,70},{7,15},{8,72},{9,1... | collective-permute-start | bytes 1572872 | tf_op jit(solution)/shard_map/ppermute | solution.py:251
  106.5 14.3 %collective-permute-start.25 = (bf16[2048,128]{1,0:T(8,128)(2,1)S(1)}, bf16[2048,128]{1,0:T(8,128)(2,1)S(1)}, u32[]{:S(2)}, u32[]{:S(2)}) collective-permute-start(bf16[2048,128]{1,0:T(8,128)(2,1)S(1)} %constant_dynamic-update-slice_fusion.2.w1), channel_id=1, source_target_pairs={{0,64},{1,9},{2,66},{3,11},{4,68},{5,13},{6,70},{7,15},{8,72},{9,1... | collective-permute-start | bytes 1572872 | tf_op jit(solution)/shard_map/ppermute | solution.py:251
  106.8 16.9 %collective-permute-start.24 = (bf16[2048,128]{1,0:T(8,128)(2,1)S(1)}, bf16[2048,128]{1,0:T(8,128)(2,1)S(1)}, u32[]{:S(2)}, u32[]{:S(2)}) collective-permute-start(bf16[2048,128]{1,0:T(8,128)(2,1)S(1)} %constant_dynamic-update-slice_fusion.w0), channel_id=1, source_target_pairs={{0,192},{1,25},{2,194},{3,27},{4,196},{5,29},{6,198},{7,31},{8,200... | collective-permute-start | bytes 1572872 | tf_op jit(solution)/shard_map/ppermute | solution.py:251
  115.1 11.5 %collective-permute-start.22 = (bf16[2048,128]{1,0:T(8,128)(2,1)S(1)}, bf16[2048,128]{1,0:T(8,128)(2,1)S(1)}, u32[]{:S(2)}, u32[]{:S(2)}) collective-permute-start(bf16[2048,128]{1,0:T(8,128)(2,1)S(1)} %collective-permute-done.20.w0), channel_id=1, source_target_pairs={{0,64},{1,9},{2,66},{3,11},{4,68},{5,13},{6,70},{7,15},{8,72},{9,1... | collective-permute-start | bytes 1572872 | tf_op jit(solution)/shard_map/ppermute | solution.py:251
  115.1 11.5 %collective-permute-start.23 = (bf16[2048,128]{1,0:T(8,128)(2,1)S(1)}, bf16[2048,128]{1,0:T(8,128)(2,1)S(1)}, u32[]{:S(2)}, u32[]{:S(2)}) collective-permute-start(bf16[2048,128]{1,0:T(8,128)(2,1)S(1)} %collective-permute-done.21.w1), channel_id=1, source_target_pairs={{0,192},{1,25},{2,194},{3,27},{4,196},{5,29},{6,198},{7,31},{8,200... | collective-permute-start | bytes 1572872 | tf_op jit(solution)/shard_map/ppermute | solution.py:251
  128.1 7.5 %collective-permute-start.26 = (f32[256,128]{1,0:T(8,128)S(1)}, f32[256,128]{1,0:T(8,128)S(1)}, u32[]{:S(2)}, u32[]{:S(2)}) collective-permute-start(f32[256,128]{1,0:T(8,128)S(1)} %get-tuple-element.117), channel_id=1, source_target_pairs={{0,1},{1,0},{2,3},{3,2},{4,5},{5,4},{6,7},{7,6},{8,9},{9,8},{10,11... | collective-permute-start | bytes 393224 | tf_op jit(solution)/shard_map/ppermute | solution.py:242
  133.1 1.3 collective-permute-start.27

commit v3 on v2

--- a/solution.py
+++ b/solution.py
@@ -60,34 +60,33 @@
         refs[8][:, rows(i, 256)] = h[...]
 
 
-def store(outs, tiles):
+def store(out, tiles):
     tiles, level = encode(tiles)
-    blocks = len(tiles) // 4
-    for a in range(blocks):
-        out, at = outs[a * len(outs) // blocks], a % (blocks // len(outs)) * 1040
+    for a in range(len(tiles) // 4):
+        at = a * 1040
         for i in range(4):
             out[at + i * 256 : at + i * 256 + 256, :] = tiles[a * 4 + i]
         out[at + 1024 : at + 1040, :] = levels_tile(level[rows(a, 4), :])
 
 
 def grad_kernel(place, lt, *refs):
-    hr, outs, tiles = refs[8], refs[9:], []
-    for i, h in enumerate(refs[:8]):
+    hr, relayed, out, tiles = refs[4], refs[5:-1], refs[-1], []
+    for i, h in enumerate(refs[:4]):
         prod = jnp.dot(lt[:, 0:256], h[...], preferred_element_type=F32)
         prod += jnp.dot(lt[:, 256:512], hr[:, rows(i, 256)], preferred_element_type=F32)
-        tiles += [prod[:, 0:T], prod[:, T:256]]
-    store(outs, tiles)
+        for half in range(2):
+            tile = prod[:, rows(half)]
+            if relayed:
+                tile += added(relayed, i % 2 * 2 + half, i // 2 * 1040)
+            tiles.append(tile)
+    store(out, tiles)
 
 
 def sum_kernel(place, *refs):
-    taken, out = refs[:-1], refs[-1]
-    tiles = []
-    for a in range(out.shape[0] // 1040):
-        tiles += [added(taken, i, a * 1040) for i in range(4)]
-    store([out], tiles)
-
-
-def second_sum_kernel(m0, m1, m2, m3, out):
+    store(refs[-1], [added(refs[:-1], i) for i in range(4)])
+
+
+def second_sum_kernel(place, m0, m1, m2, m3, out):
     low = lax.broadcasted_iota(I32, (T, T), 1) < 64
     tiles = []
     for i in range(4):
@@ -151,29 +150,28 @@
 
 def products(halves, tokens):
     totals = [None, None]
-    for i in range(8):
-        parts = [
-            jnp.concatenate(
-                [halves[i // 4][rows((i % 4 * 4 + zh) * 2 + p, 64), :] for zh in range(4)], axis=0
-            )
-            for p in range(2)
-        ]
+    for i in range(4 * len(halves)):
+        parts = []
+        for p in range(2):
+            at = [((i % 4 * 4 + zh) * 2 + p) * 64 for zh in range(4)]
+            parts.append(jnp.concatenate([halves[i // 4][a : a + 64, :] for a in at], axis=0))
         weight = jnp.concatenate(parts, axis=1)
         for n in range(2):
             part = jnp.dot(tokens(n, i), weight, preferred_element_type=F32)
-            totals[n] = part if i == 0 else totals[n] + part
+            totals[n] = part if totals[n] is None else totals[n] + part
     return totals
 
 
 def first_head_kernel(place, w0, w1, *refs):
-    total = refs[16]
-    for n, term in enumerate(products((w0, w1), lambda n, i: refs[n * 8 + i][...])):
-        total[rows(n, 256), :] = term
+    terms = products((w0, w1), lambda n, i: refs[n * 8 + i][...])
+    for n, term in enumerate(terms):
+        refs[16][rows(n, 256), :] = term
 
 
 def next_head_kernel(place, w0, w1, *refs):
     before, total = refs[16:]
-    for n, term in enumerate(products((w0, w1), lambda n, i: refs[n * 8 + i][...])):
+    terms = products((w0, w1), lambda n, i: refs[n * 8 + i][...])
+    for n, term in enumerate(terms):
         total[rows(n, 256), :] = before[rows(n, 256), :] + term
 
 
@@ -187,11 +185,12 @@
         top = jnp.max(logits, axis=1, keepdims=True)
         expsum = jnp.sum(jnp.exp(logits - top), axis=1, keepdims=True)
         hit = jnp.sum(jnp.where(column == label[...], logits, 0.0), axis=1, keepdims=True)
-        out[...] = jnp.where(lane == 0, top, jnp.where(lane == 1, expsum, hit))
+        found = jnp.where(lane == 0, top, jnp.where(lane == 1, expsum, hit))
+        out[...] = found.T[0:8, :]
 
 
 def loss_kernel(place, a, b, out):
-    a, b = a[...].T, b[...].T
+    a, b = a[...], b[...]
     top = jnp.maximum(a[0:1, :], b[0:1, :])
     total = a[1:2, :] * jnp.exp(a[0:1, :] - top) + b[1:2, :] * jnp.exp(b[0:1, :] - top)
     out[...] = top + jnp.log(total) - (a[2:3, :] + b[2:3, :])
@@ -205,7 +204,7 @@
     return pl.BlockSpec(dims, lambda *_: (0,) * len(dims))
 
 
-def call(kernel, outs, place, args, specs=None):
+def call(kernel, outs, place, args, specs=None, scratch=()):
     many = isinstance(outs, (list, tuple))
     specs = specs or [None] * len(args)
     specs = [s or whole(*a.shape) for s, a in zip(specs, args)]
@@ -217,13 +216,14 @@
             grid=(1,),
             in_specs=specs,
             out_specs=[whole(*o.shape) for o in outs] if many else whole(*outs.shape),
+            scratch_shapes=scratch,
         ),
-        compiler_params=pltpu.CompilerParams(vmem_limit_bytes=16 * 1024 * 1024),
+        compiler_params=pltpu.CompilerParams(vmem_limit_bytes=10 * 1024 * 1024),
         cost_estimate=pl.CostEstimate(flops=1, bytes_accessed=1, transcendentals=0),
     )(place, *args)
 
 
-def columns(far, sign, other=False):
+def columns(far, sign, other=False, nears=(0, 1, 2, 3)):
     def index(near, zl, place):
         x, y, c = place[0], place[1], place[2]
         c = 1 - c if other else c
@@ -233,7 +233,7 @@
 
     return [
         pl.BlockSpec((256, 256), lambda _, p, near=near, zl=zl: index(near, zl, p))
-        for near in range(4)
+        for near in nears
         for zl in range(2)
     ]
 
@@ -255,7 +255,7 @@
     hidden_first, logit_grads, hidden_second, labels_second, master, moment_one, moment_two
 ):
     hold = lax.optimization_barrier
-    place = jnp.stack([lax.axis_index("x"), lax.axis_index("y"), lax.axis_index("c")])
+    place = jnp.stack([lax.axis_index(a) for a in ("x", "y", "c")])
     labels = labels_second[:, None]
     states = (master, moment_one, moment_two)
     far_half = (1 - place[2]) * 256
@@ -268,13 +268,16 @@
         block = shape(256, 2048, dtype=BF16)
         return call(pick_kernel, block, place, args, columns(far, 1, True)), after
 
-    def grad(far, taken):
+    def grad(far, half, taken, *relayed):
         return call(
             grad_kernel,
-            [shape(2080, T, dtype=I16)] * 2,
+            shape(2080, T, dtype=I16),
             place,
-            (turned, *[hidden_first] * 8, taken),
-            [None] + columns(far, 1) + [None],
+            (turned, *[hidden_first] * 4, taken, *relayed),
+            [None]
+            + columns(far, 1, nears=(2 * half, 2 * half + 1))
+            + [pl.BlockSpec((256, 1024), lambda _, p: (0, half))]
+            + [None] * len(relayed),
         )
 
     block, _ = pick(ORDER[0], place)
@@ -290,24 +293,25 @@
     )
     block, turned = pick(ORDER[1], turned)
     following = swap(block)
-    two = grad(2, taken)
-    block, two = pick(3, two)
+    relayed = send(grad(2, 0, taken), 1, True)
+    last = grad(2, 1, taken)
+    block, last = pick(3, last)
+    other_relayed = send(last, 3, True)
     taken, following = following, swap(block)
     turned, block = hold((turned, block))
-    relayed = send(two[0], 1, True), send(two[1], 3, True)
-    ahead = grad(1, taken)
-    block, ahead = pick(0, ahead)
-    taken, following = following, swap(block)
+    last = grad(1, 1, taken)
+    from_behind = [None, send(last, 1, True)]
+    turned, last = hold((turned, last))
+    last = grad(3, 0, following)
+    block, last = pick(0, last)
+    from_ahead = [send(last, 3, True), None]
     turned, block = hold((turned, block))
-    from_behind = [None, send(ahead[1], 1, True)]
-    back = grad(3, taken)
-    from_ahead = [send(back[0], 3, True), None]
-    half_message = shape(2080, T, dtype=I16)
-    from_behind[0] = send(call(sum_kernel, half_message, place, (ahead[0], relayed[0])), 1, True)
-    from_ahead[1] = send(call(sum_kernel, half_message, place, (back[1], relayed[1])), 3, True)
-    own = grad(0, following)
+    from_behind[0] = send(grad(1, 0, taken, relayed), 1, True)
+    from_ahead[1] = send(grad(3, 1, following, other_relayed), 3, True)
+    taken = swap(block)
+    own = [grad(0, 0, taken), grad(0, 1, taken)]
     sums = [own, from_behind, from_ahead]
-    sums, state = hold((sums, state))
+    own[1], state = hold((own[1], state))
     state = swap(state)
 
     blocks = [None] * 4
@@ -322,11 +326,10 @@
         )
         if far:
             blocks[far] = send(blocks[far], far, False)
-    blocks, second, labels = hold((blocks, hidden_second, labels))
+    blocks[0], state = hold((blocks[0], state))
+    chunks = call(second_sum_kernel, shape(1152, T, dtype=I16), place, blocks)
+    chunks, second, labels = hold((chunks, hidden_second, labels))
     other_second, other_labels = swap(second), swap(labels)
-    chunks = call(
-        lambda _, *refs: second_sum_kernel(*refs), shape(1152, T, dtype=I16), place, blocks
-    )
     chunks = lax.all_to_all(chunks, ("zl", "zh"), 0, 0, tiled=True)
     kept, sent, copies = call(
         owner_kernel,
@@ -334,7 +337,6 @@
         place,
         (chunks, *states, state),
     )
-
     copies = lax.all_to_all(copies, ("zl", "zh"), 0, 0, tiled=True)
     pieces = [copies] + [None] * 3
     for far in ORDER:
@@ -348,25 +350,27 @@
     behind, ahead = [None, None], [None, None]
     behind[0], ahead[1] = send(own[0], 1, True), send(own[1], 3, True)
     behind[1], ahead[0] = send(own[1], 1, True), send(own[0], 3, True)
-    tokens = [hidden_second] * 8 + [other_second] * 8
-    specs = [[None] * 2 + columns(far, -1) * 2 for far in range(4)]
-    total = call(first_head_kernel, shape(512, 256), place, (*own, *tokens), specs[0])
+    def head(kernel, places, halves, *before):
+        specs = [columns(far, -1, nears=(2 * half, 2 * half + 1)) for far, half in places]
+        return call(
+            kernel,
+            shape(512, 256),
+            place,
+            (*halves, *[hidden_second] * 8, *[other_second] * 8, *before),
+            [None] * 2 + (specs[0] + specs[1]) * 2 + [None] * len(before),
+        )
+
+    total = head(first_head_kernel, ((0, 0), (0, 1)), own)
     behind[0], ahead[1], total = hold((behind[0], ahead[1], total))
     two = send(behind[0], 1, True), send(ahead[1], 3, True)
-    behind, sent = hold((behind, sent))
+    total = head(next_head_kernel, ((1, 0), (3, 1)), (behind[0], ahead[1]), total)
+    behind[1], total, sent = hold((behind[1], total, sent))
     sent = swap(sent)
-    for far, piece in ((1, behind), (3, ahead)):
-        total = call(
-            next_head_kernel,
-            shape(512, 256),
-            place,
-            (*piece, *tokens, total),
-            specs[far] + [None],
-        )
-    two, total = hold((two, total))
+    total = head(next_head_kernel, ((1, 1), (3, 0)), (behind[1], ahead[0]), total)
+    two, total, sent = hold((two, total, sent))
     stats, other_stats = call(
         last_head_kernel,
-        [shape(256, T)] * 2,
+        [shape(8, 256)] * 2,
         place,
         (*two, *picked, total, labels, other_labels),
     )

time: 137 us -> 129 us (0.942)
  waiting for transfers between devices: 34.8 us -> 9.09 us
  blocking collectives: 11.9 us -> 29.5 us
    all_to_all x0 -> x1, blocking collectives: none -> 19.2 us  [on_device(): chunks = lax.all_to_all(chunks, ('zl', 'zh'), 0, 0, tiled=True)]
    ppermute x18, waiting for transfers between devices: 22.2 us -> 8.64 us  [send(): return lax.ppermute(a, AXES, pairs)]
    all_to_all x1 -> x0, waiting for transfers between devices: 10.1 us -> none  [on_device(): chunks = lax.all_to_all(chunks, ('zl', 'zh'), 0, 0, tiled=True)]
    all_to_all x1 -> x0, starting transfers between devices: 8.02 us -> none  [on_device(): chunks = lax.all_to_all(chunks, ('zl', 'zh'), 0, 0, tiled=True)]
    ppermute x10, starting transfers between devices: 13 us -> 20.7 us  [swap(): return lax.ppermute(a, 'c', [(0, 1), (1, 0)])]
    ppermute x10, waiting for transfers between devices: 2.54 us -> 0.45 us  [swap(): return lax.ppermute(a, 'c', [(0, 1), (1, 0)])]
    all_to_all x1, blocking collectives: 11.9 us -> 10.3 us  [on_device(): copies = lax.all_to_all(copies, ('zl', 'zh'), 0, 0, tiled=True)]
    pallas_call x25 -> x27, Pallas kernels: 39.3 us -> 39.9 us  [call(): pl.pallas_call(kernel, out_shape=outs, grid_spec=pltpu.PrefetchScalarGrid...]
  transfers between devices with their start and end apart: 29 -> 28, of which waited for: 16 -> 6; matrix products, arithmetic and copies ran while one was open for 1% -> 1% of each run, Pallas kernels for 25% -> 28%
where the time goes in v3:
time: 129 us; the launch traced here: 128 us
  starting transfers between devices  42.1 us (33%)
  Pallas kernels  39.9 us (31%)
  blocking collectives  29.5 us (23%)
  waiting for transfers between devices  9.09 us (7%)
  local copies, waits for them, and re-layouts  6.21 us (5%)
    pallas_call x27, Pallas kernels, call(): pl.pallas_call(kernel, out_shape=outs, grid_spec=pltpu.PrefetchScalarGrid...  39.9 us
    ppermute x18, starting transfers between devices, send(): return lax.ppermute(a, AXES, pairs)  21.4 us
    ppermute x10, starting transfers between devices, swap(): return lax.ppermute(a, 'c', [(0, 1), (1, 0)])  20.7 us
    all_to_all x1, blocking collectives, on_device(): chunks = lax.all_to_all(chunks, ('zl', 'zh'), 0, 0, tiled=True)  19.2 us
    all_to_all x1, blocking collectives, on_device(): copies = lax.all_to_all(copies, ('zl', 'zh'), 0, 0, tiled=True)  10.3 us
    ppermute x18, waiting for transfers between devices, send(): return lax.ppermute(a, AXES, pairs)  8.64 us
    unnamed x18, local copies, waits for them, and re-layouts  5.22 us
  transfers between devices with their start and end apart: 28, of which 6 were waited for; matrix products, arithmetic and copies ran while one was open for 1% of the time, Pallas kernels for 28%

profile of v3, /device:TPU:33, one launch (start us, length us, event | category | flops | bytes accessed | tf_op | source)
XLA Modules:
  0.0 128.0 jit_solution(15917102587930964724)
XLA Ops:
  0.6 0.8 collective-permute-start
  1.5 2.2 %copy-done = bf16[256,8192]{1,0:T(8,128)(2,1)S(1)} copy-done((bf16[256,8192]{1,0:T(8,128)(2,1)S(1)}, bf16[256,8192]{1,0:T(8,128)(2,1)}, u32[]{:S(2)}) %copy-start) | copy-done | bytes 4194328
  7.1 1.3 %shard_map.104 = s16[2080,128]{1,0:T(8,128)(2,1)S(1)} custom-call(s32[3]{0:T(128)S(1)} %pad_add_fusion.place, bf16[256,512]{1,0:T(8,128)(2,1)S(1)} %shard_map.103.lt, bf16[256,8192]{1,0:T(8,128)(2,1)S(1)} %copy-done.1, bf16[256,8192]{1,0:T(8,128)(2,1)S(1)} %copy-done.1, bf16[256,8192]{1,0:T(8,128)(2,1)S(1)} %copy-done.1, bf16[256,8192]{1,0:T(8,128)(2,1)S(1)} %copy-done.1, ...), custom_call_target="tpu_custom_call" | custom-call | flops 1 | bytes 1 | tf_op jit(solution)/shard_map/pallas_call | solution.py:211
  8.4 0.7 shard_map.105
  9.4 1.3 %shard_map.111 = s16[2080,128]{1,0:T(8,128)(2,1)S(1)} custom-call(s32[3]{0:T(128)S(1)} %pad_add_fusion.place, bf16[256,512]{1,0:T(8,128)(2,1)S(1)} %shard_map.103.lt, bf16[256,8192]{1,0:T(8,128)(2,1)S(1)} %copy-done.1, bf16[256,8192]{1,0:T(8,128)(2,1)S(1)} %copy-done.1, bf16[256,8192]{1,0:T(8,128)(2,1)S(1)} %copy-done.1, bf16[256,8192]{1,0:T(8,128)(2,1)S(1)} %copy-done.1, ...), custom_call_target="tpu_custom_call" | custom-call | flops 1 | bytes 1 | tf_op jit(solution)/shard_map/pallas_call | solution.py:211
  10.6 1.4 %collective-permute-start.5 = (s16[2080,128]{1,0:T(8,128)(2,1)S(1)}, s16[2080,128]{1,0:T(8,128)(2,1)S(1)}, u32[]{:S(2)}, u32[]{:S(2)}) collective-permute-start(s16[2080,128]{1,0:T(8,128)(2,1)S(1)} %shard_map.111), channel_id=1, source_target_pairs={{0,64},{1,9},{2,66},{3,11},{4,68},{5,13},{6,70},{7,15},{8,72},{9,1... | collective-permute-start | bytes 1597448 | tf_op jit(solution)/shard_map/ppermute | solution.py:251
  12.1 1.5 %collective-permute-start.11 = (s16[2080,128]{1,0:T(8,128)(2,1)S(1)}, s16[2080,128]{1,0:T(8,128)(2,1)S(1)}, u32[]{:S(2)}, u32[]{:S(2)}) collective-permute-start(s16[2080,128]{1,0:T(8,128)(2,1)S(1)} %shard_map.104), channel_id=1, source_target_pairs={{0,192},{1,25},{2,194},{3,27},{4,196},{5,29},{6,198},{7,31},{8,200... | collective-permute-start | bytes 1597448 | tf_op jit(solution)/shard_map/ppermute | solution.py:251
  13.6 2.1 %shard_map.107 = s16[2080,128]{1,0:T(8,128)(2,1)} custom-call(s32[3]{0:T(128)S(1)} %pad_add_fusion.place, bf16[256,512]{1,0:T(8,128)(2,1)S(1)} %shard_map.103.lt, bf16[256,8192]{1,0:T(8,128)(2,1)S(1)} %copy-done.1, bf16[256,8192]{1,0:T(8,128)(2,1)S(1)} %copy-done.1, bf16[256,8192]{1,0:T(8,128)(2,1)S(1)} %copy-done.1, bf16[256,8192]{1,0:T(8,128)(2,1)S(1)} %copy-done.1, ...), custom_call_target="tpu_custom_call" | custom-call | flops 1 | bytes 1 | tf_op jit(solution)/shard_map/pallas_call | solution.py:211
  15.8 2.2 %shard_map.108 = s16[2080,128]{1,0:T(8,128)(2,1)} custom-call(s32[3]{0:T(128)S(1)} %pad_add_fusion.place, bf16[256,512]{1,0:T(8,128)(2,1)S(1)} %shard_map.103.lt, bf16[256,8192]{1,0:T(8,128)(2,1)S(1)} %copy-done.1, bf16[256,8192]{1,0:T(8,128)(2,1)S(1)} %copy-done.1, bf16[256,8192]{1,0:T(8,128)(2,1)S(1)} %copy-done.1, bf16[256,8192]{1,0:T(8,128)(2,1)S(1)} %copy-done.1, ...), custom_call_target="tpu_custom_call" | custom-call | flops 1 | bytes 1 | tf_op jit(solution)/shard_map/pallas_call | solution.py:211
  17.9 1.7 %shard_map.109 = bf16[256,2048]{1,0:T(8,128)(2,1)} custom-call(s32[3]{0:T(128)S(1)} %pad_add_fusion.place, bf16[256,8192]{1,0:T(8,128)(2,1)S(1)} %copy-done.1, bf16[256,8192]{1,0:T(8,128)(2,1)S(1)} %copy-done.1, bf16[256,8192]{1,0:T(8,128)(2,1)S(1)} %copy-done.1, bf16[256,8192]{1,0:T(8,128)(2,1)S(1)} %copy-done.1, bf16[256,8192]{1,0:T(8,128)(2,1)S(1)} %copy-done.1, ...), custom_call_target="tpu_custom_call" | custom-call | flops 1 | bytes 1 | tf_op jit(solution)/shard_map/pallas_call | solution.py:211
  20.3 2.8 %collective-permute-start.7 = (s16[2080,128]{1,0:T(8,128)(2,1)}, s16[2080,128]{1,0:T(8,128)(2,1)S(1)}, u32[]{:S(2)}, u32[]{:S(2)}) collective-permute-start(s16[2080,128]{1,0:T(8,128)(2,1)} %shard_map.108), channel_id=1, source_target_pairs={{0,192},{1,25},{2,194},{3,27},{4,196},{5,29},{6,198},{7,31},{8,200... | collective-permute-start | bytes 1597448 | tf_op jit(solution)/shard_map/ppermute | solution.py:251
  23.1 2.1 %shard_map.112 = s16[2080,128]{1,0:T(8,128)(2,1)} custom-call(s32[3]{0:T(128)S(1)} %pad_add_fusion.place, bf16[256,512]{1,0:T(8,128)(2,1)S(1)} %shard_map.103.lt, bf16[256,8192]{1,0:T(8,128)(2,1)S(1)} %copy-done.1, bf16[256,8192]{1,0:T(8,128)(2,1)S(1)} %copy-done.1, bf16[256,8192]{1,0:T(8,128)(2,1)S(1)} %copy-done.1, bf16[256,8192]{1,0:T(8,128)(2,1)S(1)} %copy-done.1, ...), custom_call_target="tpu_custom_call" | custom-call | flops 1 | bytes 1 | tf_op jit(solution)/shard_map/pallas_call | solution.py:211
  25.2 2.1 %shard_map.116 = s16[2080,128]{1,0:T(8,128)(2,1)} custom-call(s32[3]{0:T(128)S(1)} %pad_add_fusion.place, bf16[256,512]{1,0:T(8,128)(2,1)S(1)} %shard_map.103.lt, bf16[256,8192]{1,0:T(8,128)(2,1)S(1)} %copy-done.1, bf16[256,8192]{1,0:T(8,128)(2,1)S(1)} %copy-done.1, bf16[256,8192]{1,0:T(8,128)(2,1)S(1)} %copy-done.1, bf16[256,8192]{1,0:T(8,128)(2,1)S(1)} %copy-done.1, ...), custom_call_target="tpu_custom_call" | custom-call | flops 1 | bytes 1 | tf_op jit(solution)/shard_map/pallas_call | solution.py:211
  27.3 2.7 %collective-permute-start.12 = (s16[2080,128]{1,0:T(8,128)(2,1)}, s16[2080,128]{1,0:T(8,128)(2,1)S(1)}, u32[]{:S(2)}, u32[]{:S(2)}) collective-permute-start(s16[2080,128]{1,0:T(8,128)(2,1)} %shard_map.116), channel_id=1, source_target_pairs={{0,192},{1,25},{2,194},{3,27},{4,196},{5,29},{6,198},{7,31},{8,200... | collective-permute-start | bytes 1597448 | tf_op jit(solution)/shard_map/ppermute | solution.py:251
  30.0 0.8 constant_dynamic-slice_fusion
  30.8 2.2 %copy-done.2 = bf16[256,8192]{1,0:T(8,128)(2,1)S(1)} copy-done((bf16[256,8192]{1,0:T(8,128)(2,1)S(1)}, bf16[256,8192]{1,0:T(8,128)(2,1)}, u32[]{:S(2)}) %copy-start.2) | copy-done | bytes 4194328
  33.0 1.3 %shard_map.110.refs_0_ = s16[2080,128]{1,0:T(8,128)(2,1)S(1)} custom-call(s32[3]{0:T(128)S(1)} %pad_add_fusion.place, bf16[256,512]{1,0:T(8,128)(2,1)S(1)} %shard_map.103.lt, bf16[256,8192]{1,0:T(8,128)(2,1)S(1)} %copy-done.2, bf16[256,8192]{1,0:T(8,128)(2,1)S(1)} %copy-done.2, bf16[256,8192]{1,0:T(8,128)(2,1)S(1)} %copy-done.2, ...), custom_call_target="tpu_custom_call" | custom-call | flops 1 | bytes 1 | tf_op jit(solution)/shard_map/pallas_call | solution.py:211
  34.3 1.3 %shard_map.114.refs_0_ = s16[2080,128]{1,0:T(8,128)(2,1)S(1)} custom-call(s32[3]{0:T(128)S(1)} %pad_add_fusion.place, bf16[256,512]{1,0:T(8,128)(2,1)S(1)} %shard_map.103.lt, bf16[256,8192]{1,0:T(8,128)(2,1)S(1)} %copy-done.2, bf16[256,8192]{1,0:T(8,128)(2,1)S(1)} %copy-done.2, bf16[256,8192]{1,0:T(8,128)(2,1)S(1)} %copy-done.2, ...), custom_call_target="tpu_custom_call" | custom-call | flops 1 | bytes 1 | tf_op jit(solution)/shard_map/pallas_call | solution.py:211
  35.6 0.9 shard_map.115
  36.7 4.1 %collective-permute-done.10.refs_1_ = s16[2080,128]{1,0:T(8,128)(2,1)S(1)} collective-permute-done((s16[2080,128]{1,0:T(8,128)(2,1)}, s16[2080,128]{1,0:T(8,128)(2,1)S(1)}, u32[]{:S(2)}, u32[]{:S(2)}) %collective-permute-start.10) | collective-permute-done | bytes 532512 | tf_op jit(solution)/shard_map/ppermute | solution.py:251
  40.8 0.9 shard_map.117
  41.6 1.3 %collective-permute-start.13 = (s16[1040,128]{1,0:T(8,128)(2,1)S(1)}, s16[1040,128]{1,0:T(8,128)(2,1)S(1)}, u32[]{:S(2)}, u32[]{:S(2)}) collective-permute-start(s16[1040,128]{1,0:T(8,128)(2,1)S(1)} %shard_map.117), channel_id=1, source_target_pairs={{0,16},{1,129},{2,18},{3,131},{4,20},{5,133},{6,22},{7,135},{8,24}... | collective-permute-start | bytes 798728 | tf_op jit(solution)/shard_map/ppermute | solution.py:251
  43.0 0.9 shard_map.118
  43.9 1.3 %collective-permute-start.14 = (s16[1040,128]{1,0:T(8,128)(2,1)S(1)}, s16[1040,128]{1,0:T(8,128)(2,1)S(1)}, u32[]{:S(2)}, u32[]{:S(2)}) collective-permute-start(s16[1040,128]{1,0:T(8,128)(2,1)S(1)} %shard_map.118), channel_id=1, source_target_pairs={{0,24},{1,193},{2,26},{3,195},{4,28},{5,197},{6,30},{7,199},{8,0},... | collective-permute-start | bytes 798728 | tf_op jit(solution)/shard_map/ppermute | solution.py:251
  45.2 3.3 %collective-permute-start.8 = (f32[96,256]{1,0:T(8,128)S(1)}, f32[96,256]{1,0:T(8,128)S(1)}, u32[]{:S(2)}, u32[]{:S(2)}) collective-permute-start(f32[96,256]{1,0:T(8,128)S(1)} %pad_maximum_fusion), channel_id=1, source_target_pairs={{0,1},{1,0},{2,3},{3,2},{4,5},{5,4},{6,7},{7,6},{8,9},{9,8},{10,11... | collective-permute-start | bytes 294920 | tf_op jit(solution)/shard_map/ppermute | solution.py:242
  48.4 0.9 shard_map.113.m0
  49.4 0.8 collective-permute-done.14.m3
  50.2 1.0 shard_map.119
  51.3 3.0 %collective-permute-start.18 = (bf16[256,8192]{1,0:T(8,128)(2,1)}, bf16[256,8192]{1,0:T(8,128)(2,1)}, u32[]{:S(2)}, u32[]{:S(2)}) collective-permute-start(bf16[256,8192]{1,0:T(8,128)(2,1)} %refs_7_.11), channel_id=1, source_target_pairs={{0,1},{1,0},{2,3},{3,2},{4,5},{5,4},{6,7},{7,6},{8,9},{9,8},{10,11... | collective-permute-start | bytes 12582920 | tf_op jit(solution)/shard_map/ppermute | solution.py:242
  54.3 19.2 %all_to_all.23 = s16[8,144,128]{2,1,0:T(8,128)(2,1)S(1)} all-to-all(s16[8,144,128]{2,1,0:T(8,128)(2,1)S(1)} %bitcast.9), channel_id=1, replica_groups=mesh['x'=4,'zl'=2,'y'=4,'zh'=4,'c'=2] {'zl','zh'}, dimensions={0} | all-to-all | bytes 589824 | tf_op jit(solution)/shard_map/all_to_all | solution.py:333
  73.5 0.7 shard_map.120
  74.2 10.3 %all_to_all.24 = bf16[8,128,128]{2,1,0:T(8,128)(2,1)S(1)} all-to-all(bf16[8,128,128]{2,1,0:T(8,128)(2,1)S(1)} %bitcast.11), channel_id=1, replica_groups=mesh['x'=4,'zl'=2,'y'=4,'zh'=4,'c'=2] {'zl','zh'}, dimensions={0} | all-to-all | bytes 524288 | tf_op jit(solution)/shard_map/all_to_all | solution.py:340
  84.5 1.0 collective-permute-start.16
  86.2 7.1 %collective-permute-start.19 = (s32[256,1]{1,0:T(8,128)S(1)}, s32[256,1]{1,0:T(8,128)S(1)}, u32[]{:S(2)}, u32[]{:S(2)}) collective-permute-start(s32[256,1]{1,0:T(8,128)S(1)} %copy.11.refs_3_), channel_id=1, source_target_pairs={{0,1},{1,0},{2,3},{3,2},{4,5},{5,4},{6,7},{7,6},{8,9},{9,8},{10,11... | collective-permute-start | bytes 3080 | tf_op jit(solution)/shard_map/ppermute | solution.py:242
  93.2 2.0 %shard_map.121.refs_0_ = bf16[256,2048]{1,0:T(8,128)(2,1)S(1)} custom-call(s32[3]{0:T(128)S(1)} %pad_add_fusion.place, bf16[256,8192]{1,0:T(8,128)(2,1)} %refs_7_.11, bf16[256,8192]{1,0:T(8,128)(2,1)} %refs_7_.11, bf16[256,8192]{1,0:T(8,128)(2,1)} %refs_7_.11, bf16[256,8192]{1,0:T(8,128)(2,1)} %refs_7_.11, bf16[256,8192]{1,0:T(8,128)(2,1)} %refs_7_.11, ...), custom_call_target="tpu_custom_call" | custom-call | flops 1 | bytes 1 | tf_op jit(solution)/shard_map/pallas_call | solution.py:211
  95.2 2.0 %shard_map.122.refs_1_ = bf16[256,2048]{1,0:T(8,128)(2,1)S(1)} custom-call(s32[3]{0:T(128)S(1)} %pad_add_fusion.place, bf16[256,8192]{1,0:T(8,128)(2,1)} %collective-permute-done.18.refs_0_.refs_1_.refs_2_.refs_3_.refs_4_.refs_5_.refs_6_.refs_7_.refs_8_.refs_9_.refs_10_.refs_11_.refs_12_.refs_13_.refs_14_.refs_15_, ...), custom_call_target="tpu_custom_call" | custom-call | flops 1 | bytes 1 | tf_op jit(solution)/shard_map/pallas_call | solution.py:211
  97.4 3.0 %collective-permute-start.21 = (bf16[2048,128]{1,0:T(8,128)(2,1)S(1)}, bf16[2048,128]{1,0:T(8,128)(2,1)S(1)}, u32[]{:S(2)}, u32[]{:S(2)}) collective-permute-start(bf16[2048,128]{1,0:T(8,128)(2,1)S(1)} %constant_dynamic-update-slice_fusion.2.w1), channel_id=1, source_target_pairs={{0,192},{1,25},{2,194},{3,27},{4,196},{5,29},{6,198},{7,31},{8,200... | collective-permute-start | bytes 1572872 | tf_op jit(solution)/shard_map/ppermute | solution.py:251
  100.8 2.7 %collective-permute-start.25 = (bf16[2048,128]{1,0:T(8,128)(2,1)S(1)}, bf16[2048,128]{1,0:T(8,128)(2,1)S(1)}, u32[]{:S(2)}, u32[]{:S(2)}) collective-permute-start(bf16[2048,128]{1,0:T(8,128)(2,1)S(1)} %constant_dynamic-update-slice_fusion.w0), channel_id=1, source_target_pairs={{0,192},{1,25},{2,194},{3,27},{4,196},{5,29},{6,198},{7,31},{8,200... | collective-permute-start | bytes 1572872 | tf_op jit(solution)/shard_map/ppermute | solution.py:251
  103.5 2.9 %shard_map.123.refs_16_ = f32[512,256]{1,0:T(8,128)S(1)} custom-call(s32[3]{0:T(128)S(1)} %pad_add_fusion.place, bf16[2048,128]{1,0:T(8,128)(2,1)S(1)} %constant_dynamic-update-slice_fusion.w0, bf16[2048,128]{1,0:T(8,128)(2,1)S(1)} %constant_dynamic-update-slice_fusion.2.w1, bf16[256,8192]{1,0:T(8,128)(2,1)} %refs_7_.11, bf16[256,8192]{1,0:T(8,128)(2,1)} %refs_7_.11, ...), custom_call_target="tpu_custom_call" | custom-call | flops 1 | bytes 1 | tf_op jit(solution)/shard_map/pallas_call | solution.py:211
  106.5 3.5 %collective-permute-done.20.w0 = bf16[2048,128]{1,0:T(8,128)(2,1)S(1)} collective-permute-done((bf16[2048,128]{1,0:T(8,128)(2,1)S(1)}, bf16[2048,128]{1,0:T(8,128)(2,1)S(1)}, u32[]{:S(2)}, u32[]{:S(2)}) %collective-permute-start.20) | collective-permute-done | bytes 524320 | tf_op jit(solution)/shard_map/ppermute | solution.py:251
  110.0 2.7 %collective-permute-start.23 = (bf16[2048,128]{1,0:T(8,128)(2,1)S(1)}, bf16[2048,128]{1,0:T(8,128)(2,1)S(1)}, u32[]{:S(2)}, u32[]{:S(2)}) collective-permute-start(bf16[2048,128]{1,0:T(8,128)(2,1)S(1)} %collective-permute-done.21.w1), channel_id=1, source_target_pairs={{0,192},{1,25},{2,194},{3,27},{4,196},{5,29},{6,198},{7,31},{8,200... | collective-permute-start | bytes 1572872 | tf_op jit(solution)/shard_map/ppermute | solution.py:251
  112.7 2.9 %shard_map.124.refs_16_ = f32[512,256]{1,0:T(8,128)S(1)} custom-call(s32[3]{0:T(128)S(1)} %pad_add_fusion.place, bf16[2048,128]{1,0:T(8,128)(2,1)S(1)} %collective-permute-done.20.w0, bf16[2048,128]{1,0:T(8,128)(2,1)S(1)} %collective-permute-done.21.w1, bf16[256,8192]{1,0:T(8,128)(2,1)} %refs_7_.11, bf16[256,8192]{1,0:T(8,128)(2,1)} %refs_7_.11, ...), custom_call_target="tpu_custom_call" | custom-call | flops 1 | bytes 1 | tf_op jit(solution)/shard_map/pallas_call | solution.py:211
  115.7 3.4 %collective-permute-start.26 = (f32[96,256]{1,0:T(8,128)S(1)}, f32[96,256]{1,0:T(8,128)S(1)}, u32[]{:S(2)}, u32[]{:S(2)}) collective-permute-start(f32[96,256]{1,0:T(8,128)S(1)} %get-tuple-element.84), channel_id=1, source_target_pairs={{0,1},{1,0},{2,3},{3,2},{4,5},{5,4},{6,7},{7,6},{8,9},{9,8},{10,11... | collective-permute-start | bytes 294920 | tf_op jit(solution)/shard_map/ppermute | solution.py:242
  119.1 2.9 %shard_map.125.refs_2_ = f32[512,256]{1,0:T(8,128)S(1)} custom-call(s32[3]{0:T(128)S(1)} %pad_add_fusion.place, bf16[2048,128]{1,0:T(8,128)(2,1)S(1)} %collective-permute-done.24.w0, bf16[2048,128]{1,0:T(8,128)(2,1)S(1)} %collective-permute-done.25.w1, bf16[256,8192]{1,0:T(8,128)(2,1)} %refs_7_.11, bf16[256,8192]{1,0:T(8,128)(2,1)} %refs_7_.11, ...), custom_call_target="tpu_custom_call" | custom-call | flops 1 | bytes 1 | tf_op jit(solution)/shard_map/pallas_call | solution.py:211
  122.0 1.5 %shard_map.126 = (f32[8,256]{1,0:T(8,128)S(1)}, f32[8,256]{1,0:T(8,128)S(1)}) custom-call(s32[3]{0:T(128)S(1)} %pad_add_fusion.place, bf16[2048,128]{1,0:T(8,128)(2,1)S(1)} %collective-permute-done.22.w0, bf16[2048,128]{1,0:T(8,128)(2,1)S(1)} %collective-permute-done.23.w1, bf16[256,2048]{1,0:T(8,128)(2,1)S(1)} %shard_map.121.refs_0_, ...), custom_call_target="tpu_custom_call" | custom-call | flops 1 | bytes 1 | tf_op jit(solution)/shard_map/pallas_call | solution.py:211
  123.5 2.1 %collective-permute-start.27 = (f32[8,256]{1,0:T(8,128)S(1)}, f32[8,256]{1,0:T(8,128)S(1)}, u32[]{:S(2)}, u32[]{:S(2)}) collective-permute-start(f32[8,256]{1,0:T(8,128)S(1)} %get-tuple-element.91), channel_id=1, source_target_pairs={{0,1},{1,0},{2,3},{3,2},{4,5},{5,4},{6,7},{7,6},{8,9},{9,8},{10,11... | collective-permute-start | bytes 24584 | tf_op jit(solution)/shard_map/ppermute | solution.py:242
  125.7 1.2 shard_map.127
  126.9 1.1 shard_map.128
  (62 shorter events, 6.0 us)
Async XLA Ops:
  0.6 3.7 %collective-permute-start = (bf16[256,512]{1,0:T(8,128)(2,1)}, bf16[256,512]{1,0:T(8,128)(2,1)S(1)}, u32[]{:S(2)}, u32[]{:S(2)}) collective-permute-start(bf16[256,512]{1,0:T(8,128)(2,1)} %l.1), channel_id=1, source_target_pairs={{0,1},{1,0},{2,3},{3,2},{4,5},{5,4},{6,7},{7,6},{8,9},{9,8},{10,11... | collective-permute-start | bytes 786440 | tf_op jit(solution)/shard_map/ppermute | solution.py:242
  1.5 2.2 %copy-start = (bf16[256,8192]{1,0:T(8,128)(2,1)S(1)}, bf16[256,8192]{1,0:T(8,128)(2,1)}, u32[]{:S(2)}) copy-start(bf16[256,8192]{1,0:T(8,128)(2,1)} %refs_3_.23) | copy-start | bytes 12582916
  3.7 0.9 copy-start.3
  3.7 2.3 %copy-start.1 = (bf16[256,8192]{1,0:T(8,128)(2,1)S(1)}, bf16[256,8192]{1,0:T(8,128)(2,1)}, u32[]{:S(2)}) copy-start(bf16[256,8192]{1,0:T(8,128)(2,1)} %refs_3_.23) | copy-start | bytes 12582916
  4.4 2.7 %collective-permute-start.1 = (bf16[256,2048]{1,0:T(8,128)(2,1)S(1)}, bf16[256,2048]{1,0:T(8,128)(2,1)S(1)}, u32[]{:S(2)}, u32[]{:S(2)}) collective-permute-start(bf16[256,2048]{1,0:T(8,128)(2,1)S(1)} %shard_map.102), channel_id=1, source_target_pairs={{0,1},{1,0},{2,3},{3,2},{4,5},{5,4},{6,7},{7,6},{8,9},{9,8},{10,11... | collective-permute-start | bytes 3145736 | tf_op jit(solution)/shard_map/ppermute | solution.py:242
  6.6 7.0 %collective-permute-start.2 = (bf16[256,2048]{1,0:T(8,128)(2,1)S(1)}, bf16[256,2048]{1,0:T(8,128)(2,1)S(1)}, u32[]{:S(2)}, u32[]{:S(2)}) collective-permute-start(bf16[256,2048]{1,0:T(8,128)(2,1)S(1)} %shard_map.106), channel_id=1, source_target_pairs={{0,1},{1,0},{2,3},{3,2},{4,5},{5,4},{6,7},{7,6},{8,9},{9,8},{10,11... | collective-permute-start | bytes 3145736 | tf_op jit(solution)/shard_map/ppermute | solution.py:242
  9.1 6.6 %collective-permute-start.3 = (bf16[256,2048]{1,0:T(8,128)(2,1)S(1)}, bf16[256,2048]{1,0:T(8,128)(2,1)S(1)}, u32[]{:S(2)}, u32[]{:S(2)}) collective-permute-start(bf16[256,2048]{1,0:T(8,128)(2,1)S(1)} %shard_map.105), channel_id=1, source_target_pairs={{0,1},{1,0},{2,3},{3,2},{4,5},{5,4},{6,7},{7,6},{8,9},{9,8},{10,11... | collective-permute-start | bytes 3145736 | tf_op jit(solution)/shard_map/ppermute | solution.py:242
  10.6 12.5 %collective-permute-start.5 = (s16[2080,128]{1,0:T(8,128)(2,1)S(1)}, s16[2080,128]{1,0:T(8,128)(2,1)S(1)}, u32[]{:S(2)}, u32[]{:S(2)}) collective-permute-start(s16[2080,128]{1,0:T(8,128)(2,1)S(1)} %shard_map.111), channel_id=1, source_target_pairs={{0,64},{1,9},{2,66},{3,11},{4,68},{5,13},{6,70},{7,15},{8,72},{9,1... | collective-permute-start | bytes 1597448 | tf_op jit(solution)/shard_map/ppermute | solution.py:251
  12.1 13.2 %collective-permute-start.11 = (s16[2080,128]{1,0:T(8,128)(2,1)S(1)}, s16[2080,128]{1,0:T(8,128)(2,1)S(1)}, u32[]{:S(2)}, u32[]{:S(2)}) collective-permute-start(s16[2080,128]{1,0:T(8,128)(2,1)S(1)} %shard_map.104), channel_id=1, source_target_pairs={{0,192},{1,25},{2,194},{3,27},{4,196},{5,29},{6,198},{7,31},{8,200... | collective-permute-start | bytes 1597448 | tf_op jit(solution)/shard_map/ppermute | solution.py:251
  19.6 11.2 %collective-permute-start.4 = (bf16[256,2048]{1,0:T(8,128)(2,1)}, bf16[256,2048]{1,0:T(8,128)(2,1)S(1)}, u32[]{:S(2)}, u32[]{:S(2)}) collective-permute-start(bf16[256,2048]{1,0:T(8,128)(2,1)} %shard_map.109), channel_id=1, source_target_pairs={{0,1},{1,0},{2,3},{3,2},{4,5},{5,4},{6,7},{7,6},{8,9},{9,8},{10,11... | collective-permute-start | bytes 3145736 | tf_op jit(solution)/shard_map/ppermute | solution.py:242
  20.3 15.3 %collective-permute-start.7 = (s16[2080,128]{1,0:T(8,128)(2,1)}, s16[2080,128]{1,0:T(8,128)(2,1)S(1)}, u32[]{:S(2)}, u32[]{:S(2)}) collective-permute-start(s16[2080,128]{1,0:T(8,128)(2,1)} %shard_map.108), channel_id=1, source_target_pairs={{0,192},{1,25},{2,194},{3,27},{4,196},{5,29},{6,198},{7,31},{8,200... | collective-permute-start | bytes 1597448 | tf_op jit(solution)/shard_map/ppermute | solution.py:251
  25.2 4.8 %copy-start.4 = (f32[32,512]{1,0:T(8,128)S(1)}, f32[32,512]{1,0:T(8,128)}, u32[]{:S(2)}) copy-start(f32[32,512]{1,0:T(8,128)} %master.1) | copy-start | bytes 196612
  25.2 10.4 %collective-permute-start.6 = (s16[2080,128]{1,0:T(8,128)(2,1)}, s16[2080,128]{1,0:T(8,128)(2,1)S(1)}, u32[]{:S(2)}, u32[]{:S(2)}) collective-permute-start(s16[2080,128]{1,0:T(8,128)(2,1)} %shard_map.112), channel_id=1, source_target_pairs={{0,64},{1,9},{2,66},{3,11},{4,68},{5,13},{6,70},{7,15},{8,72},{9,1... | collective-permute-start | bytes 1597448 | tf_op jit(solution)/shard_map/ppermute | solution.py:251
  25.2 15.5 %collective-permute-start.10 = (s16[2080,128]{1,0:T(8,128)(2,1)}, s16[2080,128]{1,0:T(8,128)(2,1)S(1)}, u32[]{:S(2)}, u32[]{:S(2)}) collective-permute-start(s16[2080,128]{1,0:T(8,128)(2,1)} %shard_map.107), channel_id=1, source_target_pairs={{0,64},{1,9},{2,66},{3,11},{4,68},{5,13},{6,70},{7,15},{8,72},{9,1... | collective-permute-start | bytes 1597448 | tf_op jit(solution)/shard_map/ppermute | solution.py:251
  27.3 13.4 %collective-permute-start.12 = (s16[2080,128]{1,0:T(8,128)(2,1)}, s16[2080,128]{1,0:T(8,128)(2,1)S(1)}, u32[]{:S(2)}, u32[]{:S(2)}) collective-permute-start(s16[2080,128]{1,0:T(8,128)(2,1)} %shard_map.116), channel_id=1, source_target_pairs={{0,192},{1,25},{2,194},{3,27},{4,196},{5,29},{6,198},{7,31},{8,200... | collective-permute-start | bytes 1597448 | tf_op jit(solution)/shard_map/ppermute | solution.py:251
  30.8 2.2 %copy-start.2 = (bf16[256,8192]{1,0:T(8,128)(2,1)S(1)}, bf16[256,8192]{1,0:T(8,128)(2,1)}, u32[]{:S(2)}) copy-start(bf16[256,8192]{1,0:T(8,128)(2,1)} %refs_3_.23) | copy-start | bytes 12582916
  36.5 36.9 %copy-start.5 = (f32[32,512]{1,0:T(8,128)S(1)}, f32[32,512]{1,0:T(8,128)}, u32[]{:S(2)}) copy-start(f32[32,512]{1,0:T(8,128)} %one.1) | copy-start | bytes 196612
  36.5 36.9 %copy-start.6 = (f32[32,512]{1,0:T(8,128)S(1)}, f32[32,512]{1,0:T(8,128)}, u32[]{:S(2)}) copy-start(f32[32,512]{1,0:T(8,128)} %two.1) | copy-start | bytes 196612
  36.6 49.5 %copy-start.7 = (s32[256]{0:T(256)S(1)}, s32[256]{0:T(256)}, u32[]{:S(2)}) copy-start(s32[256]{0:T(256)} %param.10) | copy-start | bytes 3076
  36.6 12.8 %collective-permute-start.9 = (s16[1040,128]{1,0:T(8,128)(2,1)S(1)}, s16[1040,128]{1,0:T(8,128)(2,1)S(1)}, u32[]{:S(2)}, u32[]{:S(2)}) collective-permute-start(s16[1040,128]{1,0:T(8,128)(2,1)S(1)} %shard_map.115), channel_id=1, source_target_pairs={{0,8},{1,65},{2,10},{3,67},{4,12},{5,69},{6,14},{7,71},{8,16},{9,7... | collective-permute-start | bytes 798728 | tf_op jit(solution)/shard_map/ppermute | solution.py:251
  41.6 7.7 %collective-permute-start.13 = (s16[1040,128]{1,0:T(8,128)(2,1)S(1)}, s16[1040,128]{1,0:T(8,128)(2,1)S(1)}, u32[]{:S(2)}, u32[]{:S(2)}) collective-permute-start(s16[1040,128]{1,0:T(8,128)(2,1)S(1)} %shard_map.117), channel_id=1, source_target_pairs={{0,16},{1,129},{2,18},{3,131},{4,20},{5,133},{6,22},{7,135},{8,24}... | collective-permute-start | bytes 798728 | tf_op jit(solution)/shard_map/ppermute | solution.py:251
  43.9 6.4 %collective-permute-start.14 = (s16[1040,128]{1,0:T(8,128)(2,1)S(1)}, s16[1040,128]{1,0:T(8,128)(2,1)S(1)}, u32[]{:S(2)}, u32[]{:S(2)}) collective-permute-start(s16[1040,128]{1,0:T(8,128)(2,1)S(1)} %shard_map.118), channel_id=1, source_target_pairs={{0,24},{1,193},{2,26},{3,195},{4,28},{5,197},{6,30},{7,199},{8,0},... | collective-permute-start | bytes 798728 | tf_op jit(solution)/shard_map/ppermute | solution.py:251
  45.2 4.2 %collective-permute-start.8 = (f32[96,256]{1,0:T(8,128)S(1)}, f32[96,256]{1,0:T(8,128)S(1)}, u32[]{:S(2)}, u32[]{:S(2)}) collective-permute-start(f32[96,256]{1,0:T(8,128)S(1)} %pad_maximum_fusion), channel_id=1, source_target_pairs={{0,1},{1,0},{2,3},{3,2},{4,5},{5,4},{6,7},{7,6},{8,9},{9,8},{10,11... | collective-permute-start | bytes 294920 | tf_op jit(solution)/shard_map/ppermute | solution.py:242
  51.3 44.0 %collective-permute-start.18 = (bf16[256,8192]{1,0:T(8,128)(2,1)}, bf16[256,8192]{1,0:T(8,128)(2,1)}, u32[]{:S(2)}, u32[]{:S(2)}) collective-permute-start(bf16[256,8192]{1,0:T(8,128)(2,1)} %refs_7_.11), channel_id=1, source_target_pairs={{0,1},{1,0},{2,3},{3,2},{4,5},{5,4},{6,7},{7,6},{8,9},{9,8},{10,11... | collective-permute-start | bytes 12582920 | tf_op jit(solution)/shard_map/ppermute | solution.py:242
  84.5 12.7 %collective-permute-start.17 = (bf16[1024,128]{1,0:T(8,128)(2,1)S(1)}, bf16[1024,128]{1,0:T(8,128)(2,1)S(1)}, u32[]{:S(2)}, u32[]{:S(2)}) collective-permute-start(bf16[1024,128]{1,0:T(8,128)(2,1)S(1)} %bitcast.12), channel_id=1, source_target_pairs={{0,24},{1,193},{2,26},{3,195},{4,28},{5,197},{6,30},{7,199},{8,0},... | collective-permute-start | bytes 786440 | tf_op jit(solution)/shard_map/ppermute | solution.py:251
  84.5 12.7 %collective-permute-start.16 = (bf16[1024,128]{1,0:T(8,128)(2,1)S(1)}, bf16[1024,128]{1,0:T(8,128)(2,1)S(1)}, u32[]{:S(2)}, u32[]{:S(2)}) collective-permute-start(bf16[1024,128]{1,0:T(8,128)(2,1)S(1)} %bitcast.13), channel_id=1, source_target_pairs={{0,16},{1,129},{2,18},{3,131},{4,20},{5,133},{6,22},{7,135},{8,24}... | collective-permute-start | bytes 786440 | tf_op jit(solution)/shard_map/ppermute | solution.py:251
  85.5 11.7 %collective-permute-start.15 = (bf16[1024,128]{1,0:T(8,128)(2,1)S(1)}, bf16[1024,128]{1,0:T(8,128)(2,1)S(1)}, u32[]{:S(2)}, u32[]{:S(2)}) collective-permute-start(bf16[1024,128]{1,0:T(8,128)(2,1)S(1)} %bitcast.14), channel_id=1, source_target_pairs={{0,8},{1,65},{2,10},{3,67},{4,12},{5,69},{6,14},{7,71},{8,16},{9,7... | collective-permute-start | bytes 786440 | tf_op jit(solution)/shard_map/ppermute | solution.py:251
  86.2 11.1 %collective-permute-start.19 = (s32[256,1]{1,0:T(8,128)S(1)}, s32[256,1]{1,0:T(8,128)S(1)}, u32[]{:S(2)}, u32[]{:S(2)}) collective-permute-start(s32[256,1]{1,0:T(8,128)S(1)} %copy.11.refs_3_), channel_id=1, source_target_pairs={{0,1},{1,0},{2,3},{3,2},{4,5},{5,4},{6,7},{7,6},{8,9},{9,8},{10,11... | collective-permute-start | bytes 3080 | tf_op jit(solution)/shard_map/ppermute | solution.py:242
  97.4 9.2 %collective-permute-start.21 = (bf16[2048,128]{1,0:T(8,128)(2,1)S(1)}, bf16[2048,128]{1,0:T(8,128)(2,1)S(1)}, u32[]{:S(2)}, u32[]{:S(2)}) collective-permute-start(bf16[2048,128]{1,0:T(8,128)(2,1)S(1)} %constant_dynamic-update-slice_fusion.2.w1), channel_id=1, source_target_pairs={{0,192},{1,25},{2,194},{3,27},{4,196},{5,29},{6,198},{7,31},{8,200... | collective-permute-start | bytes 1572872 | tf_op jit(solution)/shard_map/ppermute | solution.py:251
  100.4 9.6 %collective-permute-start.20 = (bf16[2048,128]{1,0:T(8,128)(2,1)S(1)}, bf16[2048,128]{1,0:T(8,128)(2,1)S(1)}, u32[]{:S(2)}, u32[]{:S(2)}) collective-permute-start(bf16[2048,128]{1,0:T(8,128)(2,1)S(1)} %constant_dynamic-update-slice_fusion.w0), channel_id=1, source_target_pairs={{0,64},{1,9},{2,66},{3,11},{4,68},{5,13},{6,70},{7,15},{8,72},{9,1... | collective-permute-start | bytes 1572872 | tf_op jit(solution)/shard_map/ppermute | solution.py:251
  100.5 15.1 %collective-permute-start.24 = (bf16[2048,128]{1,0:T(8,128)(2,1)S(1)}, bf16[2048,128]{1,0:T(8,128)(2,1)S(1)}, u32[]{:S(2)}, u32[]{:S(2)}) collective-permute-start(bf16[2048,128]{1,0:T(8,128)(2,1)S(1)} %constant_dynamic-update-slice_fusion.2.w1), channel_id=1, source_target_pairs={{0,64},{1,9},{2,66},{3,11},{4,68},{5,13},{6,70},{7,15},{8,72},{9,1... | collective-permute-start | bytes 1572872 | tf_op jit(solution)/shard_map/ppermute | solution.py:251
  100.8 18.2 %collective-permute-start.25 = (bf16[2048,128]{1,0:T(8,128)(2,1)S(1)}, bf16[2048,128]{1,0:T(8,128)(2,1)S(1)}, u32[]{:S(2)}, u32[]{:S(2)}) collective-permute-start(bf16[2048,128]{1,0:T(8,128)(2,1)S(1)} %constant_dynamic-update-slice_fusion.w0), channel_id=1, source_target_pairs={{0,192},{1,25},{2,194},{3,27},{4,196},{5,29},{6,198},{7,31},{8,200... | collective-permute-start | bytes 1572872 | tf_op jit(solution)/shard_map/ppermute | solution.py:251
  110.0 11.9 %collective-permute-start.22 = (bf16[2048,128]{1,0:T(8,128)(2,1)S(1)}, bf16[2048,128]{1,0:T(8,128)(2,1)S(1)}, u32[]{:S(2)}, u32[]{:S(2)}) collective-permute-start(bf16[2048,128]{1,0:T(8,128)(2,1)S(1)} %collective-permute-done.20.w0), channel_id=1, source_target_pairs={{0,64},{1,9},{2,66},{3,11},{4,68},{5,13},{6,70},{7,15},{8,72},{9,1... | collective-permute-start | bytes 1572872 | tf_op jit(solution)/shard_map/ppermute | solution.py:251
  110.0 11.9 %collective-permute-start.23 = (bf16[2048,128]{1,0:T(8,128)(2,1)S(1)}, bf16[2048,128]{1,0:T(8,128)(2,1)S(1)}, u32[]{:S(2)}, u32[]{:S(2)}) collective-permute-start(bf16[2048,128]{1,0:T(8,128)(2,1)S(1)} %collective-permute-done.21.w1), channel_id=1, source_target_pairs={{0,192},{1,25},{2,194},{3,27},{4,196},{5,29},{6,198},{7,31},{8,200... | collective-permute-start | bytes 1572872 | tf_op jit(solution)/shard_map/ppermute | solution.py:251
  115.7 6.3 %collective-permute-start.26 = (f32[96,256]{1,0:T(8,128)S(1)}, f32[96,256]{1,0:T(8,128)S(1)}, u32[]{:S(2)}, u32[]{:S(2)}) collective-permute-start(f32[96,256]{1,0:T(8,128)S(1)} %get-tuple-element.84), channel_id=1, source_target_pairs={{0,1},{1,0},{2,3},{3,2},{4,5},{5,4},{6,7},{7,6},{8,9},{9,8},{10,11... | collective-permute-start | bytes 294920 | tf_op jit(solution)/shard_map/ppermute | solution.py:242
  123.5 3.3 %collective-permute-start.27 = (f32[8,256]{1,0:T(8,128)S(1)}, f32[8,256]{1,0:T(8,128)S(1)}, u32[]{:S(2)}, u32[]{:S(2)}) collective-permute-start(f32[8,256]{1,0:T(8,128)S(1)} %get-tuple-element.91), channel_id=1, source_target_pairs={{0,1},{1,0},{2,3},{3,2},{4,5},{5,4},{6,7},{7,6},{8,9},{9,8},{10,11... | collective-permute-start | bytes 24584 | tf_op jit(solution)/shard_map/ppermute | solution.py:242

commit v4 on v3

--- a/solution.py
+++ b/solution.py
@@ -204,7 +204,7 @@
     return pl.BlockSpec(dims, lambda *_: (0,) * len(dims))
 
 
-def call(kernel, outs, place, args, specs=None, scratch=()):
+def call(kernel, outs, place, args, specs=None, vmem=6):
     many = isinstance(outs, (list, tuple))
     specs = specs or [None] * len(args)
     specs = [s or whole(*a.shape) for s, a in zip(specs, args)]
@@ -216,9 +216,8 @@
             grid=(1,),
             in_specs=specs,
             out_specs=[whole(*o.shape) for o in outs] if many else whole(*outs.shape),
-            scratch_shapes=scratch,
         ),
-        compiler_params=pltpu.CompilerParams(vmem_limit_bytes=10 * 1024 * 1024),
+        compiler_params=pltpu.CompilerParams(vmem_limit_bytes=vmem * 1024 * 1024),
         cost_estimate=pl.CostEstimate(flops=1, bytes_accessed=1, transcendentals=0),
     )(place, *args)
 
@@ -266,7 +265,7 @@
         h, after = hold((hidden_first, after))
         args = [h] * 8
         block = shape(256, 2048, dtype=BF16)
-        return call(pick_kernel, block, place, args, columns(far, 1, True)), after
+        return call(pick_kernel, block, place, args, columns(far, 1, True, (0, 2, 1, 3))), after
 
     def grad(far, half, taken, *relayed):
         return call(
@@ -275,7 +274,7 @@
             place,
             (turned, *[hidden_first] * 4, taken, *relayed),
             [None]
-            + columns(far, 1, nears=(2 * half, 2 * half + 1))
+            + columns(far, 1, nears=(half, half + 2))
             + [pl.BlockSpec((256, 1024), lambda _, p: (0, half))]
             + [None] * len(relayed),
         )
@@ -316,21 +315,21 @@
 
     blocks = [None] * 4
     for far in ORDER + (0,):
-        spec = pl.BlockSpec((1040, T), lambda s, p, far=far: (far % 2, 0))
+        spec = pl.BlockSpec((1040, T), lambda s, p, far=far: (far // 2, 0))
         blocks[far] = call(
             sum_kernel,
             shape(1040, T, dtype=I16),
             place,
-            [taken[far // 2] for taken in sums],
+            [taken[far % 2] for taken in sums],
             [spec] * 3,
         )
         if far:
             blocks[far] = send(blocks[far], far, False)
     blocks[0], state = hold((blocks[0], state))
     chunks = call(second_sum_kernel, shape(1152, T, dtype=I16), place, blocks)
+    chunks = lax.all_to_all(chunks, ("zl", "zh"), 0, 0, tiled=True)
     chunks, second, labels = hold((chunks, hidden_second, labels))
     other_second, other_labels = swap(second), swap(labels)
-    chunks = lax.all_to_all(chunks, ("zl", "zh"), 0, 0, tiled=True)
     kept, sent, copies = call(
         owner_kernel,
         [shape(96, 256)] * 2 + [shape(1024, T, dtype=BF16)],
@@ -358,6 +357,7 @@
             place,
             (*halves, *[hidden_second] * 8, *[other_second] * 8, *before),
             [None] * 2 + (specs[0] + specs[1]) * 2 + [None] * len(before),
+            10,
         )
 
     total = head(first_head_kernel, ((0, 0), (0, 1)), own)
@@ -373,6 +373,8 @@
         [shape(8, 256)] * 2,
         place,
         (*two, *picked, total, labels, other_labels),
+        None,
+        10,
     )
     updated = call(join_kernel, [shape(32, 512)] * 3, place, (kept, sent))
     other_stats, updated = hold((swap(other_stats), updated))

time: 129 us -> 129 us (level)
  blocking collectives: 29.5 us -> 31 us
    all_to_all x1, blocking collectives: 10.3 us -> 14.7 us  [on_device(): copies = lax.all_to_all(copies, ('zl', 'zh'), 0, 0, tiled=True)]
    all_to_all x1, blocking collectives: 19.2 us -> 16.3 us  [on_device(): chunks = lax.all_to_all(chunks, ('zl', 'zh'), 0, 0, tiled=True)]
    ppermute x10, starting transfers between devices: 20.7 us -> 19.1 us  [swap(): return lax.ppermute(a, 'c', [(0, 1), (1, 0)])]
where the time goes in v4:
time: 129 us; the launch traced here: 128 us
  starting transfers between devices  41.7 us (32%)
  Pallas kernels  40 us (31%)
  blocking collectives  31 us (24%)
  waiting for transfers between devices  8.17 us (6%)
  local copies, waits for them, and re-layouts  6.2 us (5%)
    pallas_call x27, Pallas kernels, call(): pl.pallas_call(kernel, out_shape=outs, grid_spec=pltpu.PrefetchScalarGrid...  40 us
    ppermute x18, starting transfers between devices, send(): return lax.ppermute(a, AXES, pairs)  22.6 us
    ppermute x10, starting transfers between devices, swap(): return lax.ppermute(a, 'c', [(0, 1), (1, 0)])  19.1 us
    all_to_all x1, blocking collectives, on_device(): chunks = lax.all_to_all(chunks, ('zl', 'zh'), 0, 0, tiled=True)  16.3 us
    all_to_all x1, blocking collectives, on_device(): copies = lax.all_to_all(copies, ('zl', 'zh'), 0, 0, tiled=True)  14.7 us
    ppermute x18, waiting for transfers between devices, send(): return lax.ppermute(a, AXES, pairs)  7.69 us
    unnamed x18, local copies, waits for them, and re-layouts  5.21 us
  transfers between devices with their start and end apart: 28, of which 6 were waited for; matrix products, arithmetic and copies ran while one was open for 1% of the time, Pallas kernels for 28%

profile of v4, /device:TPU:33, one launch (start us, length us, event | category | flops | bytes accessed | tf_op | source)
XLA Modules:
  0.0 128.1 jit_solution(15283387314544356949)
XLA Ops:
  0.6 0.8 collective-permute-start
  1.5 2.2 %copy-done = bf16[256,8192]{1,0:T(8,128)(2,1)S(1)} copy-done((bf16[256,8192]{1,0:T(8,128)(2,1)S(1)}, bf16[256,8192]{1,0:T(8,128)(2,1)}, u32[]{:S(2)}) %copy-start) | copy-done | bytes 4194328
  7.1 1.3 %shard_map.104 = s16[2080,128]{1,0:T(8,128)(2,1)S(1)} custom-call(s32[3]{0:T(128)S(1)} %pad_add_fusion.place, bf16[256,512]{1,0:T(8,128)(2,1)S(1)} %shard_map.103.lt, bf16[256,8192]{1,0:T(8,128)(2,1)S(1)} %copy-done.1, bf16[256,8192]{1,0:T(8,128)(2,1)S(1)} %copy-done.1, bf16[256,8192]{1,0:T(8,128)(2,1)S(1)} %copy-done.1, bf16[256,8192]{1,0:T(8,128)(2,1)S(1)} %copy-done.1, ...), custom_call_target="tpu_custom_call" | custom-call | flops 1 | bytes 1 | tf_op jit(solution)/shard_map/pallas_call | solution.py:211
  9.4 1.3 %shard_map.111 = s16[2080,128]{1,0:T(8,128)(2,1)S(1)} custom-call(s32[3]{0:T(128)S(1)} %pad_add_fusion.place, bf16[256,512]{1,0:T(8,128)(2,1)S(1)} %shard_map.103.lt, bf16[256,8192]{1,0:T(8,128)(2,1)S(1)} %copy-done.1, bf16[256,8192]{1,0:T(8,128)(2,1)S(1)} %copy-done.1, bf16[256,8192]{1,0:T(8,128)(2,1)S(1)} %copy-done.1, bf16[256,8192]{1,0:T(8,128)(2,1)S(1)} %copy-done.1, ...), custom_call_target="tpu_custom_call" | custom-call | flops 1 | bytes 1 | tf_op jit(solution)/shard_map/pallas_call | solution.py:211
  10.7 1.3 %collective-permute-start.5 = (s16[2080,128]{1,0:T(8,128)(2,1)S(1)}, s16[2080,128]{1,0:T(8,128)(2,1)S(1)}, u32[]{:S(2)}, u32[]{:S(2)}) collective-permute-start(s16[2080,128]{1,0:T(8,128)(2,1)S(1)} %shard_map.111), channel_id=1, source_target_pairs={{0,64},{1,9},{2,66},{3,11},{4,68},{5,13},{6,70},{7,15},{8,72},{9,1... | collective-permute-start | bytes 1597448 | tf_op jit(solution)/shard_map/ppermute | solution.py:250
  12.0 1.5 %collective-permute-start.10 = (s16[2080,128]{1,0:T(8,128)(2,1)S(1)}, s16[2080,128]{1,0:T(8,128)(2,1)S(1)}, u32[]{:S(2)}, u32[]{:S(2)}) collective-permute-start(s16[2080,128]{1,0:T(8,128)(2,1)S(1)} %shard_map.104), channel_id=1, source_target_pairs={{0,192},{1,25},{2,194},{3,27},{4,196},{5,29},{6,198},{7,31},{8,200... | collective-permute-start | bytes 1597448 | tf_op jit(solution)/shard_map/ppermute | solution.py:250
  13.6 2.1 %shard_map.107 = s16[2080,128]{1,0:T(8,128)(2,1)} custom-call(s32[3]{0:T(128)S(1)} %pad_add_fusion.place, bf16[256,512]{1,0:T(8,128)(2,1)S(1)} %shard_map.103.lt, bf16[256,8192]{1,0:T(8,128)(2,1)S(1)} %copy-done.1, bf16[256,8192]{1,0:T(8,128)(2,1)S(1)} %copy-done.1, bf16[256,8192]{1,0:T(8,128)(2,1)S(1)} %copy-done.1, bf16[256,8192]{1,0:T(8,128)(2,1)S(1)} %copy-done.1, ...), custom_call_target="tpu_custom_call" | custom-call | flops 1 | bytes 1 | tf_op jit(solution)/shard_map/pallas_call | solution.py:211
  15.7 2.2 %shard_map.108 = s16[2080,128]{1,0:T(8,128)(2,1)} custom-call(s32[3]{0:T(128)S(1)} %pad_add_fusion.place, bf16[256,512]{1,0:T(8,128)(2,1)S(1)} %shard_map.103.lt, bf16[256,8192]{1,0:T(8,128)(2,1)S(1)} %copy-done.1, bf16[256,8192]{1,0:T(8,128)(2,1)S(1)} %copy-done.1, bf16[256,8192]{1,0:T(8,128)(2,1)S(1)} %copy-done.1, bf16[256,8192]{1,0:T(8,128)(2,1)S(1)} %copy-done.1, ...), custom_call_target="tpu_custom_call" | custom-call | flops 1 | bytes 1 | tf_op jit(solution)/shard_map/pallas_call | solution.py:211
  17.9 1.7 %shard_map.109 = bf16[256,2048]{1,0:T(8,128)(2,1)} custom-call(s32[3]{0:T(128)S(1)} %pad_add_fusion.place, bf16[256,8192]{1,0:T(8,128)(2,1)S(1)} %copy-done.1, bf16[256,8192]{1,0:T(8,128)(2,1)S(1)} %copy-done.1, bf16[256,8192]{1,0:T(8,128)(2,1)S(1)} %copy-done.1, bf16[256,8192]{1,0:T(8,128)(2,1)S(1)} %copy-done.1, bf16[256,8192]{1,0:T(8,128)(2,1)S(1)} %copy-done.1, ...), custom_call_target="tpu_custom_call" | custom-call | flops 1 | bytes 1 | tf_op jit(solution)/shard_map/pallas_call | solution.py:211
  19.6 0.7 collective-permute-start.4
  20.3 2.8 %collective-permute-start.7 = (s16[2080,128]{1,0:T(8,128)(2,1)}, s16[2080,128]{1,0:T(8,128)(2,1)S(1)}, u32[]{:S(2)}, u32[]{:S(2)}) collective-permute-start(s16[2080,128]{1,0:T(8,128)(2,1)} %shard_map.108), channel_id=1, source_target_pairs={{0,192},{1,25},{2,194},{3,27},{4,196},{5,29},{6,198},{7,31},{8,200... | collective-permute-start | bytes 1597448 | tf_op jit(solution)/shard_map/ppermute | solution.py:250
  23.1 2.1 %shard_map.112 = s16[2080,128]{1,0:T(8,128)(2,1)} custom-call(s32[3]{0:T(128)S(1)} %pad_add_fusion.place, bf16[256,512]{1,0:T(8,128)(2,1)S(1)} %shard_map.103.lt, bf16[256,8192]{1,0:T(8,128)(2,1)S(1)} %copy-done.1, bf16[256,8192]{1,0:T(8,128)(2,1)S(1)} %copy-done.1, bf16[256,8192]{1,0:T(8,128)(2,1)S(1)} %copy-done.1, bf16[256,8192]{1,0:T(8,128)(2,1)S(1)} %copy-done.1, ...), custom_call_target="tpu_custom_call" | custom-call | flops 1 | bytes 1 | tf_op jit(solution)/shard_map/pallas_call | solution.py:211
  25.2 2.1 %shard_map.115 = s16[2080,128]{1,0:T(8,128)(2,1)} custom-call(s32[3]{0:T(128)S(1)} %pad_add_fusion.place, bf16[256,512]{1,0:T(8,128)(2,1)S(1)} %shard_map.103.lt, bf16[256,8192]{1,0:T(8,128)(2,1)S(1)} %copy-done.1, bf16[256,8192]{1,0:T(8,128)(2,1)S(1)} %copy-done.1, bf16[256,8192]{1,0:T(8,128)(2,1)S(1)} %copy-done.1, bf16[256,8192]{1,0:T(8,128)(2,1)S(1)} %copy-done.1, ...), custom_call_target="tpu_custom_call" | custom-call | flops 1 | bytes 1 | tf_op jit(solution)/shard_map/pallas_call | solution.py:211
  27.3 2.7 %collective-permute-start.11 = (s16[2080,128]{1,0:T(8,128)(2,1)}, s16[2080,128]{1,0:T(8,128)(2,1)S(1)}, u32[]{:S(2)}, u32[]{:S(2)}) collective-permute-start(s16[2080,128]{1,0:T(8,128)(2,1)} %shard_map.115), channel_id=1, source_target_pairs={{0,192},{1,25},{2,194},{3,27},{4,196},{5,29},{6,198},{7,31},{8,200... | collective-permute-start | bytes 1597448 | tf_op jit(solution)/shard_map/ppermute | solution.py:250
  30.0 0.8 constant_dynamic-slice_fusion
  30.8 2.2 %copy-done.2 = bf16[256,8192]{1,0:T(8,128)(2,1)S(1)} copy-done((bf16[256,8192]{1,0:T(8,128)(2,1)S(1)}, bf16[256,8192]{1,0:T(8,128)(2,1)}, u32[]{:S(2)}) %copy-start.2) | copy-done | bytes 4194328
  33.0 1.3 %shard_map.110.refs_0_ = s16[2080,128]{1,0:T(8,128)(2,1)S(1)} custom-call(s32[3]{0:T(128)S(1)} %pad_add_fusion.place, bf16[256,512]{1,0:T(8,128)(2,1)S(1)} %shard_map.103.lt, bf16[256,8192]{1,0:T(8,128)(2,1)S(1)} %copy-done.2, bf16[256,8192]{1,0:T(8,128)(2,1)S(1)} %copy-done.2, bf16[256,8192]{1,0:T(8,128)(2,1)S(1)} %copy-done.2, ...), custom_call_target="tpu_custom_call" | custom-call | flops 1 | bytes 1 | tf_op jit(solution)/shard_map/pallas_call | solution.py:211
  34.3 1.3 %shard_map.114.refs_0_ = s16[2080,128]{1,0:T(8,128)(2,1)S(1)} custom-call(s32[3]{0:T(128)S(1)} %pad_add_fusion.place, bf16[256,512]{1,0:T(8,128)(2,1)S(1)} %shard_map.103.lt, bf16[256,8192]{1,0:T(8,128)(2,1)S(1)} %copy-done.2, bf16[256,8192]{1,0:T(8,128)(2,1)S(1)} %copy-done.2, bf16[256,8192]{1,0:T(8,128)(2,1)S(1)} %copy-done.2, ...), custom_call_target="tpu_custom_call" | custom-call | flops 1 | bytes 1 | tf_op jit(solution)/shard_map/pallas_call | solution.py:211
  35.6 0.9 shard_map.117
  36.6 1.6 %collective-permute-start.13 = (s16[1040,128]{1,0:T(8,128)(2,1)S(1)}, s16[1040,128]{1,0:T(8,128)(2,1)S(1)}, u32[]{:S(2)}, u32[]{:S(2)}) collective-permute-start(s16[1040,128]{1,0:T(8,128)(2,1)S(1)} %shard_map.117), channel_id=1, source_target_pairs={{0,16},{1,129},{2,18},{3,131},{4,20},{5,133},{6,22},{7,135},{8,24}... | collective-permute-start | bytes 798728 | tf_op jit(solution)/shard_map/ppermute | solution.py:250
  38.2 2.6 %collective-permute-done.9.refs_1_ = s16[2080,128]{1,0:T(8,128)(2,1)S(1)} collective-permute-done((s16[2080,128]{1,0:T(8,128)(2,1)}, s16[2080,128]{1,0:T(8,128)(2,1)S(1)}, u32[]{:S(2)}, u32[]{:S(2)}) %collective-permute-start.9) | collective-permute-done | bytes 532512 | tf_op jit(solution)/shard_map/ppermute | solution.py:250
  40.7 0.9 shard_map.116
  41.7 0.9 shard_map.118
  42.6 2.7 %collective-permute-start.14 = (s16[1040,128]{1,0:T(8,128)(2,1)S(1)}, s16[1040,128]{1,0:T(8,128)(2,1)S(1)}, u32[]{:S(2)}, u32[]{:S(2)}) collective-permute-start(s16[1040,128]{1,0:T(8,128)(2,1)S(1)} %shard_map.118), channel_id=1, source_target_pairs={{0,24},{1,193},{2,26},{3,195},{4,28},{5,197},{6,30},{7,199},{8,0},... | collective-permute-start | bytes 798728 | tf_op jit(solution)/shard_map/ppermute | solution.py:250
  45.4 4.0 %collective-permute-start.8 = (f32[96,256]{1,0:T(8,128)S(1)}, f32[96,256]{1,0:T(8,128)S(1)}, u32[]{:S(2)}, u32[]{:S(2)}) collective-permute-start(f32[96,256]{1,0:T(8,128)S(1)} %pad_maximum_fusion), channel_id=1, source_target_pairs={{0,1},{1,0},{2,3},{3,2},{4,5},{5,4},{6,7},{7,6},{8,9},{9,8},{10,11... | collective-permute-start | bytes 294920 | tf_op jit(solution)/shard_map/ppermute | solution.py:241
  49.4 0.9 shard_map.113.m0
  50.3 1.0 shard_map.119
  51.4 16.3 %all_to_all.24 = s16[8,144,128]{2,1,0:T(8,128)(2,1)S(1)} all-to-all(s16[8,144,128]{2,1,0:T(8,128)(2,1)S(1)} %bitcast.9), channel_id=1, replica_groups=mesh['x'=4,'zl'=2,'y'=4,'zh'=4,'c'=2] {'zl','zh'}, dimensions={0} | all-to-all | bytes 589824 | tf_op jit(solution)/shard_map/all_to_all | solution.py:330
  67.7 4.3 %collective-permute-start.18 = (bf16[256,8192]{1,0:T(8,128)(2,1)}, bf16[256,8192]{1,0:T(8,128)(2,1)}, u32[]{:S(2)}, u32[]{:S(2)}) collective-permute-start(bf16[256,8192]{1,0:T(8,128)(2,1)} %refs_7_.11), channel_id=1, source_target_pairs={{0,1},{1,0},{2,3},{3,2},{4,5},{5,4},{6,7},{7,6},{8,9},{9,8},{10,11... | collective-permute-start | bytes 12582920 | tf_op jit(solution)/shard_map/ppermute | solution.py:241
  72.0 0.7 shard_map.120
  72.8 14.7 %all_to_all.25 = bf16[8,128,128]{2,1,0:T(8,128)(2,1)S(1)} all-to-all(bf16[8,128,128]{2,1,0:T(8,128)(2,1)S(1)} %bitcast.11), channel_id=1, replica_groups=mesh['x'=4,'zl'=2,'y'=4,'zh'=4,'c'=2] {'zl','zh'}, dimensions={0} | all-to-all | bytes 524288 | tf_op jit(solution)/shard_map/all_to_all | solution.py:339
  87.4 0.9 collective-permute-start.17
  89.1 3.6 %collective-permute-start.19 = (s32[256,1]{1,0:T(8,128)S(1)}, s32[256,1]{1,0:T(8,128)S(1)}, u32[]{:S(2)}, u32[]{:S(2)}) collective-permute-start(s32[256,1]{1,0:T(8,128)S(1)} %copy.11.refs_3_), channel_id=1, source_target_pairs={{0,1},{1,0},{2,3},{3,2},{4,5},{5,4},{6,7},{7,6},{8,9},{9,8},{10,11... | collective-permute-start | bytes 3080 | tf_op jit(solution)/shard_map/ppermute | solution.py:241
  92.7 2.0 %shard_map.121.refs_0_ = bf16[256,2048]{1,0:T(8,128)(2,1)S(1)} custom-call(s32[3]{0:T(128)S(1)} %pad_add_fusion.place, bf16[256,8192]{1,0:T(8,128)(2,1)} %refs_7_.11, bf16[256,8192]{1,0:T(8,128)(2,1)} %refs_7_.11, bf16[256,8192]{1,0:T(8,128)(2,1)} %refs_7_.11, bf16[256,8192]{1,0:T(8,128)(2,1)} %refs_7_.11, bf16[256,8192]{1,0:T(8,128)(2,1)} %refs_7_.11, ...), custom_call_target="tpu_custom_call" | custom-call | flops 1 | bytes 1 | tf_op jit(solution)/shard_map/pallas_call | solution.py:211
  94.7 2.0 %shard_map.122.refs_1_ = bf16[256,2048]{1,0:T(8,128)(2,1)S(1)} custom-call(s32[3]{0:T(128)S(1)} %pad_add_fusion.place, bf16[256,8192]{1,0:T(8,128)(2,1)} %collective-permute-done.18.refs_0_.refs_1_.refs_2_.refs_3_.refs_4_.refs_5_.refs_6_.refs_7_.refs_8_.refs_9_.refs_10_.refs_11_.refs_12_.refs_13_.refs_14_.refs_15_, ...), custom_call_target="tpu_custom_call" | custom-call | flops 1 | bytes 1 | tf_op jit(solution)/shard_map/pallas_call | solution.py:211
  96.7 1.4 %collective-permute-done.15 = bf16[1024,128]{1,0:T(8,128)(2,1)S(1)} collective-permute-done((bf16[1024,128]{1,0:T(8,128)(2,1)S(1)}, bf16[1024,128]{1,0:T(8,128)(2,1)S(1)}, u32[]{:S(2)}, u32[]{:S(2)}) %collective-permute-start.15) | collective-permute-done | bytes 262176 | tf_op jit(solution)/shard_map/ppermute | solution.py:250
  98.2 2.6 %collective-permute-start.21 = (bf16[2048,128]{1,0:T(8,128)(2,1)S(1)}, bf16[2048,128]{1,0:T(8,128)(2,1)S(1)}, u32[]{:S(2)}, u32[]{:S(2)}) collective-permute-start(bf16[2048,128]{1,0:T(8,128)(2,1)S(1)} %constant_dynamic-update-slice_fusion.2.w1), channel_id=1, source_target_pairs={{0,192},{1,25},{2,194},{3,27},{4,196},{5,29},{6,198},{7,31},{8,200... | collective-permute-start | bytes 1572872 | tf_op jit(solution)/shard_map/ppermute | solution.py:250
  101.3 2.7 %collective-permute-start.25 = (bf16[2048,128]{1,0:T(8,128)(2,1)S(1)}, bf16[2048,128]{1,0:T(8,128)(2,1)S(1)}, u32[]{:S(2)}, u32[]{:S(2)}) collective-permute-start(bf16[2048,128]{1,0:T(8,128)(2,1)S(1)} %constant_dynamic-update-slice_fusion.w0), channel_id=1, source_target_pairs={{0,192},{1,25},{2,194},{3,27},{4,196},{5,29},{6,198},{7,31},{8,200... | collective-permute-start | bytes 1572872 | tf_op jit(solution)/shard_map/ppermute | solution.py:250
  103.9 2.9 %shard_map.123.refs_16_ = f32[512,256]{1,0:T(8,128)S(1)} custom-call(s32[3]{0:T(128)S(1)} %pad_add_fusion.place, bf16[2048,128]{1,0:T(8,128)(2,1)S(1)} %constant_dynamic-update-slice_fusion.w0, bf16[2048,128]{1,0:T(8,128)(2,1)S(1)} %constant_dynamic-update-slice_fusion.2.w1, bf16[256,8192]{1,0:T(8,128)(2,1)} %refs_7_.11, bf16[256,8192]{1,0:T(8,128)(2,1)} %refs_7_.11, ...), custom_call_target="tpu_custom_call" | custom-call | flops 1 | bytes 1 | tf_op jit(solution)/shard_map/pallas_call | solution.py:211
  107.0 3.5 %collective-permute-done.20.w0 = bf16[2048,128]{1,0:T(8,128)(2,1)S(1)} collective-permute-done((bf16[2048,128]{1,0:T(8,128)(2,1)S(1)}, bf16[2048,128]{1,0:T(8,128)(2,1)S(1)}, u32[]{:S(2)}, u32[]{:S(2)}) %collective-permute-start.20) | collective-permute-done | bytes 524320 | tf_op jit(solution)/shard_map/ppermute | solution.py:250
  110.5 2.7 %collective-permute-start.23 = (bf16[2048,128]{1,0:T(8,128)(2,1)S(1)}, bf16[2048,128]{1,0:T(8,128)(2,1)S(1)}, u32[]{:S(2)}, u32[]{:S(2)}) collective-permute-start(bf16[2048,128]{1,0:T(8,128)(2,1)S(1)} %collective-permute-done.21.w1), channel_id=1, source_target_pairs={{0,192},{1,25},{2,194},{3,27},{4,196},{5,29},{6,198},{7,31},{8,200... | collective-permute-start | bytes 1572872 | tf_op jit(solution)/shard_map/ppermute | solution.py:250
  113.2 2.9 %shard_map.124.refs_16_ = f32[512,256]{1,0:T(8,128)S(1)} custom-call(s32[3]{0:T(128)S(1)} %pad_add_fusion.place, bf16[2048,128]{1,0:T(8,128)(2,1)S(1)} %collective-permute-done.20.w0, bf16[2048,128]{1,0:T(8,128)(2,1)S(1)} %collective-permute-done.21.w1, bf16[256,8192]{1,0:T(8,128)(2,1)} %refs_7_.11, bf16[256,8192]{1,0:T(8,128)(2,1)} %refs_7_.11, ...), custom_call_target="tpu_custom_call" | custom-call | flops 1 | bytes 1 | tf_op jit(solution)/shard_map/pallas_call | solution.py:211
  116.1 3.0 %collective-permute-start.26 = (f32[96,256]{1,0:T(8,128)S(1)}, f32[96,256]{1,0:T(8,128)S(1)}, u32[]{:S(2)}, u32[]{:S(2)}) collective-permute-start(f32[96,256]{1,0:T(8,128)S(1)} %get-tuple-element.84), channel_id=1, source_target_pairs={{0,1},{1,0},{2,3},{3,2},{4,5},{5,4},{6,7},{7,6},{8,9},{9,8},{10,11... | collective-permute-start | bytes 294920 | tf_op jit(solution)/shard_map/ppermute | solution.py:241
  119.1 2.9 %shard_map.125.refs_2_ = f32[512,256]{1,0:T(8,128)S(1)} custom-call(s32[3]{0:T(128)S(1)} %pad_add_fusion.place, bf16[2048,128]{1,0:T(8,128)(2,1)S(1)} %collective-permute-done.24.w0, bf16[2048,128]{1,0:T(8,128)(2,1)S(1)} %collective-permute-done.25.w1, bf16[256,8192]{1,0:T(8,128)(2,1)} %refs_7_.11, bf16[256,8192]{1,0:T(8,128)(2,1)} %refs_7_.11, ...), custom_call_target="tpu_custom_call" | custom-call | flops 1 | bytes 1 | tf_op jit(solution)/shard_map/pallas_call | solution.py:211
  122.1 1.5 %shard_map.126 = (f32[8,256]{1,0:T(8,128)S(1)}, f32[8,256]{1,0:T(8,128)S(1)}) custom-call(s32[3]{0:T(128)S(1)} %pad_add_fusion.place, bf16[2048,128]{1,0:T(8,128)(2,1)S(1)} %collective-permute-done.22.w0, bf16[2048,128]{1,0:T(8,128)(2,1)S(1)} %collective-permute-done.23.w1, bf16[256,2048]{1,0:T(8,128)(2,1)S(1)} %shard_map.121.refs_0_, ...), custom_call_target="tpu_custom_call" | custom-call | flops 1 | bytes 1 | tf_op jit(solution)/shard_map/pallas_call | solution.py:211
  123.6 2.1 %collective-permute-start.27 = (f32[8,256]{1,0:T(8,128)S(1)}, f32[8,256]{1,0:T(8,128)S(1)}, u32[]{:S(2)}, u32[]{:S(2)}) collective-permute-start(f32[8,256]{1,0:T(8,128)S(1)} %get-tuple-element.91), channel_id=1, source_target_pairs={{0,1},{1,0},{2,3},{3,2},{4,5},{5,4},{6,7},{7,6},{8,9},{9,8},{10,11... | collective-permute-start | bytes 24584 | tf_op jit(solution)/shard_map/ppermute | solution.py:241
  125.7 1.2 shard_map.127
  126.9 1.1 shard_map.128
  (62 shorter events, 6.1 us)
Async XLA Ops:
  0.6 3.8 %collective-permute-start = (bf16[256,512]{1,0:T(8,128)(2,1)}, bf16[256,512]{1,0:T(8,128)(2,1)S(1)}, u32[]{:S(2)}, u32[]{:S(2)}) collective-permute-start(bf16[256,512]{1,0:T(8,128)(2,1)} %l.1), channel_id=1, source_target_pairs={{0,1},{1,0},{2,3},{3,2},{4,5},{5,4},{6,7},{7,6},{8,9},{9,8},{10,11... | collective-permute-start | bytes 786440 | tf_op jit(solution)/shard_map/ppermute | solution.py:241
  1.5 2.2 %copy-start = (bf16[256,8192]{1,0:T(8,128)(2,1)S(1)}, bf16[256,8192]{1,0:T(8,128)(2,1)}, u32[]{:S(2)}) copy-start(bf16[256,8192]{1,0:T(8,128)(2,1)} %refs_3_.23) | copy-start | bytes 12582916
  3.7 0.9 copy-start.3
  3.7 2.3 %copy-start.1 = (bf16[256,8192]{1,0:T(8,128)(2,1)S(1)}, bf16[256,8192]{1,0:T(8,128)(2,1)}, u32[]{:S(2)}) copy-start(bf16[256,8192]{1,0:T(8,128)(2,1)} %refs_3_.23) | copy-start | bytes 12582916
  4.4 2.7 %collective-permute-start.1 = (bf16[256,2048]{1,0:T(8,128)(2,1)S(1)}, bf16[256,2048]{1,0:T(8,128)(2,1)S(1)}, u32[]{:S(2)}, u32[]{:S(2)}) collective-permute-start(bf16[256,2048]{1,0:T(8,128)(2,1)S(1)} %shard_map.102), channel_id=1, source_target_pairs={{0,1},{1,0},{2,3},{3,2},{4,5},{5,4},{6,7},{7,6},{8,9},{9,8},{10,11... | collective-permute-start | bytes 3145736 | tf_op jit(solution)/shard_map/ppermute | solution.py:241
  6.6 6.9 %collective-permute-start.2 = (bf16[256,2048]{1,0:T(8,128)(2,1)S(1)}, bf16[256,2048]{1,0:T(8,128)(2,1)S(1)}, u32[]{:S(2)}, u32[]{:S(2)}) collective-permute-start(bf16[256,2048]{1,0:T(8,128)(2,1)S(1)} %shard_map.106), channel_id=1, source_target_pairs={{0,1},{1,0},{2,3},{3,2},{4,5},{5,4},{6,7},{7,6},{8,9},{9,8},{10,11... | collective-permute-start | bytes 3145736 | tf_op jit(solution)/shard_map/ppermute | solution.py:241
  9.1 6.6 %collective-permute-start.3 = (bf16[256,2048]{1,0:T(8,128)(2,1)S(1)}, bf16[256,2048]{1,0:T(8,128)(2,1)S(1)}, u32[]{:S(2)}, u32[]{:S(2)}) collective-permute-start(bf16[256,2048]{1,0:T(8,128)(2,1)S(1)} %shard_map.105), channel_id=1, source_target_pairs={{0,1},{1,0},{2,3},{3,2},{4,5},{5,4},{6,7},{7,6},{8,9},{9,8},{10,11... | collective-permute-start | bytes 3145736 | tf_op jit(solution)/shard_map/ppermute | solution.py:241
  10.7 12.4 %collective-permute-start.5 = (s16[2080,128]{1,0:T(8,128)(2,1)S(1)}, s16[2080,128]{1,0:T(8,128)(2,1)S(1)}, u32[]{:S(2)}, u32[]{:S(2)}) collective-permute-start(s16[2080,128]{1,0:T(8,128)(2,1)S(1)} %shard_map.111), channel_id=1, source_target_pairs={{0,64},{1,9},{2,66},{3,11},{4,68},{5,13},{6,70},{7,15},{8,72},{9,1... | collective-permute-start | bytes 1597448 | tf_op jit(solution)/shard_map/ppermute | solution.py:250
  12.0 13.2 %collective-permute-start.10 = (s16[2080,128]{1,0:T(8,128)(2,1)S(1)}, s16[2080,128]{1,0:T(8,128)(2,1)S(1)}, u32[]{:S(2)}, u32[]{:S(2)}) collective-permute-start(s16[2080,128]{1,0:T(8,128)(2,1)S(1)} %shard_map.104), channel_id=1, source_target_pairs={{0,192},{1,25},{2,194},{3,27},{4,196},{5,29},{6,198},{7,31},{8,200... | collective-permute-start | bytes 1597448 | tf_op jit(solution)/shard_map/ppermute | solution.py:250
  19.6 11.2 %collective-permute-start.4 = (bf16[256,2048]{1,0:T(8,128)(2,1)}, bf16[256,2048]{1,0:T(8,128)(2,1)S(1)}, u32[]{:S(2)}, u32[]{:S(2)}) collective-permute-start(bf16[256,2048]{1,0:T(8,128)(2,1)} %shard_map.109), channel_id=1, source_target_pairs={{0,1},{1,0},{2,3},{3,2},{4,5},{5,4},{6,7},{7,6},{8,9},{9,8},{10,11... | collective-permute-start | bytes 3145736 | tf_op jit(solution)/shard_map/ppermute | solution.py:241
  20.3 15.3 %collective-permute-start.7 = (s16[2080,128]{1,0:T(8,128)(2,1)}, s16[2080,128]{1,0:T(8,128)(2,1)S(1)}, u32[]{:S(2)}, u32[]{:S(2)}) collective-permute-start(s16[2080,128]{1,0:T(8,128)(2,1)} %shard_map.108), channel_id=1, source_target_pairs={{0,192},{1,25},{2,194},{3,27},{4,196},{5,29},{6,198},{7,31},{8,200... | collective-permute-start | bytes 1597448 | tf_op jit(solution)/shard_map/ppermute | solution.py:250
  25.2 4.8 %copy-start.4 = (f32[32,512]{1,0:T(8,128)S(1)}, f32[32,512]{1,0:T(8,128)}, u32[]{:S(2)}) copy-start(f32[32,512]{1,0:T(8,128)} %master.1) | copy-start | bytes 196612
  25.2 10.4 %collective-permute-start.6 = (s16[2080,128]{1,0:T(8,128)(2,1)}, s16[2080,128]{1,0:T(8,128)(2,1)S(1)}, u32[]{:S(2)}, u32[]{:S(2)}) collective-permute-start(s16[2080,128]{1,0:T(8,128)(2,1)} %shard_map.112), channel_id=1, source_target_pairs={{0,64},{1,9},{2,66},{3,11},{4,68},{5,13},{6,70},{7,15},{8,72},{9,1... | collective-permute-start | bytes 1597448 | tf_op jit(solution)/shard_map/ppermute | solution.py:250
  25.2 15.5 %collective-permute-start.9 = (s16[2080,128]{1,0:T(8,128)(2,1)}, s16[2080,128]{1,0:T(8,128)(2,1)S(1)}, u32[]{:S(2)}, u32[]{:S(2)}) collective-permute-start(s16[2080,128]{1,0:T(8,128)(2,1)} %shard_map.107), channel_id=1, source_target_pairs={{0,64},{1,9},{2,66},{3,11},{4,68},{5,13},{6,70},{7,15},{8,72},{9,1... | collective-permute-start | bytes 1597448 | tf_op jit(solution)/shard_map/ppermute | solution.py:250
  27.3 13.4 %collective-permute-start.11 = (s16[2080,128]{1,0:T(8,128)(2,1)}, s16[2080,128]{1,0:T(8,128)(2,1)S(1)}, u32[]{:S(2)}, u32[]{:S(2)}) collective-permute-start(s16[2080,128]{1,0:T(8,128)(2,1)} %shard_map.115), channel_id=1, source_target_pairs={{0,192},{1,25},{2,194},{3,27},{4,196},{5,29},{6,198},{7,31},{8,200... | collective-permute-start | bytes 1597448 | tf_op jit(solution)/shard_map/ppermute | solution.py:250
  30.8 2.2 %copy-start.2 = (bf16[256,8192]{1,0:T(8,128)(2,1)S(1)}, bf16[256,8192]{1,0:T(8,128)(2,1)}, u32[]{:S(2)}) copy-start(bf16[256,8192]{1,0:T(8,128)(2,1)} %refs_3_.23) | copy-start | bytes 12582916
  36.5 35.5 %copy-start.5 = (f32[32,512]{1,0:T(8,128)S(1)}, f32[32,512]{1,0:T(8,128)}, u32[]{:S(2)}) copy-start(f32[32,512]{1,0:T(8,128)} %one.1) | copy-start | bytes 196612
  36.5 35.5 %copy-start.6 = (f32[32,512]{1,0:T(8,128)S(1)}, f32[32,512]{1,0:T(8,128)}, u32[]{:S(2)}) copy-start(f32[32,512]{1,0:T(8,128)} %two.1) | copy-start | bytes 196612
  36.5 52.4 %copy-start.7 = (s32[256]{0:T(256)S(1)}, s32[256]{0:T(256)}, u32[]{:S(2)}) copy-start(s32[256]{0:T(256)} %param.10) | copy-start | bytes 3076
  36.6 13.8 %collective-permute-start.13 = (s16[1040,128]{1,0:T(8,128)(2,1)S(1)}, s16[1040,128]{1,0:T(8,128)(2,1)S(1)}, u32[]{:S(2)}, u32[]{:S(2)}) collective-permute-start(s16[1040,128]{1,0:T(8,128)(2,1)S(1)} %shard_map.117), channel_id=1, source_target_pairs={{0,16},{1,129},{2,18},{3,131},{4,20},{5,133},{6,22},{7,135},{8,24}... | collective-permute-start | bytes 798728 | tf_op jit(solution)/shard_map/ppermute | solution.py:250
  41.6 8.7 %collective-permute-start.12 = (s16[1040,128]{1,0:T(8,128)(2,1)S(1)}, s16[1040,128]{1,0:T(8,128)(2,1)S(1)}, u32[]{:S(2)}, u32[]{:S(2)}) collective-permute-start(s16[1040,128]{1,0:T(8,128)(2,1)S(1)} %shard_map.116), channel_id=1, source_target_pairs={{0,8},{1,65},{2,10},{3,67},{4,12},{5,69},{6,14},{7,71},{8,16},{9,7... | collective-permute-start | bytes 798728 | tf_op jit(solution)/shard_map/ppermute | solution.py:250
  42.6 7.7 %collective-permute-start.14 = (s16[1040,128]{1,0:T(8,128)(2,1)S(1)}, s16[1040,128]{1,0:T(8,128)(2,1)S(1)}, u32[]{:S(2)}, u32[]{:S(2)}) collective-permute-start(s16[1040,128]{1,0:T(8,128)(2,1)S(1)} %shard_map.118), channel_id=1, source_target_pairs={{0,24},{1,193},{2,26},{3,195},{4,28},{5,197},{6,30},{7,199},{8,0},... | collective-permute-start | bytes 798728 | tf_op jit(solution)/shard_map/ppermute | solution.py:250
  45.4 5.0 %collective-permute-start.8 = (f32[96,256]{1,0:T(8,128)S(1)}, f32[96,256]{1,0:T(8,128)S(1)}, u32[]{:S(2)}, u32[]{:S(2)}) collective-permute-start(f32[96,256]{1,0:T(8,128)S(1)} %pad_maximum_fusion), channel_id=1, source_target_pairs={{0,1},{1,0},{2,3},{3,2},{4,5},{5,4},{6,7},{7,6},{8,9},{9,8},{10,11... | collective-permute-start | bytes 294920 | tf_op jit(solution)/shard_map/ppermute | solution.py:241
  67.7 27.0 %collective-permute-start.18 = (bf16[256,8192]{1,0:T(8,128)(2,1)}, bf16[256,8192]{1,0:T(8,128)(2,1)}, u32[]{:S(2)}, u32[]{:S(2)}) collective-permute-start(bf16[256,8192]{1,0:T(8,128)(2,1)} %refs_7_.11), channel_id=1, source_target_pairs={{0,1},{1,0},{2,3},{3,2},{4,5},{5,4},{6,7},{7,6},{8,9},{9,8},{10,11... | collective-permute-start | bytes 12582920 | tf_op jit(solution)/shard_map/ppermute | solution.py:241
  87.4 9.3 %collective-permute-start.17 = (bf16[1024,128]{1,0:T(8,128)(2,1)S(1)}, bf16[1024,128]{1,0:T(8,128)(2,1)S(1)}, u32[]{:S(2)}, u32[]{:S(2)}) collective-permute-start(bf16[1024,128]{1,0:T(8,128)(2,1)S(1)} %bitcast.12), channel_id=1, source_target_pairs={{0,24},{1,193},{2,26},{3,195},{4,28},{5,197},{6,30},{7,199},{8,0},... | collective-permute-start | bytes 786440 | tf_op jit(solution)/shard_map/ppermute | solution.py:250
  88.4 8.4 %collective-permute-start.16 = (bf16[1024,128]{1,0:T(8,128)(2,1)S(1)}, bf16[1024,128]{1,0:T(8,128)(2,1)S(1)}, u32[]{:S(2)}, u32[]{:S(2)}) collective-permute-start(bf16[1024,128]{1,0:T(8,128)(2,1)S(1)} %bitcast.13), channel_id=1, source_target_pairs={{0,16},{1,129},{2,18},{3,131},{4,20},{5,133},{6,22},{7,135},{8,24}... | collective-permute-start | bytes 786440 | tf_op jit(solution)/shard_map/ppermute | solution.py:250
  88.4 9.8 %collective-permute-start.15 = (bf16[1024,128]{1,0:T(8,128)(2,1)S(1)}, bf16[1024,128]{1,0:T(8,128)(2,1)S(1)}, u32[]{:S(2)}, u32[]{:S(2)}) collective-permute-start(bf16[1024,128]{1,0:T(8,128)(2,1)S(1)} %bitcast.14), channel_id=1, source_target_pairs={{0,8},{1,65},{2,10},{3,67},{4,12},{5,69},{6,14},{7,71},{8,16},{9,7... | collective-permute-start | bytes 786440 | tf_op jit(solution)/shard_map/ppermute | solution.py:250
  89.1 7.6 %collective-permute-start.19 = (s32[256,1]{1,0:T(8,128)S(1)}, s32[256,1]{1,0:T(8,128)S(1)}, u32[]{:S(2)}, u32[]{:S(2)}) collective-permute-start(s32[256,1]{1,0:T(8,128)S(1)} %copy.11.refs_3_), channel_id=1, source_target_pairs={{0,1},{1,0},{2,3},{3,2},{4,5},{5,4},{6,7},{7,6},{8,9},{9,8},{10,11... | collective-permute-start | bytes 3080 | tf_op jit(solution)/shard_map/ppermute | solution.py:241
  98.2 8.7 %collective-permute-start.21 = (bf16[2048,128]{1,0:T(8,128)(2,1)S(1)}, bf16[2048,128]{1,0:T(8,128)(2,1)S(1)}, u32[]{:S(2)}, u32[]{:S(2)}) collective-permute-start(bf16[2048,128]{1,0:T(8,128)(2,1)S(1)} %constant_dynamic-update-slice_fusion.2.w1), channel_id=1, source_target_pairs={{0,192},{1,25},{2,194},{3,27},{4,196},{5,29},{6,198},{7,31},{8,200... | collective-permute-start | bytes 1572872 | tf_op jit(solution)/shard_map/ppermute | solution.py:250
  100.9 9.6 %collective-permute-start.20 = (bf16[2048,128]{1,0:T(8,128)(2,1)S(1)}, bf16[2048,128]{1,0:T(8,128)(2,1)S(1)}, u32[]{:S(2)}, u32[]{:S(2)}) collective-permute-start(bf16[2048,128]{1,0:T(8,128)(2,1)S(1)} %constant_dynamic-update-slice_fusion.w0), channel_id=1, source_target_pairs={{0,64},{1,9},{2,66},{3,11},{4,68},{5,13},{6,70},{7,15},{8,72},{9,1... | collective-permute-start | bytes 1572872 | tf_op jit(solution)/shard_map/ppermute | solution.py:250
  101.0 15.1 %collective-permute-start.24 = (bf16[2048,128]{1,0:T(8,128)(2,1)S(1)}, bf16[2048,128]{1,0:T(8,128)(2,1)S(1)}, u32[]{:S(2)}, u32[]{:S(2)}) collective-permute-start(bf16[2048,128]{1,0:T(8,128)(2,1)S(1)} %constant_dynamic-update-slice_fusion.2.w1), channel_id=1, source_target_pairs={{0,64},{1,9},{2,66},{3,11},{4,68},{5,13},{6,70},{7,15},{8,72},{9,1... | collective-permute-start | bytes 1572872 | tf_op jit(solution)/shard_map/ppermute | solution.py:250
  101.3 17.8 %collective-permute-start.25 = (bf16[2048,128]{1,0:T(8,128)(2,1)S(1)}, bf16[2048,128]{1,0:T(8,128)(2,1)S(1)}, u32[]{:S(2)}, u32[]{:S(2)}) collective-permute-start(bf16[2048,128]{1,0:T(8,128)(2,1)S(1)} %constant_dynamic-update-slice_fusion.w0), channel_id=1, source_target_pairs={{0,192},{1,25},{2,194},{3,27},{4,196},{5,29},{6,198},{7,31},{8,200... | collective-permute-start | bytes 1572872 | tf_op jit(solution)/shard_map/ppermute | solution.py:250
  110.5 11.5 %collective-permute-start.22 = (bf16[2048,128]{1,0:T(8,128)(2,1)S(1)}, bf16[2048,128]{1,0:T(8,128)(2,1)S(1)}, u32[]{:S(2)}, u32[]{:S(2)}) collective-permute-start(bf16[2048,128]{1,0:T(8,128)(2,1)S(1)} %collective-permute-done.20.w0), channel_id=1, source_target_pairs={{0,64},{1,9},{2,66},{3,11},{4,68},{5,13},{6,70},{7,15},{8,72},{9,1... | collective-permute-start | bytes 1572872 | tf_op jit(solution)/shard_map/ppermute | solution.py:250
  110.5 11.6 %collective-permute-start.23 = (bf16[2048,128]{1,0:T(8,128)(2,1)S(1)}, bf16[2048,128]{1,0:T(8,128)(2,1)S(1)}, u32[]{:S(2)}, u32[]{:S(2)}) collective-permute-start(bf16[2048,128]{1,0:T(8,128)(2,1)S(1)} %collective-permute-done.21.w1), channel_id=1, source_target_pairs={{0,192},{1,25},{2,194},{3,27},{4,196},{5,29},{6,198},{7,31},{8,200... | collective-permute-start | bytes 1572872 | tf_op jit(solution)/shard_map/ppermute | solution.py:250
  116.1 5.9 %collective-permute-start.26 = (f32[96,256]{1,0:T(8,128)S(1)}, f32[96,256]{1,0:T(8,128)S(1)}, u32[]{:S(2)}, u32[]{:S(2)}) collective-permute-start(f32[96,256]{1,0:T(8,128)S(1)} %get-tuple-element.84), channel_id=1, source_target_pairs={{0,1},{1,0},{2,3},{3,2},{4,5},{5,4},{6,7},{7,6},{8,9},{9,8},{10,11... | collective-permute-start | bytes 294920 | tf_op jit(solution)/shard_map/ppermute | solution.py:241
  123.6 3.3 %collective-permute-start.27 = (f32[8,256]{1,0:T(8,128)S(1)}, f32[8,256]{1,0:T(8,128)S(1)}, u32[]{:S(2)}, u32[]{:S(2)}) collective-permute-start(f32[8,256]{1,0:T(8,128)S(1)} %get-tuple-element.91), channel_id=1, source_target_pairs={{0,1},{1,0},{2,3},{3,2},{4,5},{5,4},{6,7},{7,6},{8,9},{9,8},{10,11... | collective-permute-start | bytes 24584 | tf_op jit(solution)/shard_map/ppermute | solution.py:241
